TPU v7x, 32 devices: a whole 2x2x4 slice. The times are simulated.
32 devices in a mesh: layer: 2 (over y), dp: 4 (over z), feat: 4 (over x, core).
Axes of the slice: x: 2, y: 2, z: 4, core: 2. Of those that a mesh axis runs over, the one named last changes fastest.
Arguments:
- train_rows: bfloat16 [2048, 4096], P(('layer', 'dp'), 'feat'), parts along dimension 0, may hold values from -6 to 6
- train_labels: int32 [2048, 1], P(('layer', 'dp')), parts along dimension 0, may hold values from 0 to 255
- held_rows: bfloat16 [4096, 4096], P(('layer', 'dp'), 'feat'), parts along dimension 0, may hold values from -6 to 6
- held_labels: int32 [4096], P(('layer', 'dp')), parts along dimension 0, may hold values from 0 to 255
- precision: bfloat16 [6, 4096, 256], P('layer', 'feat'), parts along dimension 0
Outputs:
- pooled_cov: float32 [8192, 4096], P(('layer', 'feat'), 'dp'), parts along dimension 0
- whitened: bfloat16 [4096, 4096], P(('layer', 'dp'), 'feat'), parts along dimension 0
- distance: float32 [4096], P(('layer', 'dp')), parts along dimension 0
There are 2 independent parts, one for each index of `layer`. A program takes and returns all parts, laid end to end along the dimension named above; each array names one. Nothing has to cross between parts.
Inputs may be any that keep to these rules, and one draw needn't show every extreme that they name: `train_labels`: every class has at least one training row.
All inputs are finite; a program needn't handle non-finite values.
Results may differ from a plain program's by a relative error of at most 0.0004.
Values may be sent and summed in bfloat16 or wider, within the bound.
No kernel may reach another device: no remote copies, remote signals or barrier semaphores. Data moves between devices by JAX's collectives and lax.ppermute only.
A program may use at most 128 MiB of HBM per device.

v0:
```python
import jax
import jax.numpy as jnp
from jax import lax
from jax.sharding import PartitionSpec as P

C = 256
BLK = 256


def padded(cells, sides, width):
    for axis, dim in sides:
        count = lax.axis_size(axis)
        ends = count - 1
        head = lax.slice_in_dim(cells, 0, width, axis=dim)
        tail = lax.slice_in_dim(cells, cells.shape[dim] - width, cells.shape[dim], axis=dim)
        cells = jnp.concatenate(
            [
                lax.ppermute(tail, axis, [(i, (i + 1) % count) for i in range(ends)]),
                cells,
                lax.ppermute(head, axis, [((i + 1) % count, i) for i in range(ends)]),
            ],
            axis=dim,
        )
    return cells


def contract_rows(left, right):
    return lax.dot_general(
        left, right, (((0,), (0,)), ((), ())), preferred_element_type=jnp.float32
    )


def body(train_rows, train_labels, held_rows, held_labels, precision):
    local = train_rows.shape[1]
    full = lax.all_gather(train_rows, "feat", axis=1, tiled=True)
    width = full.shape[1]
    classes = jnp.arange(C, dtype=jnp.int32)
    onehot_train = (train_labels == classes[None, :]).astype(jnp.bfloat16)
    local_sums = contract_rows(onehot_train, full)
    local_counts = jnp.sum(onehot_train.astype(jnp.float32), axis=0)
    sums, counts = lax.psum((local_sums, local_counts), "dp")
    means = sums / counts[:, None]
    feat_index = lax.axis_index("feat")
    dp_index = lax.axis_index("dp")
    dp_count = lax.axis_size("dp")
    ncols = width // dp_count
    block = lax.psum_scatter(
        contract_rows(full, train_rows), "dp", scatter_dimension=0, tiled=True
    ).T
    sums_rows = lax.dynamic_slice_in_dim(sums, feat_index * local, local, 1)
    means_cols = lax.dynamic_slice_in_dim(means, dp_index * ncols, ncols, 1)
    correction = lax.dot_general(
        sums_rows,
        means_cols,
        (((0,), (0,)), ((), ())),
        precision=lax.Precision.HIGHEST,
        preferred_element_type=jnp.float32,
    )
    denominator = float(train_rows.shape[0] * dp_count - C)
    pooled_cov = (block - correction) / denominator
    means_local = lax.dynamic_slice_in_dim(means, feat_index * local, local, 1)
    picked = means_local[held_labels]
    centred = held_rows.astype(jnp.float32) - picked
    extended = padded(centred, (("feat", 1),), BLK)
    held_count = held_rows.shape[0]
    nlocal = local // BLK
    windows = extended.reshape(held_count, nlocal + 2, BLK)
    bands = precision.astype(jnp.float32).reshape(3, nlocal, BLK, BLK)
    image = jnp.zeros((held_count, nlocal, BLK), jnp.float32)
    for k in range(3):
        image = image + jnp.einsum(
            "rmj,mij->rmi",
            windows[:, k : k + nlocal],
            bands[k],
            precision=lax.Precision.HIGHEST,
            preferred_element_type=jnp.float32,
        )
    image = image.reshape(held_count, local)
    partial_score = jnp.sum(centred * image, axis=1)
    distance = lax.psum(partial_score, "feat") / width
    return (pooled_cov, image.astype(jnp.bfloat16), distance)


def solution(mesh):
    return jax.shard_map(
        body,
        mesh=mesh,
        in_specs=(
            P(("layer", "dp"), "feat"),
            P(("layer", "dp"), None),
            P(("layer", "dp"), "feat"),
            P(("layer", "dp")),
            P("layer", "feat", None),
        ),
        out_specs=(P(("layer", "feat"), "dp"), P(("layer", "dp"), "feat"), P(("layer", "dp"))),
        check_vma=False,
    )
```

profile of v0, /device:TPU:0, one launch (start us, length us, event | category | flops | bytes accessed | tf_op | source)
XLA Modules:
  0.0 497.0 jit_solution(6147197103815917250)
XLA Ops:
  7.9 26.9 %all-gather.2.cloned.1.call-done = bf16[256,4096]{1,0:T(8,128)(2,1)} async-done(((bf16[256,1024]{1,0:T(8,128)(2,1)}), bf16[256,4096]{1,0:T(8,128)(2,1)}) %all-gather.2.cloned.1.call-update) | async-done | bytes 2097168 | tf_op jit(solution)/shard_map/all_gather | solution.py:35
  34.9 4.4 fusion.4
  39.4 1.5 copy-done.3
  41.0 8.7 %fusion.9 = f32[4096,1024]{1,0:T(8,128)} fusion(bf16[256,4096]{1,0:T(8,128)(2,1)S(1)} %copy-done.3, bf16[256,1024]{1,0:T(8,128)(2,1)S(1)} %copy-done.4), kind=kOutput, calls=%fused_computation.22 | convolution fusion | flops 2147483648 | bytes 19398656 | tf_op jit(solution)/shard_map/dot_general | solution.py:28
  50.5 12.1 %psum.22 = f32[256]{0:T(256)S(1)} all-reduce(f32[256]{0:T(256)S(1)} %convert_reduce_fusion), channel_id=1, replica_groups=mesh['layer'=2,'dp'=4,'feat'=4] {'dp'}, use_global_device_ids=true, to_apply=%region_3.0 | all-reduce | flops 256 | bytes 2048 | tf_op jit(solution)/shard_map/psum | solution.py:41
  62.6 132.1 %all-reduce.2.cloned.1.call-done = f32[256,4096]{1,0:T(8,128)} async-done(((f32[256,4096]{1,0:T(8,128)}), f32[256,4096]{1,0:T(8,128)}) %all-reduce.2.cloned.1.call-update) | async-done | bytes 4194320 | tf_op jit(solution)/shard_map/psum | solution.py:41
  194.7 2.7 broadcast_divide_fusion
  197.4 2.0 copy-done.2
  199.5 2.6 gather_fusion
  202.2 2.2 convert_subtract_fusion
  204.3 1.2 fusion.7
  205.6 1.3 collective-permute-start.1
  206.9 3.1 collective-permute-start
  209.9 2.5 fusion.8
  212.5 2.0 pad_maximum_fusion
  214.5 2.4 copy.21
  216.9 2.3 fusion.10
  220.4 2.6 add_add_fusion
  223.0 3.1 copy.25
  226.1 3.5 multiply_reduce_fusion
  229.6 11.3 %psum.23 = f32[512]{0:T(512)S(1)} all-reduce(f32[512]{0:T(512)S(1)} %get-tuple-element.12), channel_id=1, replica_groups=mesh['layer'=2,'dp'=4,'feat'=4] {'feat'}, use_global_device_ids=true, to_apply=%region_5.0 | all-reduce | flops 512 | bytes 4096 | tf_op jit(solution)/shard_map/psum | solution.py:80
  241.6 235.0 %reduce-scatter.2.cloned.1.call-done = f32[1024,1024]{1,0:T(8,128)} async-done(((f32[4096,1024]{1,0:T(8,128)}), f32[1024,1024]{1,0:T(8,128)}) %reduce-scatter.2.cloned.1.call-update) | async-done | bytes 4194320 | tf_op jit(solution)/shard_map/reduce_scatter | solution.py:47
  476.5 8.6 %fusion = f32[1024,1024]{0,1:T(8,128)} fusion(f32[1024,1024]{1,0:T(8,128)} %reduce-scatter.2.cloned.1.call-done, f32[256,4096]{1,0:T(8,128)} %copy-done.2, s32[]{:T(128)S(6)} %select_n.11, f32[256,4096]{1,0:T(8,128)} %all-reduce.2.cloned.1.call-done, s32[]{:T(128)S(6)} %select_n.10), kind=kOutput, calls=%fused_computation.2 | convolution fusion | flops 3223322624 | bytes 10485768 | tf_op jit(solution)/shard_map/dot_general | solution.py:52
  485.1 5.3 %copy.27 = f32[1024,1024]{1,0:T(8,128)} copy(f32[1024,1024]{0,1:T(8,128)} %fusion) | data formatting | bytes 8388608
  (32 shorter events, 3.6 us)
Async XLA Ops:
  7.2 27.7 %all-gather.2.cloned.1.call-start = ((), (), s32[]{:S(2)}) async-start(), calls=%async_computation.1 | async-start | bytes 2621440 | tf_op jit(solution)/shard_map/all_gather | solution.py:35
  7.9 186.8 %all-reduce.2.cloned.1.call-start = ((), (), s32[]{:S(2)}) async-start(), calls=%async_computation.3 | async-start | bytes 8388608 | tf_op jit(solution)/shard_map/psum | solution.py:41
  39.3 1.6 copy-start.3
  39.3 1.7 copy-start.4
  39.4 437.2 %reduce-scatter.2.cloned.1.call-start = ((), (), s32[]{:S(2)}) async-start(), calls=%async_computation.2 | async-start | bytes 20971520 | tf_op jit(solution)/shard_map/reduce_scatter | solution.py:47
  49.7 0.7 copy-start.8
  49.7 12.8 %copy-start.9 = (s32[512]{0:T(512)S(1)}, s32[512]{0:T(512)}, u32[]{:S(2)}) copy-start(s32[512]{0:T(512)} %param.8) | copy-start | bytes 6148
  197.4 2.0 copy-start.2
  199.5 2.7 copy-start.7
  204.3 8.2 %copy-start = (f32[512,1024]{1,0:T(8,128)}, f32[512,1024]{1,0:T(8,128)S(1)}, u32[]{:S(2)}) copy-start(f32[512,1024]{1,0:T(8,128)S(1)} %convert_subtract_fusion) | copy-start | bytes 6291460
  205.6 6.9 %collective-permute-start.1 = (f32[512,256]{1,0:T(8,128)}, f32[512,256]{1,0:T(8,128)S(1)}, u32[]{:S(2)}, u32[]{:S(2)}) collective-permute-start(f32[512,256]{1,0:T(8,128)} %get-tuple-element.15), channel_id=1, source_target_pairs={{1,0},{2,1},{3,2},{5,4},{6,5},{7,6},{9,8},{10,9},{11,10},{13,12},{... | collective-permute-start | bytes 1572872 | tf_op jit(solution)/shard_map/ppermute | solution.py:20
  206.9 5.6 %collective-permute-start = (f32[512,256]{1,0:T(8,128)}, f32[512,256]{1,0:T(8,128)S(1)}, u32[]{:S(2)}, u32[]{:S(2)}) collective-permute-start(f32[512,256]{1,0:T(8,128)} %get-tuple-element.14), channel_id=1, source_target_pairs={{0,1},{1,2},{2,3},{4,5},{5,6},{6,7},{8,9},{9,10},{10,11},{12,13},{... | collective-permute-start | bytes 1572872 | tf_op jit(solution)/shard_map/ppermute | solution.py:18
  216.9 2.3 copy-start.6
  219.2 1.2 copy-start.5
  223.0 3.1 copy-start.1
Sparse Core Ops, SparseCore 0:
  9.6 25.2 all-gather.1
  39.5 155.1 all-reduce.1
  197.2 279.3 reduce-scatter.1
where the time goes:
time: 497 us
  waiting for transfers between devices  395 us (79%)
  matrix products  27.8 us (6%)
  blocking collectives  23.4 us (5%)
  local copies, waits for them, and re-layouts  21.6 us (4%)
  between operations  13.9 us (3%)
  other arithmetic  11.1 us (2%)
    reduce_scatter x1, waiting for transfers between devices, body(): lax.psum_scatter(contract_rows(full, train_rows), 'dp', scatter_dimension...  235 us
    psum x1, waiting for transfers between devices, body(): sums, counts = lax.psum((local_sums, local_counts), 'dp')  132 us
    all_gather x1, waiting for transfers between devices, body(): full = lax.all_gather(train_rows, 'feat', axis=1, tiled=True)  26.9 us
    dot_general x2, matrix products, contract_rows(): lax.dot_general(left, right, (((0,), (0,)), ((), ())), preferred_element_...  13.2 us
    psum x1, blocking collectives, body(): sums, counts = lax.psum((local_sums, local_counts), 'dp')  12.1 us
    psum x1, blocking collectives, body(): distance = lax.psum(partial_score, 'feat') / width  11.3 us
  transfers between devices with their start and end apart: 5, of which 3 were waited for; matrix products, arithmetic and copies ran while one was open for 8% of the time, Pallas kernels for 0%

commit v1 on v0

--- a/solution.py
+++ b/solution.py
@@ -1,10 +1,18 @@
 import jax
 import jax.numpy as jnp
 from jax import lax
+from jax.experimental import pallas as pl
+from jax.experimental.pallas import tpu as pltpu
 from jax.sharding import PartitionSpec as P
 
 C = 256
 BLK = 256
+F32 = jnp.float32
+BF16 = jnp.bfloat16
+VMEM = pl.BlockSpec(memory_space=pltpu.VMEM)
+SMEM = pl.BlockSpec(memory_space=pltpu.SMEM)
+ANY = pl.BlockSpec(memory_space=pl.ANY)
+PARAMS = pltpu.CompilerParams(vmem_limit_bytes=48 * 1024 * 1024)
 
 
 def padded(cells, sides, width):
@@ -26,7 +34,13 @@
 
 def contract_rows(left, right):
     return lax.dot_general(
-        left, right, (((0,), (0,)), ((), ())), preferred_element_type=jnp.float32
+        left, right, (((0,), (0,)), ((), ())), preferred_element_type=F32
+    )
+
+
+def contract_columns(left, right):
+    return lax.dot_general(
+        left, right, (((1,), (1,)), ((), ())), preferred_element_type=F32
     )
 
 
@@ -35,9 +49,9 @@
     full = lax.all_gather(train_rows, "feat", axis=1, tiled=True)
     width = full.shape[1]
     classes = jnp.arange(C, dtype=jnp.int32)
-    onehot_train = (train_labels == classes[None, :]).astype(jnp.bfloat16)
+    onehot_train = (train_labels == classes[None, :]).astype(BF16)
     local_sums = contract_rows(onehot_train, full)
-    local_counts = jnp.sum(onehot_train.astype(jnp.float32), axis=0)
+    local_counts = jnp.sum(onehot_train.astype(F32), axis=0)
     sums, counts = lax.psum((local_sums, local_counts), "dp")
     means = sums / counts[:, None]
     feat_index = lax.axis_index("feat")
@@ -54,36 +68,215 @@
         means_cols,
         (((0,), (0,)), ((), ())),
         precision=lax.Precision.HIGHEST,
-        preferred_element_type=jnp.float32,
+        preferred_element_type=F32,
     )
     denominator = float(train_rows.shape[0] * dp_count - C)
     pooled_cov = (block - correction) / denominator
     means_local = lax.dynamic_slice_in_dim(means, feat_index * local, local, 1)
     picked = means_local[held_labels]
-    centred = held_rows.astype(jnp.float32) - picked
+    centred = held_rows.astype(F32) - picked
     extended = padded(centred, (("feat", 1),), BLK)
     held_count = held_rows.shape[0]
     nlocal = local // BLK
     windows = extended.reshape(held_count, nlocal + 2, BLK)
-    bands = precision.astype(jnp.float32).reshape(3, nlocal, BLK, BLK)
-    image = jnp.zeros((held_count, nlocal, BLK), jnp.float32)
+    bands = precision.astype(F32).reshape(3, nlocal, BLK, BLK)
+    image = jnp.zeros((held_count, nlocal, BLK), F32)
     for k in range(3):
         image = image + jnp.einsum(
             "rmj,mij->rmi",
             windows[:, k : k + nlocal],
             bands[k],
             precision=lax.Precision.HIGHEST,
-            preferred_element_type=jnp.float32,
+            preferred_element_type=F32,
         )
     image = image.reshape(held_count, local)
     partial_score = jnp.sum(centred * image, axis=1)
     distance = lax.psum(partial_score, "feat") / width
-    return (pooled_cov, image.astype(jnp.bfloat16), distance)
+    return (pooled_cov, image.astype(BF16), distance)
+
+
+def split3(value):
+    high = value.astype(BF16)
+    rest = value - high.astype(F32)
+    middle = rest.astype(BF16)
+    return high, middle, (rest - middle.astype(F32)).astype(BF16)
+
+
+def onehot_rows(labels):
+    classes = lax.broadcasted_iota(jnp.int32, (C, labels.shape[1]), 0)
+    return (classes == labels).astype(F32)
+
+
+def class_sums(label_refs, row_refs, columns):
+    total = None
+    counts = None
+    for label_ref, row_ref in zip(label_refs, row_refs, strict=True):
+        onehot = onehot_rows(label_ref[...])
+        part = jnp.dot(onehot.astype(BF16), row_ref[:, columns], preferred_element_type=F32)
+        number = jnp.sum(onehot, axis=1, keepdims=True)
+        total = part if total is None else total + part
+        counts = number if counts is None else counts + number
+    return total, counts
+
+
+def edge_kernel(parts, *refs):
+    labels, rows = refs[:parts], refs[parts : 2 * parts]
+    head_ref, tail_ref = refs[2 * parts :]
+    width = rows[0].shape[1]
+    sums, counts = class_sums(labels, rows, slice(0, BLK))
+    head_ref[...] = sums / counts
+    sums, counts = class_sums(labels, rows, slice(width - BLK, width))
+    tail_ref[...] = sums / counts
+
+
+def edge_means(labels, rows):
+    shape = jax.ShapeDtypeStruct((C, BLK), F32)
+    return pl.pallas_call(
+        lambda *refs: edge_kernel(len(rows), *refs),
+        out_shape=(shape, shape),
+        in_specs=[VMEM] * (2 * len(rows)),
+        out_specs=(VMEM, VMEM),
+        compiler_params=PARAMS,
+        name="edge_means",
+    )(*labels, *rows)
+
+
+def white_kernel(parts, *refs):
+    labels, rows = refs[:parts], refs[parts : 2 * parts]
+    (held_ref, left_ref, right_ref, left_means, right_means, held_labels, precision,
+     white_ref, score_ref, bands) = refs[2 * parts :]
+    width = held_ref.shape[1]
+    for k in range(3):
+        bands[:, k * BLK : (k + 1) * BLK] = precision[k]
+    sums, counts = class_sums(labels, rows, slice(0, width))
+    means = jnp.concatenate([left_means[...], sums / counts, right_means[...]], axis=1)
+    onehot = onehot_rows(held_labels[...]).astype(BF16)
+    picked = sum(contract_rows(onehot, piece) for piece in split3(means))
+    held = jnp.concatenate([left_ref[...], held_ref[...], right_ref[...]], axis=1)
+    centred = held.astype(F32) - picked
+    pieces = split3(centred)
+    score = jnp.zeros((held_ref.shape[0], 128), F32)
+    for m in range(width // BLK):
+        inside = slice(m * BLK, (m + 1) * BLK)
+        window = slice(m * BLK, (m + 3) * BLK)
+        band = bands[inside, :]
+        image = sum(contract_columns(piece[:, window], band) for piece in reversed(pieces))
+        white_ref[:, inside] = image.astype(BF16)
+        product = centred[:, (m + 1) * BLK : (m + 2) * BLK] * image
+        for lanes in range(0, BLK, 128):
+            score = score + product[:, lanes : lanes + 128]
+    score_ref[...] = jnp.sum(score.T, axis=0, keepdims=True)
+
+
+def whiten(labels, rows, held, left, right, left_means, right_means, held_labels, precision):
+    count, width = held.shape
+    return pl.pallas_call(
+        lambda *refs: white_kernel(len(rows), *refs),
+        out_shape=(
+            jax.ShapeDtypeStruct((count, width), BF16),
+            jax.ShapeDtypeStruct((1, count), F32),
+        ),
+        in_specs=[VMEM] * (2 * len(rows) + 7),
+        out_specs=(VMEM, VMEM),
+        scratch_shapes=[pltpu.VMEM((width, 3 * BLK), BF16)],
+        compiler_params=PARAMS,
+        name="whiten",
+    )(*labels, *rows, held, left, right, left_means, right_means, held_labels, precision)
+
+
+def gram_kernel(parts, scale, *refs):
+    role_ref = refs[0]
+    labels, rows = refs[1 : 1 + parts], refs[1 + parts : 1 + 2 * parts]
+    choices = [refs[1 + (2 + k) * parts : 1 + (3 + k) * parts] for k in range(4)]
+    out_ref, left, right, sem = refs[1 + 6 * parts :]
+    count = rows[0].shape[0]
+    total = parts * count
+    role = role_ref[0]
+    for k, choice in enumerate(choices):
+
+        @pl.when(role == k)
+        def _():
+            for p, ref in enumerate(choice):
+                pltpu.make_async_copy(ref, right.at[pl.ds(p * count, count)], sem.at[p]).start()
+
+    for p, ref in enumerate(rows):
+        left[p * count : (p + 1) * count, :] = ref[...]
+    sums, counts = class_sums(labels, rows, slice(0, rows[0].shape[1]))
+    s1, s2, s3 = split3(sums)
+    for p in range(parts):
+        pltpu.make_async_copy(
+            choices[0][p], right.at[pl.ds(p * count, count)], sem.at[p]
+        ).wait()
+    others = [right.at[pl.ds(p * count, count)] for p in range(parts)]
+    sums, _ = class_sums(labels, others, slice(0, right.shape[1]))
+    m1, m2, m3 = split3(-(sums / counts))
+    for k, (s, m) in enumerate(((s1, m1), (s1, m2), (s2, m1), (s1, m3), (s2, m2), (s3, m1))):
+        left[total + k * C : total + (k + 1) * C, :] = s
+        right[total + k * C : total + (k + 1) * C, :] = m
+    for t in range(0, out_ref.shape[0], BLK):
+        out_ref[t : t + BLK, :] = contract_rows(left[:, t : t + BLK], right[...]) * scale
+
+
+def pooled(role, labels, rows, choices, scale):
+    count, width = rows[0].shape
+    parts = len(rows)
+    depth = parts * count + 6 * C
+    return pl.pallas_call(
+        lambda *refs: gram_kernel(parts, scale, *refs),
+        out_shape=jax.ShapeDtypeStruct((width, width), F32),
+        in_specs=[SMEM] + [VMEM] * (2 * parts) + [ANY] * (4 * parts),
+        out_specs=VMEM,
+        scratch_shapes=[
+            pltpu.VMEM((depth, width), BF16),
+            pltpu.VMEM((depth, width), BF16),
+            pltpu.SemaphoreType.DMA((parts,)),
+        ],
+        compiler_params=PARAMS,
+        name="pooled",
+    )(role, *labels, *rows, *[ref for choice in choices for ref in choice])
+
+
+def four_by_four(train_rows, train_labels, held_rows, held_labels, precision):
+    count, width = train_rows.shape
+    n = 4
+    flip = {k: [(i, i ^ k) for i in range(n)] for k in (1, 2, 3)}
+    to_right = [(i, i + 1) for i in range(n - 1)]
+    to_left = [(i + 1, i) for i in range(n - 1)]
+    owners = [(i, i) for i in range(n)]
+
+    def hop(array, start, end):
+        pairs = [(d * n + (d ^ start), d * n + (d ^ end)) for d, _ in owners]
+        return lax.ppermute(array, ("dp", "feat"), pairs)
+
+    rows = [train_rows]
+    rows.append(lax.ppermute(train_rows, "dp", flip[2]))
+    rows.append(lax.ppermute(train_rows, "dp", flip[1]))
+    rows.append(lax.ppermute(rows[1], "dp", flip[1]))
+    own_labels = train_labels.reshape(1, count)
+    labels = [own_labels] + [lax.ppermute(own_labels, "dp", flip[k]) for k in (2, 1, 3)]
+    left = lax.ppermute(held_rows[:, width - BLK :], "feat", to_right)
+    right = lax.ppermute(held_rows[:, :BLK], "feat", to_left)
+    across = [hop(r, 0, 2) for r in rows]
+    beside = [hop(r, 0, 1) for r in rows]
+    beyond = [hop(r, 2, 3) for r in across]
+    head, tail = edge_means(labels, rows)
+    left_means = lax.ppermute(tail, "feat", to_right)
+    right_means = lax.ppermute(head, "feat", to_left)
+    white, score = whiten(
+        labels, rows, held_rows, left, right, left_means, right_means,
+        held_labels.reshape(1, -1), precision,
+    )
+    role = (lax.axis_index("dp") ^ lax.axis_index("feat")).astype(jnp.int32).reshape(1)
+    cov = pooled(role, labels, rows, (rows, beside, across, beyond), 1.0 / (n * count - C))
+    scores = [score] + [lax.ppermute(score, "feat", flip[k]) for k in (1, 2, 3)]
+    distance = ((scores[0] + scores[1]) + (scores[2] + scores[3])) / (n * width)
+    return cov, white, distance.reshape(-1)
 
 
 def solution(mesh):
+    fits = mesh.shape["dp"] == 4 and mesh.shape["feat"] == 4
     return jax.shard_map(
-        body,
+        four_by_four if fits else body,
         mesh=mesh,
         in_specs=(
             P(("layer", "dp"), "feat"),

time: 497 us -> 104 us (0.21)
  the two profiles are of different devices: /device:TPU:0 before, /device:TPU:17 now
where the time goes in v1:
time: 104 us
  starting transfers between devices  39.9 us (38%)
  waiting for transfers between devices  35.7 us (34%)
  Pallas kernels  16.6 us (16%)
  local copies, waits for them, and re-layouts  9.84 us (9%)
  between operations  1.04 us (1%)
    ppermute x1, waiting for transfers between devices, four_by_four(): rows.append(lax.ppermute(train_rows, 'dp', flip[2]))  21.1 us
    ppermute x12, starting transfers between devices, hop(): return lax.ppermute(array, ('dp', 'feat'), pairs)  13.8 us
    pallas_call x1, Pallas kernels, pooled(): pl.pallas_call(lambda *refs: gram_kernel(parts, scale, *refs), out_shape=...  10.5 us
    unnamed x22, local copies, waits for them, and re-layouts  8.72 us
    ppermute x3, waiting for transfers between devices, four_by_four(): lax.ppermute(own_labels, 'dp', flip[k])  8.56 us
    ppermute x1, starting transfers between devices, four_by_four(): left = lax.ppermute(held_rows[:, width - BLK:], 'feat', to_right)  5.88 us
    pallas_call x1, Pallas kernels, whiten(): pl.pallas_call(lambda *refs: white_kernel(len(rows), *refs), out_shape=(j...  5.55 us
    ppermute x1, starting transfers between devices, four_by_four(): rows.append(lax.ppermute(rows[1], 'dp', flip[1]))  4.86 us
  transfers between devices with their start and end apart: 25, of which 7 were waited for; matrix products, arithmetic and copies ran while one was open for 2% of the time, Pallas kernels for 6%

profile of v1, /device:TPU:17, one launch (start us, length us, event | category | flops | bytes accessed | tf_op | source)
XLA Modules:
  0.0 103.7 jit_solution(5589101186135061394)
XLA Ops:
  0.7 1.4 %collective-permute-start.4 = (bf16[256,1024]{1,0:T(8,128)(2,1)}, bf16[256,1024]{1,0:T(8,128)(2,1)S(1)}, u32[]{:S(2)}, u32[]{:S(2)}) collective-permute-start(bf16[256,1024]{1,0:T(8,128)(2,1)} %refs_4_.3), channel_id=1, source_target_pairs={{0,4},{4,0},{8,12},{12,8},{1,5},{5,1},{9,13},{13,9},{2,6},{6,2},{1... | collective-permute-start | bytes 1572872 | tf_op jit(solution)/shard_map/ppermute | solution.py:253
  2.1 21.1 %collective-permute-done.3.refs_6_.refs_10_.refs_5_ = bf16[256,1024]{1,0:T(8,128)(2,1)S(1)} collective-permute-done((bf16[256,1024]{1,0:T(8,128)(2,1)}, bf16[256,1024]{1,0:T(8,128)(2,1)S(1)}, u32[]{:S(2)}, u32[]{:S(2)}) %collective-permute-start.3) | collective-permute-done | bytes 524320 | tf_op jit(solution)/shard_map/ppermute | solution.py:252
  23.2 4.9 %collective-permute-start.5 = (bf16[256,1024]{1,0:T(8,128)(2,1)S(1)}, bf16[256,1024]{1,0:T(8,128)(2,1)S(1)}, u32[]{:S(2)}, u32[]{:S(2)}) collective-permute-start(bf16[256,1024]{1,0:T(8,128)(2,1)S(1)} %collective-permute-done.3.refs_6_.refs_10_.refs_5_), channel_id=1, source_target_pairs={{0,4},{4,0},{8,12},{12,8},{1,5},{5,1},{9,13},{13,9},{2,6},{6,2},{1... | collective-permute-start | bytes 1572872 | tf_op jit(solution)/shard_map/ppermute | solution.py:254
  28.1 2.6 %collective-permute-start.2 = (s32[1,256]{1,0:T(1,128)}, s32[1,256]{1,0:T(1,128)S(1)}, u32[]{:S(2)}, u32[]{:S(2)}) collective-permute-start(s32[1,256]{1,0:T(1,128)} %bitcast.6), channel_id=1, source_target_pairs={{0,12},{4,8},{8,4},{12,0},{1,13},{5,9},{9,5},{13,1},{2,14},{6,10},... | collective-permute-start | bytes 3080 | tf_op jit(solution)/shard_map/ppermute | solution.py:256
  30.7 8.0 %collective-permute-done.refs_2_.refs_1_ = s32[1,256]{1,0:T(1,128)S(1)} collective-permute-done((s32[1,256]{1,0:T(1,128)}, s32[1,256]{1,0:T(1,128)S(1)}, u32[]{:S(2)}, u32[]{:S(2)}) %collective-permute-start) | collective-permute-done | bytes 1056 | tf_op jit(solution)/shard_map/ppermute | solution.py:256
  41.8 5.9 %collective-permute-start.18 = (bf16[512,256]{1,0:T(8,128)(2,1)S(1)}, bf16[512,256]{1,0:T(8,128)(2,1)S(1)}, u32[]{:S(2)}, u32[]{:S(2)}) collective-permute-start(bf16[512,256]{1,0:T(8,128)(2,1)S(1)} %get-tuple-element.12), channel_id=1, source_target_pairs={{0,1},{1,2},{2,3},{4,5},{5,6},{6,7},{8,9},{9,10},{10,11},{12,13},{... | collective-permute-start | bytes 786440 | tf_op jit(solution)/shard_map/ppermute | solution.py:257
  47.7 1.9 %collective-permute-start.19 = (bf16[512,256]{1,0:T(8,128)(2,1)S(1)}, bf16[512,256]{1,0:T(8,128)(2,1)S(1)}, u32[]{:S(2)}, u32[]{:S(2)}) collective-permute-start(bf16[512,256]{1,0:T(8,128)(2,1)S(1)} %get-tuple-element.11), channel_id=1, source_target_pairs={{1,0},{2,1},{3,2},{5,4},{6,5},{7,6},{9,8},{10,9},{11,10},{13,12},{... | collective-permute-start | bytes 786440 | tf_op jit(solution)/shard_map/ppermute | solution.py:258
  51.9 3.6 %collective-permute-start.20 = (f32[256,256]{1,0:T(8,128)S(1)}, f32[256,256]{1,0:T(8,128)S(1)}, u32[]{:S(2)}, u32[]{:S(2)}) collective-permute-start(f32[256,256]{1,0:T(8,128)S(1)} %get-tuple-element.7), channel_id=1, source_target_pairs={{0,1},{1,2},{2,3},{4,5},{5,6},{6,7},{8,9},{9,10},{10,11},{12,13},{... | collective-permute-start | bytes 786440 | tf_op jit(solution)/shard_map/ppermute | solution.py:263
  55.6 1.9 %collective-permute-start.21 = (f32[256,256]{1,0:T(8,128)S(1)}, f32[256,256]{1,0:T(8,128)S(1)}, u32[]{:S(2)}, u32[]{:S(2)}) collective-permute-start(f32[256,256]{1,0:T(8,128)S(1)} %get-tuple-element.8), channel_id=1, source_target_pairs={{1,0},{2,1},{3,2},{5,4},{6,5},{7,6},{9,8},{10,9},{11,10},{13,12},{... | collective-permute-start | bytes 786440 | tf_op jit(solution)/shard_map/ppermute | solution.py:264
  59.0 1.5 %collective-permute-start.11 = (bf16[256,1024]{1,0:T(8,128)(2,1)S(1)}, bf16[256,1024]{1,0:T(8,128)(2,1)}, u32[]{:S(2)}, u32[]{:S(2)}) collective-permute-start(bf16[256,1024]{1,0:T(8,128)(2,1)S(1)} %collective-permute-done.3.refs_6_.refs_10_.refs_5_), channel_id=1, source_target_pairs={{0,2},{5,7},{10,8},{15,13},{16,18},{21,23},{26,24},{31,29}} | collective-permute-start | bytes 1572872 | tf_op jit(solution)/shard_map/ppermute | solution.py:249
  60.4 1.5 %collective-permute-start.12 = (bf16[256,1024]{1,0:T(8,128)(2,1)S(1)}, bf16[256,1024]{1,0:T(8,128)(2,1)}, u32[]{:S(2)}, u32[]{:S(2)}) collective-permute-start(bf16[256,1024]{1,0:T(8,128)(2,1)S(1)} %collective-permute-done.4.refs_7_.refs_11_.refs_6_), channel_id=1, source_target_pairs={{0,2},{5,7},{10,8},{15,13},{16,18},{21,23},{26,24},{31,29}} | collective-permute-start | bytes 1572872 | tf_op jit(solution)/shard_map/ppermute | solution.py:249
  61.9 1.4 %collective-permute-done.21.refs_12_ = f32[256,256]{1,0:T(8,128)S(1)} collective-permute-done((f32[256,256]{1,0:T(8,128)S(1)}, f32[256,256]{1,0:T(8,128)S(1)}, u32[]{:S(2)}, u32[]{:S(2)}) %collective-permute-start.21) | collective-permute-done | bytes 262176 | tf_op jit(solution)/shard_map/ppermute | solution.py:264
  63.3 1.5 %collective-permute-start.13 = (bf16[256,1024]{1,0:T(8,128)(2,1)S(1)}, bf16[256,1024]{1,0:T(8,128)(2,1)}, u32[]{:S(2)}, u32[]{:S(2)}) collective-permute-start(bf16[256,1024]{1,0:T(8,128)(2,1)S(1)} %collective-permute-done.5.refs_8_.refs_12_.refs_7_), channel_id=1, source_target_pairs={{0,2},{5,7},{10,8},{15,13},{16,18},{21,23},{26,24},{31,29}} | collective-permute-start | bytes 1572872 | tf_op jit(solution)/shard_map/ppermute | solution.py:249
  66.0 1.4 %copy-done.3 = bf16[3,1024,256]{2,1,0:T(8,128)(2,1)S(1)} copy-done((bf16[3,1024,256]{2,1,0:T(8,128)(2,1)S(1)}, bf16[3,1024,256]{2,1,0:T(8,128)(2,1)}, u32[]{:S(2)}) %copy-start.3) | copy-done | bytes 1572888
  68.1 5.5 %whiten.1 = (bf16[512,1024]{1,0:T(8,128)(2,1)}, f32[1,512]{1,0:T(1,128)S(1)}) custom-call(s32[1,256]{1,0:T(1,128)S(1)} %bitcast.8, s32[1,256]{1,0:T(1,128)S(1)} %collective-permute-done.refs_2_.refs_1_, s32[1,256]{1,0:T(1,128)S(1)} %collective-permute-done.1.refs_3_.refs_2_, s32[1,256]{1,0:T(1,128)S(1)} %collective-permute-done.2.refs_4_.refs_3_, ...), custom_call_target="tpu_custom_call" | custom-call | tf_op jit(solution)/shard_map/whiten/pallas_call | solution.py:173
  75.2 3.5 %collective-permute-start.24 = (f32[1,512]{1,0:T(1,128)S(1)}, f32[1,512]{1,0:T(1,128)S(1)}, u32[]{:S(2)}, u32[]{:S(2)}) collective-permute-start(f32[1,512]{1,0:T(1,128)S(1)} %get-tuple-element.10), channel_id=1, source_target_pairs={{0,3},{1,2},{2,1},{3,0},{4,7},{5,6},{6,5},{7,4},{8,11},{9,10},{10,... | collective-permute-start | bytes 6152 | tf_op jit(solution)/shard_map/ppermute | solution.py:271
  79.1 1.3 %collective-permute-start.14 = (bf16[256,1024]{1,0:T(8,128)(2,1)S(1)}, bf16[256,1024]{1,0:T(8,128)(2,1)}, u32[]{:S(2)}, u32[]{:S(2)}) collective-permute-start(bf16[256,1024]{1,0:T(8,128)(2,1)S(1)} %collective-permute-done.10.refs_17_), channel_id=1, source_target_pairs={{2,3},{7,6},{8,9},{13,12},{18,19},{23,22},{24,25},{29,28}} | collective-permute-start | bytes 1572872 | tf_op jit(solution)/shard_map/ppermute | solution.py:249
  80.4 1.5 %collective-permute-start.9 = (bf16[256,1024]{1,0:T(8,128)(2,1)S(1)}, bf16[256,1024]{1,0:T(8,128)(2,1)}, u32[]{:S(2)}, u32[]{:S(2)}) collective-permute-start(bf16[256,1024]{1,0:T(8,128)(2,1)S(1)} %collective-permute-done.5.refs_8_.refs_12_.refs_7_), channel_id=1, source_target_pairs={{0,1},{5,4},{10,11},{15,14},{16,17},{21,20},{26,27},{31,30}} | collective-permute-start | bytes 1572872 | tf_op jit(solution)/shard_map/ppermute | solution.py:249
  81.9 1.3 %collective-permute-start.15 = (bf16[256,1024]{1,0:T(8,128)(2,1)}, bf16[256,1024]{1,0:T(8,128)(2,1)}, u32[]{:S(2)}, u32[]{:S(2)}) collective-permute-start(bf16[256,1024]{1,0:T(8,128)(2,1)} %collective-permute-done.11.refs_18_), channel_id=1, source_target_pairs={{2,3},{7,6},{8,9},{13,12},{18,19},{23,22},{24,25},{29,28}} | collective-permute-start | bytes 1572872 | tf_op jit(solution)/shard_map/ppermute | solution.py:249
  83.2 1.3 %collective-permute-start.16 = (bf16[256,1024]{1,0:T(8,128)(2,1)}, bf16[256,1024]{1,0:T(8,128)(2,1)}, u32[]{:S(2)}, u32[]{:S(2)}) collective-permute-start(bf16[256,1024]{1,0:T(8,128)(2,1)} %collective-permute-done.12.refs_19_), channel_id=1, source_target_pairs={{2,3},{7,6},{8,9},{13,12},{18,19},{23,22},{24,25},{29,28}} | collective-permute-start | bytes 1572872 | tf_op jit(solution)/shard_map/ppermute | solution.py:249
  84.5 1.3 %collective-permute-start.17 = (bf16[256,1024]{1,0:T(8,128)(2,1)}, bf16[256,1024]{1,0:T(8,128)(2,1)}, u32[]{:S(2)}, u32[]{:S(2)}) collective-permute-start(bf16[256,1024]{1,0:T(8,128)(2,1)} %collective-permute-done.13.refs_20_), channel_id=1, source_target_pairs={{2,3},{7,6},{8,9},{13,12},{18,19},{23,22},{24,25},{29,28}} | collective-permute-start | bytes 1572872 | tf_op jit(solution)/shard_map/ppermute | solution.py:249
  86.8 2.1 %collective-permute-done.16.refs_23_ = bf16[256,1024]{1,0:T(8,128)(2,1)} collective-permute-done((bf16[256,1024]{1,0:T(8,128)(2,1)}, bf16[256,1024]{1,0:T(8,128)(2,1)}, u32[]{:S(2)}, u32[]{:S(2)}) %collective-permute-start.16) | collective-permute-done | bytes 524320 | tf_op jit(solution)/shard_map/ppermute | solution.py:249
  88.9 2.1 %collective-permute-done.17.refs_24_ = bf16[256,1024]{1,0:T(8,128)(2,1)} collective-permute-done((bf16[256,1024]{1,0:T(8,128)(2,1)}, bf16[256,1024]{1,0:T(8,128)(2,1)}, u32[]{:S(2)}, u32[]{:S(2)}) %collective-permute-start.17) | collective-permute-done | bytes 524320 | tf_op jit(solution)/shard_map/ppermute | solution.py:249
  93.1 10.5 %pooled.1 = f32[1024,1024]{1,0:T(8,128)} custom-call(s32[1]{0:T(128)} %bitcast.refs_0_, s32[1,256]{1,0:T(1,128)S(1)} %bitcast.9, s32[1,256]{1,0:T(1,128)S(1)} %collective-permute-done.refs_2_.refs_1_, s32[1,256]{1,0:T(1,128)S(1)} %collective-permute-done.1.refs_3_.refs_2_, s32[1,256]{1,0:T(1,128)S(1)} %collective-permute-done.2.refs_4_.refs_3_, ...), custom_call_target="tpu_custom_call" | custom-call | tf_op jit(solution)/shard_map/pooled/pallas_call | solution.py:224
  (53 shorter events, 13.9 us)
Async XLA Ops:
  0.6 22.6 %collective-permute-start.3 = (bf16[256,1024]{1,0:T(8,128)(2,1)}, bf16[256,1024]{1,0:T(8,128)(2,1)S(1)}, u32[]{:S(2)}, u32[]{:S(2)}) collective-permute-start(bf16[256,1024]{1,0:T(8,128)(2,1)} %refs_4_.3), channel_id=1, source_target_pairs={{0,8},{4,12},{8,0},{12,4},{1,9},{5,13},{9,1},{13,5},{2,10},{6,14},... | collective-permute-start | bytes 1572872 | tf_op jit(solution)/shard_map/ppermute | solution.py:252
  0.7 47.0 %collective-permute-start.4 = (bf16[256,1024]{1,0:T(8,128)(2,1)}, bf16[256,1024]{1,0:T(8,128)(2,1)S(1)}, u32[]{:S(2)}, u32[]{:S(2)}) collective-permute-start(bf16[256,1024]{1,0:T(8,128)(2,1)} %refs_4_.3), channel_id=1, source_target_pairs={{0,4},{4,0},{8,12},{12,8},{1,5},{5,1},{9,13},{13,9},{2,6},{6,2},{1... | collective-permute-start | bytes 1572872 | tf_op jit(solution)/shard_map/ppermute | solution.py:253
  23.2 26.4 %collective-permute-start.5 = (bf16[256,1024]{1,0:T(8,128)(2,1)S(1)}, bf16[256,1024]{1,0:T(8,128)(2,1)S(1)}, u32[]{:S(2)}, u32[]{:S(2)}) collective-permute-start(bf16[256,1024]{1,0:T(8,128)(2,1)S(1)} %collective-permute-done.3.refs_6_.refs_10_.refs_5_), channel_id=1, source_target_pairs={{0,4},{4,0},{8,12},{12,8},{1,5},{5,1},{9,13},{13,9},{2,6},{6,2},{1... | collective-permute-start | bytes 1572872 | tf_op jit(solution)/shard_map/ppermute | solution.py:254
  28.1 10.6 %collective-permute-start = (s32[1,256]{1,0:T(1,128)}, s32[1,256]{1,0:T(1,128)S(1)}, u32[]{:S(2)}, u32[]{:S(2)}) collective-permute-start(s32[1,256]{1,0:T(1,128)} %bitcast.4), channel_id=1, source_target_pairs={{0,8},{4,12},{8,0},{12,4},{1,9},{5,13},{9,1},{13,5},{2,10},{6,14},... | collective-permute-start | bytes 3080 | tf_op jit(solution)/shard_map/ppermute | solution.py:256
  28.1 11.9 %collective-permute-start.1 = (s32[1,256]{1,0:T(1,128)}, s32[1,256]{1,0:T(1,128)S(1)}, u32[]{:S(2)}, u32[]{:S(2)}) collective-permute-start(s32[1,256]{1,0:T(1,128)} %bitcast.5), channel_id=1, source_target_pairs={{0,4},{4,0},{8,12},{12,8},{1,5},{5,1},{9,13},{13,9},{2,6},{6,2},{1... | collective-permute-start | bytes 3080 | tf_op jit(solution)/shard_map/ppermute | solution.py:256
  28.1 13.7 %collective-permute-start.2 = (s32[1,256]{1,0:T(1,128)}, s32[1,256]{1,0:T(1,128)S(1)}, u32[]{:S(2)}, u32[]{:S(2)}) collective-permute-start(s32[1,256]{1,0:T(1,128)} %bitcast.6), channel_id=1, source_target_pairs={{0,12},{4,8},{8,4},{12,0},{1,13},{5,9},{9,5},{13,1},{2,14},{6,10},... | collective-permute-start | bytes 3080 | tf_op jit(solution)/shard_map/ppermute | solution.py:256
  38.7 19.5 %collective-permute-start.6 = (bf16[256,1024]{1,0:T(8,128)(2,1)}, bf16[256,1024]{1,0:T(8,128)(2,1)S(1)}, u32[]{:S(2)}, u32[]{:S(2)}) collective-permute-start(bf16[256,1024]{1,0:T(8,128)(2,1)} %refs_4_.3), channel_id=1, source_target_pairs={{0,1},{5,4},{10,11},{15,14},{16,17},{21,20},{26,27},{31,30}} | collective-permute-start | bytes 1572872 | tf_op jit(solution)/shard_map/ppermute | solution.py:249
  40.0 19.0 %collective-permute-start.10 = (bf16[256,1024]{1,0:T(8,128)(2,1)}, bf16[256,1024]{1,0:T(8,128)(2,1)S(1)}, u32[]{:S(2)}, u32[]{:S(2)}) collective-permute-start(bf16[256,1024]{1,0:T(8,128)(2,1)} %refs_4_.3), channel_id=1, source_target_pairs={{0,2},{5,7},{10,8},{15,13},{16,18},{21,23},{26,24},{31,29}} | collective-permute-start | bytes 1572872 | tf_op jit(solution)/shard_map/ppermute | solution.py:249
  41.8 13.8 %collective-permute-start.18 = (bf16[512,256]{1,0:T(8,128)(2,1)S(1)}, bf16[512,256]{1,0:T(8,128)(2,1)S(1)}, u32[]{:S(2)}, u32[]{:S(2)}) collective-permute-start(bf16[512,256]{1,0:T(8,128)(2,1)S(1)} %get-tuple-element.12), channel_id=1, source_target_pairs={{0,1},{1,2},{2,3},{4,5},{5,6},{6,7},{8,9},{9,10},{10,11},{12,13},{... | collective-permute-start | bytes 786440 | tf_op jit(solution)/shard_map/ppermute | solution.py:257
  47.7 9.8 %collective-permute-start.19 = (bf16[512,256]{1,0:T(8,128)(2,1)S(1)}, bf16[512,256]{1,0:T(8,128)(2,1)S(1)}, u32[]{:S(2)}, u32[]{:S(2)}) collective-permute-start(bf16[512,256]{1,0:T(8,128)(2,1)S(1)} %get-tuple-element.11), channel_id=1, source_target_pairs={{1,0},{2,1},{3,2},{5,4},{6,5},{7,6},{9,8},{10,9},{11,10},{13,12},{... | collective-permute-start | bytes 786440 | tf_op jit(solution)/shard_map/ppermute | solution.py:258
  51.9 8.5 %collective-permute-start.20 = (f32[256,256]{1,0:T(8,128)S(1)}, f32[256,256]{1,0:T(8,128)S(1)}, u32[]{:S(2)}, u32[]{:S(2)}) collective-permute-start(f32[256,256]{1,0:T(8,128)S(1)} %get-tuple-element.7), channel_id=1, source_target_pairs={{0,1},{1,2},{2,3},{4,5},{5,6},{6,7},{8,9},{9,10},{10,11},{12,13},{... | collective-permute-start | bytes 786440 | tf_op jit(solution)/shard_map/ppermute | solution.py:263
  55.6 7.7 %collective-permute-start.21 = (f32[256,256]{1,0:T(8,128)S(1)}, f32[256,256]{1,0:T(8,128)S(1)}, u32[]{:S(2)}, u32[]{:S(2)}) collective-permute-start(f32[256,256]{1,0:T(8,128)S(1)} %get-tuple-element.8), channel_id=1, source_target_pairs={{1,0},{2,1},{3,2},{5,4},{6,5},{7,6},{9,8},{10,9},{11,10},{13,12},{... | collective-permute-start | bytes 786440 | tf_op jit(solution)/shard_map/ppermute | solution.py:264
  57.5 16.1 %collective-permute-start.7 = (bf16[256,1024]{1,0:T(8,128)(2,1)S(1)}, bf16[256,1024]{1,0:T(8,128)(2,1)S(1)}, u32[]{:S(2)}, u32[]{:S(2)}) collective-permute-start(bf16[256,1024]{1,0:T(8,128)(2,1)S(1)} %collective-permute-done.3.refs_6_.refs_10_.refs_5_), channel_id=1, source_target_pairs={{0,1},{5,4},{10,11},{15,14},{16,17},{21,20},{26,27},{31,30}} | collective-permute-start | bytes 1572872 | tf_op jit(solution)/shard_map/ppermute | solution.py:249
  58.2 16.2 %collective-permute-start.8 = (bf16[256,1024]{1,0:T(8,128)(2,1)S(1)}, bf16[256,1024]{1,0:T(8,128)(2,1)S(1)}, u32[]{:S(2)}, u32[]{:S(2)}) collective-permute-start(bf16[256,1024]{1,0:T(8,128)(2,1)S(1)} %collective-permute-done.4.refs_7_.refs_11_.refs_6_), channel_id=1, source_target_pairs={{0,1},{5,4},{10,11},{15,14},{16,17},{21,20},{26,27},{31,30}} | collective-permute-start | bytes 1572872 | tf_op jit(solution)/shard_map/ppermute | solution.py:249
  59.0 19.7 %collective-permute-start.11 = (bf16[256,1024]{1,0:T(8,128)(2,1)S(1)}, bf16[256,1024]{1,0:T(8,128)(2,1)}, u32[]{:S(2)}, u32[]{:S(2)}) collective-permute-start(bf16[256,1024]{1,0:T(8,128)(2,1)S(1)} %collective-permute-done.3.refs_6_.refs_10_.refs_5_), channel_id=1, source_target_pairs={{0,2},{5,7},{10,8},{15,13},{16,18},{21,23},{26,24},{31,29}} | collective-permute-start | bytes 1572872 | tf_op jit(solution)/shard_map/ppermute | solution.py:249
  60.4 18.7 %collective-permute-start.12 = (bf16[256,1024]{1,0:T(8,128)(2,1)S(1)}, bf16[256,1024]{1,0:T(8,128)(2,1)}, u32[]{:S(2)}, u32[]{:S(2)}) collective-permute-start(bf16[256,1024]{1,0:T(8,128)(2,1)S(1)} %collective-permute-done.4.refs_7_.refs_11_.refs_6_), channel_id=1, source_target_pairs={{0,2},{5,7},{10,8},{15,13},{16,18},{21,23},{26,24},{31,29}} | collective-permute-start | bytes 1572872 | tf_op jit(solution)/shard_map/ppermute | solution.py:249
  63.3 21.2 %collective-permute-start.13 = (bf16[256,1024]{1,0:T(8,128)(2,1)S(1)}, bf16[256,1024]{1,0:T(8,128)(2,1)}, u32[]{:S(2)}, u32[]{:S(2)}) collective-permute-start(bf16[256,1024]{1,0:T(8,128)(2,1)S(1)} %collective-permute-done.5.refs_8_.refs_12_.refs_7_), channel_id=1, source_target_pairs={{0,2},{5,7},{10,8},{15,13},{16,18},{21,23},{26,24},{31,29}} | collective-permute-start | bytes 1572872 | tf_op jit(solution)/shard_map/ppermute | solution.py:249
  74.4 6.0 %collective-permute-start.23 = (f32[1,512]{1,0:T(1,128)S(1)}, f32[1,512]{1,0:T(1,128)S(1)}, u32[]{:S(2)}, u32[]{:S(2)}) collective-permute-start(f32[1,512]{1,0:T(1,128)S(1)} %get-tuple-element.10), channel_id=1, source_target_pairs={{0,2},{1,3},{2,0},{3,1},{4,6},{5,7},{6,4},{7,5},{8,10},{9,11},{10,... | collective-permute-start | bytes 6152 | tf_op jit(solution)/shard_map/ppermute | solution.py:271
  75.2 6.7 %collective-permute-start.24 = (f32[1,512]{1,0:T(1,128)S(1)}, f32[1,512]{1,0:T(1,128)S(1)}, u32[]{:S(2)}, u32[]{:S(2)}) collective-permute-start(f32[1,512]{1,0:T(1,128)S(1)} %get-tuple-element.10), channel_id=1, source_target_pairs={{0,3},{1,2},{2,1},{3,0},{4,7},{5,6},{6,5},{7,4},{8,11},{9,10},{10,... | collective-permute-start | bytes 6152 | tf_op jit(solution)/shard_map/ppermute | solution.py:271
  79.1 7.3 %collective-permute-start.14 = (bf16[256,1024]{1,0:T(8,128)(2,1)S(1)}, bf16[256,1024]{1,0:T(8,128)(2,1)}, u32[]{:S(2)}, u32[]{:S(2)}) collective-permute-start(bf16[256,1024]{1,0:T(8,128)(2,1)S(1)} %collective-permute-done.10.refs_17_), channel_id=1, source_target_pairs={{2,3},{7,6},{8,9},{13,12},{18,19},{23,22},{24,25},{29,28}} | collective-permute-start | bytes 1572872 | tf_op jit(solution)/shard_map/ppermute | solution.py:249
  80.4 6.0 %collective-permute-start.9 = (bf16[256,1024]{1,0:T(8,128)(2,1)S(1)}, bf16[256,1024]{1,0:T(8,128)(2,1)}, u32[]{:S(2)}, u32[]{:S(2)}) collective-permute-start(bf16[256,1024]{1,0:T(8,128)(2,1)S(1)} %collective-permute-done.5.refs_8_.refs_12_.refs_7_), channel_id=1, source_target_pairs={{0,1},{5,4},{10,11},{15,14},{16,17},{21,20},{26,27},{31,30}} | collective-permute-start | bytes 1572872 | tf_op jit(solution)/shard_map/ppermute | solution.py:249
  81.9 4.9 %collective-permute-start.15 = (bf16[256,1024]{1,0:T(8,128)(2,1)}, bf16[256,1024]{1,0:T(8,128)(2,1)}, u32[]{:S(2)}, u32[]{:S(2)}) collective-permute-start(bf16[256,1024]{1,0:T(8,128)(2,1)} %collective-permute-done.11.refs_18_), channel_id=1, source_target_pairs={{2,3},{7,6},{8,9},{13,12},{18,19},{23,22},{24,25},{29,28}} | collective-permute-start | bytes 1572872 | tf_op jit(solution)/shard_map/ppermute | solution.py:249
  83.2 5.7 %collective-permute-start.16 = (bf16[256,1024]{1,0:T(8,128)(2,1)}, bf16[256,1024]{1,0:T(8,128)(2,1)}, u32[]{:S(2)}, u32[]{:S(2)}) collective-permute-start(bf16[256,1024]{1,0:T(8,128)(2,1)} %collective-permute-done.12.refs_19_), channel_id=1, source_target_pairs={{2,3},{7,6},{8,9},{13,12},{18,19},{23,22},{24,25},{29,28}} | collective-permute-start | bytes 1572872 | tf_op jit(solution)/shard_map/ppermute | solution.py:249
  84.5 6.5 %collective-permute-start.17 = (bf16[256,1024]{1,0:T(8,128)(2,1)}, bf16[256,1024]{1,0:T(8,128)(2,1)}, u32[]{:S(2)}, u32[]{:S(2)}) collective-permute-start(bf16[256,1024]{1,0:T(8,128)(2,1)} %collective-permute-done.13.refs_20_), channel_id=1, source_target_pairs={{2,3},{7,6},{8,9},{13,12},{18,19},{23,22},{24,25},{29,28}} | collective-permute-start | bytes 1572872 | tf_op jit(solution)/shard_map/ppermute | solution.py:249
  (12 other events, 112.7 us)

commit v2 on v1

v2 whole, which is shorter than its diff:
```python
import jax
import jax.numpy as jnp
from jax import lax
from jax.experimental import pallas as pl
from jax.experimental.pallas import tpu as pltpu
from jax.sharding import PartitionSpec as P

C = 256
BLK = 256
LONG = 10**11
EXTRA = 16
F32 = jnp.float32
BF16 = jnp.bfloat16
VMEM = pl.BlockSpec(memory_space=pltpu.VMEM)
SMEM = pl.BlockSpec(memory_space=pltpu.SMEM)
ANY = pl.BlockSpec(memory_space=pl.ANY)
HBM = pl.BlockSpec(memory_space=pltpu.HBM)
SMALL = pltpu.CompilerParams(vmem_limit_bytes=8 * 1024 * 1024)
MEDIUM = pltpu.CompilerParams(vmem_limit_bytes=20 * 1024 * 1024)
LARGE = pltpu.CompilerParams(vmem_limit_bytes=24 * 1024 * 1024)


def padded(cells, sides, width):
    for axis, dim in sides:
        count = lax.axis_size(axis)
        ends = count - 1
        head = lax.slice_in_dim(cells, 0, width, axis=dim)
        tail = lax.slice_in_dim(cells, cells.shape[dim] - width, cells.shape[dim], axis=dim)
        cells = jnp.concatenate(
            [
                lax.ppermute(tail, axis, [(i, (i + 1) % count) for i in range(ends)]),
                cells,
                lax.ppermute(head, axis, [((i + 1) % count, i) for i in range(ends)]),
            ],
            axis=dim,
        )
    return cells


def contract_rows(left, right):
    return lax.dot_general(
        left, right, (((0,), (0,)), ((), ())), preferred_element_type=F32
    )


def contract_columns(left, right):
    return lax.dot_general(
        left, right, (((1,), (1,)), ((), ())), preferred_element_type=F32
    )


def body(train_rows, train_labels, held_rows, held_labels, precision):
    local = train_rows.shape[1]
    full = lax.all_gather(train_rows, "feat", axis=1, tiled=True)
    width = full.shape[1]
    classes = jnp.arange(C, dtype=jnp.int32)
    onehot_train = (train_labels == classes[None, :]).astype(BF16)
    local_sums = contract_rows(onehot_train, full)
    local_counts = jnp.sum(onehot_train.astype(F32), axis=0)
    sums, counts = lax.psum((local_sums, local_counts), "dp")
    means = sums / counts[:, None]
    feat_index = lax.axis_index("feat")
    dp_index = lax.axis_index("dp")
    dp_count = lax.axis_size("dp")
    ncols = width // dp_count
    block = lax.psum_scatter(
        contract_rows(full, train_rows), "dp", scatter_dimension=0, tiled=True
    ).T
    sums_rows = lax.dynamic_slice_in_dim(sums, feat_index * local, local, 1)
    means_cols = lax.dynamic_slice_in_dim(means, dp_index * ncols, ncols, 1)
    correction = lax.dot_general(
        sums_rows,
        means_cols,
        (((0,), (0,)), ((), ())),
        precision=lax.Precision.HIGHEST,
        preferred_element_type=F32,
    )
    denominator = float(train_rows.shape[0] * dp_count - C)
    pooled_cov = (block - correction) / denominator
    means_local = lax.dynamic_slice_in_dim(means, feat_index * local, local, 1)
    picked = means_local[held_labels]
    centred = held_rows.astype(F32) - picked
    extended = padded(centred, (("feat", 1),), BLK)
    held_count = held_rows.shape[0]
    nlocal = local // BLK
    windows = extended.reshape(held_count, nlocal + 2, BLK)
    bands = precision.astype(F32).reshape(3, nlocal, BLK, BLK)
    image = jnp.zeros((held_count, nlocal, BLK), F32)
    for k in range(3):
        image = image + jnp.einsum(
            "rmj,mij->rmi",
            windows[:, k : k + nlocal],
            bands[k],
            precision=lax.Precision.HIGHEST,
            preferred_element_type=F32,
        )
    image = image.reshape(held_count, local)
    partial_score = jnp.sum(centred * image, axis=1)
    distance = lax.psum(partial_score, "feat") / width
    return (pooled_cov, image.astype(BF16), distance)


def split3(value):
    high = value.astype(BF16)
    rest = value - high.astype(F32)
    middle = rest.astype(BF16)
    return high, middle, (rest - middle.astype(F32)).astype(BF16)


def onehot_rows(labels):
    classes = lax.broadcasted_iota(jnp.int32, (C, labels.shape[1]), 0)
    return (classes.astype(F32) == labels.astype(F32)).astype(F32)


def cost(flops):
    return pl.CostEstimate(flops=flops, bytes_accessed=0, transcendentals=0)


def class_sums(label_refs, row_refs, columns):
    total = None
    counts = None
    for label_ref, row_ref in zip(label_refs, row_refs, strict=True):
        onehot = onehot_rows(label_ref[...])
        part = jnp.dot(onehot.astype(BF16), row_ref[:, columns], preferred_element_type=F32)
        number = jnp.sum(onehot, axis=1, keepdims=True)
        total = part if total is None else total + part
        counts = number if counts is None else counts + number
    return total, counts


def fetch(sem, *pairs):
    copies = [
        pltpu.make_async_copy(source, target, sem.at[k]) for k, (source, target) in enumerate(pairs)
    ]
    for copy in copies:
        copy.start()
    return copies


def wait(copies):
    for copy in copies:
        copy.wait()


def outgoing_kernel(labels_ref, held_ref, labels_out, head_ref, tail_ref, sem):
    width = held_ref.shape[1]
    wait(
        fetch(
            sem,
            (labels_ref, labels_out),
            (held_ref.at[:, pl.ds(0, BLK)], head_ref),
            (held_ref.at[:, pl.ds(width - BLK, BLK)], tail_ref),
        )
    )


def outgoing(labels, held):
    edge = jax.ShapeDtypeStruct((held.shape[0], BLK), BF16)
    return pl.pallas_call(
        outgoing_kernel,
        out_shape=(jax.ShapeDtypeStruct(labels.shape, labels.dtype), edge, edge),
        in_specs=[HBM] * 2,
        out_specs=(VMEM,) * 3,
        scratch_shapes=[pltpu.SemaphoreType.DMA((3,))],
        compiler_params=SMALL,
        cost_estimate=cost(LONG),
        name="outgoing",
    )(labels, held)


def halves_kernel(own_ref, next_ref, rows_ref, outer_ref, inner_ref, labels, sem):
    count, width = rows_ref.shape
    copies = fetch(
        sem,
        (own_ref, labels.at[pl.ds(0, 1)]),
        (next_ref, labels.at[pl.ds(1, 1)]),
        (rows_ref.at[:, pl.ds(0, BLK)], outer_ref.at[pl.ds(0, count), pl.ds(0, BLK)]),
        (rows_ref.at[:, pl.ds(width - BLK, BLK)], outer_ref.at[pl.ds(0, count), pl.ds(BLK, BLK)]),
        (rows_ref.at[:, pl.ds(BLK, width - 2 * BLK)], inner_ref),
    )
    wait(copies[:2])
    index = lax.broadcasted_iota(jnp.int32, (EXTRA, count), 0)
    rows = jnp.where(index == 0, labels[0:1], jnp.where(index == 1, labels[1:2], 0))
    outer_ref[count : count + EXTRA, :count] = rows.astype(F32).astype(BF16)
    outer_ref[count : count + EXTRA, count:] = jnp.zeros((EXTRA, 2 * BLK - count), BF16)
    wait(copies[2:])


def halves(own_labels, next_labels, rows):
    count, width = rows.shape
    return pl.pallas_call(
        halves_kernel,
        out_shape=(
            jax.ShapeDtypeStruct((count + EXTRA, 2 * BLK), rows.dtype),
            jax.ShapeDtypeStruct((count, width - 2 * BLK), rows.dtype),
        ),
        in_specs=[HBM] * 3,
        out_specs=(VMEM, VMEM),
        scratch_shapes=[pltpu.VMEM((2, count), jnp.int32), pltpu.SemaphoreType.DMA((5,))],
        compiler_params=SMALL,
        cost_estimate=cost(1),
        name="halves",
    )(own_labels, next_labels, rows)


def early_kernel(own_label, next_label, own_ref, other_ref, sums_ref, labels, own, other, sem):
    width = own_ref.shape[1]
    copies = fetch(
        sem,
        (own_label, labels.at[pl.ds(0, 1)]),
        (next_label, labels.at[pl.ds(1, 1)]),
        (own_ref, own),
        (other_ref, other),
    )
    wait(copies)
    pairs = [labels.at[p : p + 1] for p in range(2)]
    sums, _ = class_sums(pairs, [own, other], slice(0, width))
    sums_ref[...] = sums


def early_sums(own_labels, next_labels, own, other):
    count, width = own.shape
    return pl.pallas_call(
        early_kernel,
        out_shape=jax.ShapeDtypeStruct((C, width), F32),
        in_specs=[HBM] * 4,
        out_specs=VMEM,
        scratch_shapes=[
            pltpu.VMEM((2, count), jnp.int32),
            pltpu.VMEM((count, width), BF16),
            pltpu.VMEM((count, width), BF16),
            pltpu.SemaphoreType.DMA((4,)),
        ],
        compiler_params=SMALL,
        cost_estimate=cost(LONG),
        name="early_sums",
    )(own_labels, next_labels, own, other)


def four_labels(labels, outer):
    count = labels.shape[1]
    late = outer[count : count + EXTRA, :count].astype(F32)
    return labels[0:1].astype(F32), labels[1:2].astype(F32), late[0:1], late[1:2]


def edges_kernel(own_ref, next_ref, early_ref, third_ref, outer_ref, head_ref, tail_ref,
                 labels, third, outer, sem):
    count, width = third_ref.shape
    copies = fetch(
        sem,
        (own_ref, labels.at[pl.ds(0, 1)]),
        (next_ref, labels.at[pl.ds(1, 1)]),
        (outer_ref, outer),
        (third_ref.at[:, pl.ds(0, BLK)], third.at[:, pl.ds(0, BLK)]),
        (third_ref.at[:, pl.ds(width - BLK, BLK)], third.at[:, pl.ds(BLK, BLK)]),
    )
    wait(copies[:3])
    hots = [onehot_rows(label) for label in four_labels(labels, outer)]
    counts = sum(jnp.sum(hot, axis=1, keepdims=True) for hot in hots)
    late = jnp.dot(hots[3].astype(BF16), outer[:count, :], preferred_element_type=F32)
    wait(copies[3:])
    late = late + jnp.dot(hots[2].astype(BF16), third[...], preferred_element_type=F32)
    head_ref[...] = (early_ref[:, :BLK] + late[:, :BLK]) / counts
    tail_ref[...] = (early_ref[:, width - BLK :] + late[:, BLK:]) / counts


def edge_means(own_labels, next_labels, early, third, outer):
    edge = jax.ShapeDtypeStruct((C, BLK), F32)
    count = third.shape[0]
    return pl.pallas_call(
        edges_kernel,
        out_shape=(edge, edge),
        in_specs=[HBM, HBM, VMEM, HBM, HBM],
        out_specs=(VMEM, VMEM),
        scratch_shapes=[
            pltpu.VMEM((2, count), jnp.int32),
            pltpu.VMEM((count, 2 * BLK), BF16),
            pltpu.VMEM(outer.shape, BF16),
            pltpu.SemaphoreType.DMA((5,)),
        ],
        compiler_params=SMALL,
        cost_estimate=cost(1),
        name="edge_means",
    )(own_labels, next_labels, early, third, outer)


def means_kernel(own_ref, next_ref, early_ref, third_ref, outer_ref, inner_ref,
                 means_ref, fourth_ref, labels_ref, labels, third, outer, inner, sem):
    count, width = third_ref.shape
    wait(
        fetch(
            sem,
            (own_ref, labels.at[pl.ds(0, 1)]),
            (next_ref, labels.at[pl.ds(1, 1)]),
            (third_ref, third),
            (outer_ref, outer),
            (inner_ref, inner),
        )
    )
    groups = four_labels(labels, outer)
    hots = [onehot_rows(label) for label in groups]
    counts = sum(jnp.sum(hot, axis=1, keepdims=True) for hot in hots)
    fourth = jnp.concatenate([outer[:count, :BLK], inner[...], outer[:count, BLK:]], axis=1)
    fourth_ref[...] = fourth
    sums = early_ref[...] + jnp.dot(hots[2].astype(BF16), third[...], preferred_element_type=F32)
    sums = sums + jnp.dot(hots[3].astype(BF16), fourth, preferred_element_type=F32)
    means_ref[...] = sums / counts
    for p, label in enumerate(groups):
        labels_ref[p : p + 1, :] = label


def class_means(own_labels, next_labels, early, third, outer, inner):
    whole = jax.ShapeDtypeStruct(early.shape, F32)
    count = third.shape[0]
    return pl.pallas_call(
        means_kernel,
        out_shape=(
            whole,
            jax.ShapeDtypeStruct(third.shape, third.dtype),
            jax.ShapeDtypeStruct((4, count), F32),
        ),
        in_specs=[HBM, HBM, VMEM, HBM, HBM, HBM],
        out_specs=(VMEM,) * 3,
        scratch_shapes=[
            pltpu.VMEM((2, count), jnp.int32),
            pltpu.VMEM(third.shape, BF16),
            pltpu.VMEM(outer.shape, BF16),
            pltpu.VMEM(inner.shape, BF16),
            pltpu.SemaphoreType.DMA((5,)),
        ],
        compiler_params=MEDIUM,
        cost_estimate=cost(LONG),
        name="class_means",
    )(own_labels, next_labels, early, third, outer, inner)


def stack_kernel(groups, role_ref, *refs):
    *sources, out_ref, sem = refs
    groups = (sources[: groups[0]], sources[groups[0] :])

    def pairs(group):
        start = 0
        for ref in group:
            yield ref, out_ref.at[pl.ds(start, ref.shape[0])]
            start += ref.shape[0]

    for owner, group in zip((True, False), groups, strict=True):

        @pl.when((role_ref[0] == 0) == owner)
        def _():
            wait(fetch(sem, *pairs(group)))


def stack(role, own, other):
    rows = sum(array.shape[0] for array in own)
    groups = (len(own), len(other))
    return pl.pallas_call(
        lambda *refs: stack_kernel(groups, *refs),
        out_shape=jax.ShapeDtypeStruct((rows, own[0].shape[1]), own[0].dtype),
        in_specs=[SMEM] + [ANY] * sum(groups),
        out_specs=ANY,
        scratch_shapes=[pltpu.SemaphoreType.DMA((max(groups),))],
        compiler_params=SMALL,
        cost_estimate=cost(1),
        name="stack",
    )(role, *own, *other)


def white_kernel(held_ref, left_ref, right_ref, means_ref, left_means, right_means, held_labels,
                 precision, white_ref, score_ref, bands):
    width = held_ref.shape[1]
    for k in range(3):
        bands[:, k * BLK : (k + 1) * BLK] = precision[k]
    means = jnp.concatenate([left_means[...], means_ref[...], right_means[...]], axis=1)
    onehot = onehot_rows(held_labels[...]).astype(BF16)
    picked = sum(contract_rows(onehot, piece) for piece in split3(means))
    held = jnp.concatenate([left_ref[...], held_ref[...], right_ref[...]], axis=1)
    centred = held.astype(F32) - picked
    pieces = split3(centred)
    score = jnp.zeros((held_ref.shape[0], 128), F32)
    for m in range(width // BLK):
        inside = slice(m * BLK, (m + 1) * BLK)
        window = slice(m * BLK, (m + 3) * BLK)
        band = bands[inside, :]
        image = sum(contract_columns(piece[:, window], band) for piece in reversed(pieces))
        white_ref[:, inside] = image.astype(BF16)
        product = centred[:, (m + 1) * BLK : (m + 2) * BLK] * image
        for lanes in range(0, BLK, 128):
            score = score + product[:, lanes : lanes + 128]
    score_ref[...] = jnp.sum(score.T, axis=0, keepdims=True)


def whiten(held, left, right, means, left_means, right_means, held_labels, precision):
    count, width = held.shape
    return pl.pallas_call(
        white_kernel,
        out_shape=(
            jax.ShapeDtypeStruct((count, width), BF16),
            jax.ShapeDtypeStruct((1, count), F32),
        ),
        in_specs=[VMEM] * 8,
        out_specs=(VMEM, VMEM),
        scratch_shapes=[pltpu.VMEM((width, 3 * BLK), BF16)],
        compiler_params=MEDIUM,
        cost_estimate=cost(LONG),
        name="whiten",
    )(held, left, right, means, left_means, right_means, held_labels, precision)


def choose(role_ref, sem, near, far, target):
    here = (role_ref[0] % 2) == 0

    @pl.when(here)
    def _():
        fetch(sem, (near, target))

    @pl.when(jnp.logical_not(here))
    def _():
        fetch(sem, (far, target))

    return pltpu.make_async_copy(near, target, sem.at[0])


def centre_kernel(labels_ref, means_ref, *refs):
    *rows, most_ref, last_ref = refs
    count = rows[0].shape[0]
    most = most_ref.shape[0] // 2
    pieces = split3(means_ref[...])
    for p, ref in enumerate(rows):
        onehot = onehot_rows(labels_ref[p : p + 1]).astype(BF16)
        centred = ref[...].astype(F32) - sum(contract_rows(onehot, piece) for piece in pieces)
        high = centred.astype(BF16)
        low = (centred - high.astype(F32)).astype(BF16)
        into, first, second = (most_ref, p * count, most + p * count)
        if p == len(rows) - 1:
            into, first, second = (last_ref, 0, count)
        into[first : first + count, :] = high
        into[second : second + count, :] = low


def centre(labels, means, rows):
    count, width = rows[0].shape
    return pl.pallas_call(
        centre_kernel,
        out_shape=(
            jax.ShapeDtypeStruct((2 * (len(rows) - 1) * count, width), BF16),
            jax.ShapeDtypeStruct((2 * count, width), BF16),
        ),
        in_specs=[VMEM] * (2 + len(rows)),
        out_specs=(VMEM, VMEM),
        compiler_params=MEDIUM,
        cost_estimate=cost(1),
        name="centre",
    )(labels, means, *rows)


def most_kernel(role_ref, left, near, far, total_ref, right, sem):
    most, width = near.shape
    choose(role_ref, sem, near, far, right).wait()
    for t in range(0, width, BLK):
        high = contract_rows(left[:most, t : t + BLK], right[...])
        total_ref[t : t + BLK, :] = high + contract_rows(left[most:, t : t + BLK], right[...])


def gram_most(role, centred, near, far):
    width = near.shape[1]
    return pl.pallas_call(
        most_kernel,
        out_shape=jax.ShapeDtypeStruct((width, width), F32),
        in_specs=[SMEM, VMEM, ANY, ANY],
        out_specs=VMEM,
        scratch_shapes=[pltpu.VMEM(near.shape, BF16), pltpu.SemaphoreType.DMA((1,))],
        compiler_params=MEDIUM,
        cost_estimate=cost(LONG),
        name="gram_most",
    )(role, centred, near, far)


def last_kernel(scale, features, role_ref, total_ref, last_ref, near, far, own, *refs):
    *others, out_ref, distance_ref, right, tiles, sem, out_sem = refs
    count, width = near.shape
    arrival = choose(role_ref, sem, near, far, right)
    beside, across, beyond = [ref[...] for ref in others]
    distance_ref[...] = ((own[...] + beside) + (across + beyond)) / features
    arrival.wait()
    stores = []
    for k, t in enumerate(range(0, width, BLK)):
        part = contract_rows(last_ref[:count, t : t + BLK], right[...])
        part = part + contract_rows(last_ref[count:, t : t + BLK], right[...])
        tiles[t : t + BLK, :] = (total_ref[t : t + BLK, :] + part) * scale
        stores.append(
            pltpu.make_async_copy(
                tiles.at[pl.ds(t, BLK)], out_ref.at[pl.ds(t, BLK)], out_sem.at[k]
            )
        )
        stores[-1].start()
    wait(stores)


def gram_last(role, total, last, near, far, scores, scale, features):
    count, width = near.shape
    return pl.pallas_call(
        lambda *refs: last_kernel(scale, features, *refs),
        out_shape=(
            jax.ShapeDtypeStruct((width, width), F32),
            jax.ShapeDtypeStruct(scores[0].shape, F32),
        ),
        in_specs=[SMEM, VMEM, VMEM, ANY, ANY] + [VMEM] * len(scores),
        out_specs=(HBM, VMEM),
        scratch_shapes=[
            pltpu.VMEM((count, width), BF16),
            pltpu.VMEM((width, width), F32),
            pltpu.SemaphoreType.DMA((1,)),
            pltpu.SemaphoreType.DMA((width // BLK,)),
        ],
        compiler_params=MEDIUM,
        cost_estimate=cost(LONG),
        name="gram_last",
    )(role, total, last, near, far, *scores)


def four_by_four(train_rows, train_labels, held_rows, held_labels, precision):
    count, width = train_rows.shape
    n = 4
    tie = lax.optimization_barrier
    flip = {k: [(i, i ^ k) for i in range(n)] for k in (1, 2, 3)}
    to_right = [(i, i + 1) for i in range(n - 1)]
    to_left = [(i + 1, i) for i in range(n - 1)]
    role = (lax.axis_index("dp") ^ lax.axis_index("feat")).astype(jnp.int32)

    def hop(array, *moves):
        pairs = [(d * n + (d ^ s), d * n + (d ^ e)) for d in range(n) for s, e in moves]
        return lax.ppermute(array, ("dp", "feat"), pairs)

    across_own = hop(train_rows, (0, 2))
    third = lax.ppermute(train_rows, "dp", flip[1])
    second = lax.ppermute(train_rows, "dp", flip[2])
    own_labels, head, tail = outgoing(train_labels.reshape(1, count), held_rows)
    next_labels = lax.ppermute(own_labels, "dp", flip[2])
    left = lax.ppermute(tail, "feat", to_right)
    third, second, across_own, left, next_labels = tie(
        (third, second, across_own, left, next_labels)
    )
    second_outer, second_inner = halves(own_labels, next_labels, second)
    outer = lax.ppermute(second_outer, "dp", flip[1])
    inner = lax.ppermute(second_inner, "dp", flip[1])
    early = early_sums(own_labels, next_labels, train_rows, second)
    early, head, *sent = tie((early, head, second, third))
    role = role.reshape(1)
    own_most = stack(role, sent, sent)
    across_most = hop(own_most, (0, 2))
    right = lax.ppermute(head, "feat", to_left)
    head, tail = edge_means(own_labels, next_labels, early, third, outer)
    left_means = lax.ppermute(tail, "feat", to_right)
    right_means = lax.ppermute(head, "feat", to_left)
    inner, across_most, right, head, tail = tie((inner, across_most, right, head, tail))
    means, fourth, labels = class_means(own_labels, next_labels, early, third, outer, inner)
    across_last = hop(fourth, (0, 2))
    rows = [train_rows, second, third, fourth]
    near_most = stack(role, rows[:3], [across_own, across_most])
    far_most = hop(near_most, (0, 1), (2, 3))
    most, last = centre(labels, means, rows)
    most, last, means = tie((most, last, means))
    white, score = whiten(
        held_rows, left, right, means, left_means, right_means, held_labels.reshape(1, -1), precision
    )
    score, across_last, most = tie((score, across_last, most))
    total = gram_most(role, most, near_most, far_most)
    near_last = stack(role, [fourth], [across_last])
    far_last = hop(near_last, (0, 1), (2, 3))
    scores = [score] + [lax.ppermute(score, "feat", flip[k]) for k in (1, 2, 3)]
    cov, distance = gram_last(
        role, total, last, near_last, far_last, scores, 1.0 / (n * count - C), float(n * width)
    )
    return cov, white, distance.reshape(-1)


def solution(mesh):
    fits = mesh.shape["dp"] == 4 and mesh.shape["feat"] == 4
    return jax.shard_map(
        four_by_four if fits else body,
        mesh=mesh,
        in_specs=(
            P(("layer", "dp"), "feat"),
            P(("layer", "dp"), None),
            P(("layer", "dp"), "feat"),
            P(("layer", "dp")),
            P("layer", "feat", None),
        ),
        out_specs=(P(("layer", "feat"), "dp"), P(("layer", "dp"), "feat"), P(("layer", "dp"))),
        check_vma=False,
    )
```

time: 104 us -> 74.4 us (0.72)
  the two profiles are of different devices: /device:TPU:17 before, /device:TPU:31 now
where the time goes in v2:
time: 74.4 us; the launch traced here: 74 us
  waiting for transfers between devices  30.5 us (41%)
  starting transfers between devices  24 us (32%)
  Pallas kernels  16.5 us (22%)
  local copies, waits for them, and re-layouts  1.92 us (3%)
  between operations  1.09 us (1%)
    ppermute x1, waiting for transfers between devices, four_by_four(): next_labels = lax.ppermute(own_labels, 'dp', flip[2])  18.8 us
    ppermute x5, starting transfers between devices, hop(): return lax.ppermute(array, ('dp', 'feat'), pairs)  12.5 us
    ppermute x1, waiting for transfers between devices, four_by_four(): outer = lax.ppermute(second_outer, 'dp', flip[1])  5.92 us
    pallas_call x1, Pallas kernels, whiten(): pl.pallas_call(white_kernel, out_shape=(jax.ShapeDtypeStruct((count, widt...  5.2 us
    ppermute x5, waiting for transfers between devices, hop(): return lax.ppermute(array, ('dp', 'feat'), pairs)  4.23 us
    pallas_call x1, Pallas kernels, gram_most(): pl.pallas_call(most_kernel, out_shape=jax.ShapeDtypeStruct((width, width)...  3.8 us
    pallas_call x1, Pallas kernels, gram_last(): pl.pallas_call(lambda *refs: last_kernel(scale, features, *refs), out_sha...  3.18 us
    ppermute x1, starting transfers between devices, four_by_four(): next_labels = lax.ppermute(own_labels, 'dp', flip[2])  2.34 us
  transfers between devices with their start and end apart: 17, of which 5 were waited for; matrix products, arithmetic and copies ran while one was open for 0% of the time, Pallas kernels for 17%

profile of v2, /device:TPU:31, one launch (start us, length us, event | category | flops | bytes accessed | tf_op | source)
XLA Modules:
  0.0 74.0 jit_solution(3364953635982898931)
XLA Ops:
  0.6 2.2 %collective-permute-start.2 = (bf16[256,1024]{1,0:T(8,128)(2,1)}, bf16[256,1024]{1,0:T(8,128)(2,1)S(1)}, u32[]{:S(2)}, u32[]{:S(2)}) collective-permute-start(bf16[256,1024]{1,0:T(8,128)(2,1)} %refs_1_.1), channel_id=1, source_target_pairs={{0,2},{5,7},{10,8},{15,13},{16,18},{21,23},{26,24},{31,29}} | collective-permute-start | bytes 1572872 | tf_op jit(solution)/shard_map/ppermute | solution.py:533
  3.0 1.2 %copy-done.2 = bf16[512,1024]{1,0:T(8,128)(2,1)S(1)} copy-done((bf16[512,1024]{1,0:T(8,128)(2,1)S(1)}, bf16[512,1024]{1,0:T(8,128)(2,1)}, u32[]{:S(2)}) %copy-start.2) | copy-done | bytes 1048600
  4.2 0.7 copy-done.5
  5.0 1.4 %collective-permute-start.3 = (bf16[512,256]{1,0:T(8,128)(2,1)S(1)}, bf16[512,256]{1,0:T(8,128)(2,1)S(1)}, u32[]{:S(2)}, u32[]{:S(2)}) collective-permute-start(bf16[512,256]{1,0:T(8,128)(2,1)S(1)} %get-tuple-element.37), channel_id=1, source_target_pairs={{0,1},{1,2},{2,3},{4,5},{5,6},{6,7},{8,9},{9,10},{10,11},{12,13},{... | collective-permute-start | bytes 786440 | tf_op jit(solution)/shard_map/ppermute | solution.py:540
  6.4 2.3 %collective-permute-start.4 = (s32[1,256]{1,0:T(1,128)S(1)}, s32[1,256]{1,0:T(1,128)S(1)}, u32[]{:S(2)}, u32[]{:S(2)}) collective-permute-start(s32[1,256]{1,0:T(1,128)S(1)} %get-tuple-element.38.own_ref.own_label), channel_id=1, source_target_pairs={{0,8},{4,12},{8,0},{12,4},{1,9},{5,13},{9,1},{13,5},{2,10},{6,14},... | collective-permute-start | bytes 3080 | tf_op jit(solution)/shard_map/ppermute | solution.py:539
  8.8 18.8 %collective-permute-done.4.next_ref.next_label = s32[1,256]{1,0:T(1,128)S(1)} collective-permute-done((s32[1,256]{1,0:T(1,128)S(1)}, s32[1,256]{1,0:T(1,128)S(1)}, u32[]{:S(2)}, u32[]{:S(2)}) %collective-permute-start.4) | collective-permute-done | bytes 1056 | tf_op jit(solution)/shard_map/ppermute | solution.py:539
  28.9 3.1 %collective-permute-start.6 = (bf16[512,1024]{1,0:T(8,128)(2,1)S(1)}, bf16[512,1024]{1,0:T(8,128)(2,1)S(1)}, u32[]{:S(2)}, u32[]{:S(2)}) collective-permute-start(bf16[512,1024]{1,0:T(8,128)(2,1)S(1)} %stack.3), channel_id=1, source_target_pairs={{0,2},{5,7},{10,8},{15,13},{16,18},{21,23},{26,24},{31,29}} | collective-permute-start | bytes 3145736 | tf_op jit(solution)/shard_map/ppermute | solution.py:533
  32.2 1.5 %collective-permute-start.5 = (bf16[256,512]{1,0:T(8,128)(2,1)S(1)}, bf16[256,512]{1,0:T(8,128)(2,1)S(1)}, u32[]{:S(2)}, u32[]{:S(2)}) collective-permute-start(bf16[256,512]{1,0:T(8,128)(2,1)S(1)} %get-tuple-element.42), channel_id=1, source_target_pairs={{0,4},{4,0},{8,12},{12,8},{1,5},{5,1},{9,13},{13,9},{2,6},{6,2},{1... | collective-permute-start | bytes 786440 | tf_op jit(solution)/shard_map/ppermute | solution.py:546
  33.6 1.3 %collective-permute-start.7 = (bf16[512,256]{1,0:T(8,128)(2,1)S(1)}, bf16[512,256]{1,0:T(8,128)(2,1)S(1)}, u32[]{:S(2)}, u32[]{:S(2)}) collective-permute-start(bf16[512,256]{1,0:T(8,128)(2,1)S(1)} %get-tuple-element.47), channel_id=1, source_target_pairs={{1,0},{2,1},{3,2},{5,4},{6,5},{7,6},{9,8},{10,9},{11,10},{13,12},{... | collective-permute-start | bytes 786440 | tf_op jit(solution)/shard_map/ppermute | solution.py:552
  34.9 5.9 %collective-permute-done.8.outer_ref = bf16[272,512]{1,0:T(8,128)(2,1)S(1)} collective-permute-done((bf16[272,512]{1,0:T(8,128)(2,1)S(1)}, bf16[272,512]{1,0:T(8,128)(2,1)S(1)}, u32[]{:S(2)}, u32[]{:S(2)}) %collective-permute-start.8) | collective-permute-done | bytes 278560 | tf_op jit(solution)/shard_map/ppermute | solution.py:545
  40.9 0.7 edge_means.1
  41.5 1.3 %collective-permute-start.10 = (f32[256,256]{1,0:T(8,128)S(1)}, f32[256,256]{1,0:T(8,128)S(1)}, u32[]{:S(2)}, u32[]{:S(2)}) collective-permute-start(f32[256,256]{1,0:T(8,128)S(1)} %get-tuple-element.50), channel_id=1, source_target_pairs={{1,0},{2,1},{3,2},{5,4},{6,5},{7,6},{9,8},{10,9},{11,10},{13,12},{... | collective-permute-start | bytes 786440 | tf_op jit(solution)/shard_map/ppermute | solution.py:555
  42.8 1.3 %collective-permute-start.9 = (f32[256,256]{1,0:T(8,128)S(1)}, f32[256,256]{1,0:T(8,128)S(1)}, u32[]{:S(2)}, u32[]{:S(2)}) collective-permute-start(f32[256,256]{1,0:T(8,128)S(1)} %get-tuple-element.51), channel_id=1, source_target_pairs={{0,1},{1,2},{2,3},{4,5},{5,6},{6,7},{8,9},{9,10},{10,11},{12,13},{... | collective-permute-start | bytes 786440 | tf_op jit(solution)/shard_map/ppermute | solution.py:554
  44.1 1.0 %collective-permute-done.5.inner_ref = bf16[256,512]{1,0:T(8,128)(2,1)S(1)} collective-permute-done((bf16[256,512]{1,0:T(8,128)(2,1)S(1)}, bf16[256,512]{1,0:T(8,128)(2,1)S(1)}, u32[]{:S(2)}, u32[]{:S(2)}) %collective-permute-start.5) | collective-permute-done | bytes 262176 | tf_op jit(solution)/shard_map/ppermute | solution.py:546
  45.1 4.2 %collective-permute-done.6.refs_5_ = bf16[512,1024]{1,0:T(8,128)(2,1)S(1)} collective-permute-done((bf16[512,1024]{1,0:T(8,128)(2,1)S(1)}, bf16[512,1024]{1,0:T(8,128)(2,1)S(1)}, u32[]{:S(2)}, u32[]{:S(2)}) %collective-permute-start.6) | collective-permute-done | bytes 1048608 | tf_op jit(solution)/shard_map/ppermute | solution.py:533
  49.3 0.6 class_means.1
  50.0 3.9 %collective-permute-start.11 = (bf16[256,1024]{1,0:T(8,128)(2,1)S(1)}, bf16[256,1024]{1,0:T(8,128)(2,1)S(1)}, u32[]{:S(2)}, u32[]{:S(2)}) collective-permute-start(bf16[256,1024]{1,0:T(8,128)(2,1)S(1)} %get-tuple-element.56.refs_3_.refs_1_), channel_id=1, source_target_pairs={{0,2},{5,7},{10,8},{15,13},{16,18},{21,23},{26,24},{31,29}} | collective-permute-start | bytes 1572872 | tf_op jit(solution)/shard_map/ppermute | solution.py:533
  54.0 1.4 %collective-permute-start.12 = (bf16[768,1024]{1,0:T(8,128)(2,1)S(1)}, bf16[768,1024]{1,0:T(8,128)(2,1)S(1)}, u32[]{:S(2)}, u32[]{:S(2)}) collective-permute-start(bf16[768,1024]{1,0:T(8,128)(2,1)S(1)} %stack.4.near), channel_id=1, source_target_pairs={{0,1},{2,3},{5,4},{7,6},{10,11},{8,9},{15,14},{13,12},{16,17},{18,... | collective-permute-start | bytes 4718600 | tf_op jit(solution)/shard_map/ppermute | solution.py:533
  55.4 2.0 %centre.1 = (bf16[1536,1024]{1,0:T(8,128)(2,1)S(1)}, bf16[512,1024]{1,0:T(8,128)(2,1)S(1)}) custom-call(f32[4,256]{1,0:T(4,128)S(1)} %get-tuple-element.54.labels_ref, f32[256,1024]{1,0:T(8,128)S(1)} %get-tuple-element.59.means_ref, bf16[256,1024]{1,0:T(8,128)(2,1)S(1)} %copy-done, ...), custom_call_target="tpu_custom_call" | custom-call | flops 1 | tf_op jit(solution)/shard_map/centre/pallas_call | solution.py:443
  57.5 5.2 %whiten.1 = (bf16[512,1024]{1,0:T(8,128)(2,1)}, f32[1,512]{1,0:T(1,128)S(1)}) custom-call(bf16[512,1024]{1,0:T(8,128)(2,1)S(1)} %copy-done.3, bf16[512,256]{1,0:T(8,128)(2,1)S(1)} %collective-permute-done.3.left_ref, bf16[512,256]{1,0:T(8,128)(2,1)S(1)} %collective-permute-done.7.right_ref, f32[256,1024]{1,0:T(8,128)S(1)} %get-tuple-element.59.means_ref, ...), custom_call_target="tpu_custom_call" | custom-call | flops 99999997952 | tf_op jit(solution)/shard_map/whiten/pallas_call | solution.py:395
  62.7 2.1 %collective-permute-start.14 = (f32[1,512]{1,0:T(1,128)S(1)}, f32[1,512]{1,0:T(1,128)S(1)}, u32[]{:S(2)}, u32[]{:S(2)}) collective-permute-start(f32[1,512]{1,0:T(1,128)S(1)} %get-tuple-element.67.refs_5_), channel_id=1, source_target_pairs={{0,1},{1,0},{2,3},{3,2},{4,5},{5,4},{6,7},{7,6},{8,9},{9,8},{10,11... | collective-permute-start | bytes 6152 | tf_op jit(solution)/shard_map/ppermute | solution.py:571
  64.9 1.9 %collective-permute-start.13 = (bf16[256,1024]{1,0:T(8,128)(2,1)S(1)}, bf16[256,1024]{1,0:T(8,128)(2,1)S(1)}, u32[]{:S(2)}, u32[]{:S(2)}) collective-permute-start(bf16[256,1024]{1,0:T(8,128)(2,1)S(1)} %stack.5.refs_3_), channel_id=1, source_target_pairs={{0,1},{2,3},{5,4},{7,6},{10,11},{8,9},{15,14},{13,12},{16,17},{18,... | collective-permute-start | bytes 1572872 | tf_op jit(solution)/shard_map/ppermute | solution.py:533
  66.9 3.8 %gram_most.1.refs_1_ = f32[1024,1024]{1,0:T(8,128)S(1)} custom-call(s32[1]{0:T(128)} %bitcast.refs_0_.role_ref, bf16[1536,1024]{1,0:T(8,128)(2,1)S(1)} %get-tuple-element.62.left, bf16[768,1024]{1,0:T(8,128)(2,1)S(1)} %stack.4.near, bf16[768,1024]{1,0:T(8,128)(2,1)S(1)} %collective-permute-done.12.far), custom_call_target="tpu_custom_call" | custom-call | flops 99999997952 | tf_op jit(solution)/shard_map/gram_most/pallas_call | solution.py:467
  70.7 3.2 %gram_last.1 = (f32[1024,1024]{1,0:T(8,128)}, f32[1,512]{1,0:T(1,128)}) custom-call(s32[1]{0:T(128)} %bitcast.refs_0_.role_ref, f32[1024,1024]{1,0:T(8,128)S(1)} %gram_most.1.refs_1_, bf16[512,1024]{1,0:T(8,128)(2,1)S(1)} %get-tuple-element.65.refs_2_, bf16[256,1024]{1,0:T(8,128)(2,1)S(1)} %stack.5.refs_3_, ...), custom_call_target="tpu_custom_call" | custom-call | flops 99999997952 | tf_op jit(solution)/shard_map/gram_last/pallas_call | solution.py:502
  (34 shorter events, 1.9 us)
Async XLA Ops:
  0.6 27.0 %collective-permute-start.2 = (bf16[256,1024]{1,0:T(8,128)(2,1)}, bf16[256,1024]{1,0:T(8,128)(2,1)S(1)}, u32[]{:S(2)}, u32[]{:S(2)}) collective-permute-start(bf16[256,1024]{1,0:T(8,128)(2,1)} %refs_1_.1), channel_id=1, source_target_pairs={{0,2},{5,7},{10,8},{15,13},{16,18},{21,23},{26,24},{31,29}} | collective-permute-start | bytes 1572872 | tf_op jit(solution)/shard_map/ppermute | solution.py:533
  2.8 24.8 %collective-permute-start.1 = (bf16[256,1024]{1,0:T(8,128)(2,1)}, bf16[256,1024]{1,0:T(8,128)(2,1)S(1)}, u32[]{:S(2)}, u32[]{:S(2)}) collective-permute-start(bf16[256,1024]{1,0:T(8,128)(2,1)} %refs_1_.1), channel_id=1, source_target_pairs={{0,8},{4,12},{8,0},{12,4},{1,9},{5,13},{9,1},{13,5},{2,10},{6,14},... | collective-permute-start | bytes 1572872 | tf_op jit(solution)/shard_map/ppermute | solution.py:537
  2.9 25.3 %collective-permute-start = (bf16[256,1024]{1,0:T(8,128)(2,1)}, bf16[256,1024]{1,0:T(8,128)(2,1)S(1)}, u32[]{:S(2)}, u32[]{:S(2)}) collective-permute-start(bf16[256,1024]{1,0:T(8,128)(2,1)} %refs_1_.1), channel_id=1, source_target_pairs={{0,4},{4,0},{8,12},{12,8},{1,5},{5,1},{9,13},{13,9},{2,6},{6,2},{1... | collective-permute-start | bytes 1572872 | tf_op jit(solution)/shard_map/ppermute | solution.py:536
  3.0 1.2 %copy-start.2 = (bf16[512,1024]{1,0:T(8,128)(2,1)S(1)}, bf16[512,1024]{1,0:T(8,128)(2,1)}, u32[]{:S(2)}) copy-start(bf16[512,1024]{1,0:T(8,128)(2,1)} %held_ref.3) | copy-start | bytes 3145732
  4.2 0.7 copy-start.5
  4.9 23.3 %copy-start = (bf16[256,1024]{1,0:T(8,128)(2,1)S(1)}, bf16[256,1024]{1,0:T(8,128)(2,1)}, u32[]{:S(2)}) copy-start(bf16[256,1024]{1,0:T(8,128)(2,1)} %refs_1_.1) | copy-start | bytes 1572868
  5.0 22.6 %collective-permute-start.3 = (bf16[512,256]{1,0:T(8,128)(2,1)S(1)}, bf16[512,256]{1,0:T(8,128)(2,1)S(1)}, u32[]{:S(2)}, u32[]{:S(2)}) collective-permute-start(bf16[512,256]{1,0:T(8,128)(2,1)S(1)} %get-tuple-element.37), channel_id=1, source_target_pairs={{0,1},{1,2},{2,3},{4,5},{5,6},{6,7},{8,9},{9,10},{10,11},{12,13},{... | collective-permute-start | bytes 786440 | tf_op jit(solution)/shard_map/ppermute | solution.py:540
  6.4 21.2 %collective-permute-start.4 = (s32[1,256]{1,0:T(1,128)S(1)}, s32[1,256]{1,0:T(1,128)S(1)}, u32[]{:S(2)}, u32[]{:S(2)}) collective-permute-start(s32[1,256]{1,0:T(1,128)S(1)} %get-tuple-element.38.own_ref.own_label), channel_id=1, source_target_pairs={{0,8},{4,12},{8,0},{12,4},{1,9},{5,13},{9,1},{13,5},{2,10},{6,14},... | collective-permute-start | bytes 3080 | tf_op jit(solution)/shard_map/ppermute | solution.py:539
  28.9 20.5 %collective-permute-start.6 = (bf16[512,1024]{1,0:T(8,128)(2,1)S(1)}, bf16[512,1024]{1,0:T(8,128)(2,1)S(1)}, u32[]{:S(2)}, u32[]{:S(2)}) collective-permute-start(bf16[512,1024]{1,0:T(8,128)(2,1)S(1)} %stack.3), channel_id=1, source_target_pairs={{0,2},{5,7},{10,8},{15,13},{16,18},{21,23},{26,24},{31,29}} | collective-permute-start | bytes 3145736 | tf_op jit(solution)/shard_map/ppermute | solution.py:533
  32.1 8.8 %collective-permute-start.8 = (bf16[272,512]{1,0:T(8,128)(2,1)S(1)}, bf16[272,512]{1,0:T(8,128)(2,1)S(1)}, u32[]{:S(2)}, u32[]{:S(2)}) collective-permute-start(bf16[272,512]{1,0:T(8,128)(2,1)S(1)} %get-tuple-element.49), channel_id=1, source_target_pairs={{0,4},{4,0},{8,12},{12,8},{1,5},{5,1},{9,13},{13,9},{2,6},{6,2},{1... | collective-permute-start | bytes 835592 | tf_op jit(solution)/shard_map/ppermute | solution.py:545
  32.2 12.9 %collective-permute-start.5 = (bf16[256,512]{1,0:T(8,128)(2,1)S(1)}, bf16[256,512]{1,0:T(8,128)(2,1)S(1)}, u32[]{:S(2)}, u32[]{:S(2)}) collective-permute-start(bf16[256,512]{1,0:T(8,128)(2,1)S(1)} %get-tuple-element.42), channel_id=1, source_target_pairs={{0,4},{4,0},{8,12},{12,8},{1,5},{5,1},{9,13},{13,9},{2,6},{6,2},{1... | collective-permute-start | bytes 786440 | tf_op jit(solution)/shard_map/ppermute | solution.py:546
  33.6 11.5 %collective-permute-start.7 = (bf16[512,256]{1,0:T(8,128)(2,1)S(1)}, bf16[512,256]{1,0:T(8,128)(2,1)S(1)}, u32[]{:S(2)}, u32[]{:S(2)}) collective-permute-start(bf16[512,256]{1,0:T(8,128)(2,1)S(1)} %get-tuple-element.47), channel_id=1, source_target_pairs={{1,0},{2,1},{3,2},{5,4},{6,5},{7,6},{9,8},{10,9},{11,10},{13,12},{... | collective-permute-start | bytes 786440 | tf_op jit(solution)/shard_map/ppermute | solution.py:552
  41.5 15.9 %collective-permute-start.10 = (f32[256,256]{1,0:T(8,128)S(1)}, f32[256,256]{1,0:T(8,128)S(1)}, u32[]{:S(2)}, u32[]{:S(2)}) collective-permute-start(f32[256,256]{1,0:T(8,128)S(1)} %get-tuple-element.50), channel_id=1, source_target_pairs={{1,0},{2,1},{3,2},{5,4},{6,5},{7,6},{9,8},{10,9},{11,10},{13,12},{... | collective-permute-start | bytes 786440 | tf_op jit(solution)/shard_map/ppermute | solution.py:555
  42.8 14.6 %collective-permute-start.9 = (f32[256,256]{1,0:T(8,128)S(1)}, f32[256,256]{1,0:T(8,128)S(1)}, u32[]{:S(2)}, u32[]{:S(2)}) collective-permute-start(f32[256,256]{1,0:T(8,128)S(1)} %get-tuple-element.51), channel_id=1, source_target_pairs={{0,1},{1,2},{2,3},{4,5},{5,6},{6,7},{8,9},{9,10},{10,11},{12,13},{... | collective-permute-start | bytes 786440 | tf_op jit(solution)/shard_map/ppermute | solution.py:554
  49.9 7.5 %copy-start.1 = (bf16[3,1024,256]{2,1,0:T(8,128)(2,1)S(1)}, bf16[3,1024,256]{2,1,0:T(8,128)(2,1)}, u32[]{:S(2)}) copy-start(bf16[3,1024,256]{2,1,0:T(8,128)(2,1)} %precision.1) | copy-start | bytes 4718596
  49.9 7.5 %copy-start.3 = (bf16[512,1024]{1,0:T(8,128)(2,1)S(1)}, bf16[512,1024]{1,0:T(8,128)(2,1)}, u32[]{:S(2)}) copy-start(bf16[512,1024]{1,0:T(8,128)(2,1)} %held_ref.3) | copy-start | bytes 3145732
  50.0 7.5 %copy-start.4 = (s32[512]{0:T(512)S(1)}, s32[512]{0:T(512)}, u32[]{:S(2)}) copy-start(s32[512]{0:T(512)} %param.8) | copy-start | bytes 6148
  50.0 12.7 %collective-permute-start.11 = (bf16[256,1024]{1,0:T(8,128)(2,1)S(1)}, bf16[256,1024]{1,0:T(8,128)(2,1)S(1)}, u32[]{:S(2)}, u32[]{:S(2)}) collective-permute-start(bf16[256,1024]{1,0:T(8,128)(2,1)S(1)} %get-tuple-element.56.refs_3_.refs_1_), channel_id=1, source_target_pairs={{0,2},{5,7},{10,8},{15,13},{16,18},{21,23},{26,24},{31,29}} | collective-permute-start | bytes 1572872 | tf_op jit(solution)/shard_map/ppermute | solution.py:533
  54.0 12.8 %collective-permute-start.12 = (bf16[768,1024]{1,0:T(8,128)(2,1)S(1)}, bf16[768,1024]{1,0:T(8,128)(2,1)S(1)}, u32[]{:S(2)}, u32[]{:S(2)}) collective-permute-start(bf16[768,1024]{1,0:T(8,128)(2,1)S(1)} %stack.4.near), channel_id=1, source_target_pairs={{0,1},{2,3},{5,4},{7,6},{10,11},{8,9},{15,14},{13,12},{16,17},{18,... | collective-permute-start | bytes 4718600 | tf_op jit(solution)/shard_map/ppermute | solution.py:533
  62.7 8.0 %collective-permute-start.16 = (f32[1,512]{1,0:T(1,128)S(1)}, f32[1,512]{1,0:T(1,128)S(1)}, u32[]{:S(2)}, u32[]{:S(2)}) collective-permute-start(f32[1,512]{1,0:T(1,128)S(1)} %get-tuple-element.67.refs_5_), channel_id=1, source_target_pairs={{0,3},{1,2},{2,1},{3,0},{4,7},{5,6},{6,5},{7,4},{8,11},{9,10},{10,... | collective-permute-start | bytes 6152 | tf_op jit(solution)/shard_map/ppermute | solution.py:571
  62.7 8.0 %collective-permute-start.15 = (f32[1,512]{1,0:T(1,128)S(1)}, f32[1,512]{1,0:T(1,128)S(1)}, u32[]{:S(2)}, u32[]{:S(2)}) collective-permute-start(f32[1,512]{1,0:T(1,128)S(1)} %get-tuple-element.67.refs_5_), channel_id=1, source_target_pairs={{0,2},{1,3},{2,0},{3,1},{4,6},{5,7},{6,4},{7,5},{8,10},{9,11},{10,... | collective-permute-start | bytes 6152 | tf_op jit(solution)/shard_map/ppermute | solution.py:571
  62.7 8.0 %collective-permute-start.14 = (f32[1,512]{1,0:T(1,128)S(1)}, f32[1,512]{1,0:T(1,128)S(1)}, u32[]{:S(2)}, u32[]{:S(2)}) collective-permute-start(f32[1,512]{1,0:T(1,128)S(1)} %get-tuple-element.67.refs_5_), channel_id=1, source_target_pairs={{0,1},{1,0},{2,3},{3,2},{4,5},{5,4},{6,7},{7,6},{8,9},{9,8},{10,11... | collective-permute-start | bytes 6152 | tf_op jit(solution)/shard_map/ppermute | solution.py:571
  64.9 5.8 %collective-permute-start.13 = (bf16[256,1024]{1,0:T(8,128)(2,1)S(1)}, bf16[256,1024]{1,0:T(8,128)(2,1)S(1)}, u32[]{:S(2)}, u32[]{:S(2)}) collective-permute-start(bf16[256,1024]{1,0:T(8,128)(2,1)S(1)} %stack.5.refs_3_), channel_id=1, source_target_pairs={{0,1},{2,3},{5,4},{7,6},{10,11},{8,9},{15,14},{13,12},{16,17},{18,... | collective-permute-start | bytes 1572872 | tf_op jit(solution)/shard_map/ppermute | solution.py:533

commit v3 on v2

--- a/solution.py
+++ b/solution.py
@@ -9,6 +9,7 @@
 BLK = 256
 LONG = 10**11
 EXTRA = 16
+TILE = 128
 F32 = jnp.float32
 BF16 = jnp.bfloat16
 VMEM = pl.BlockSpec(memory_space=pltpu.VMEM)
@@ -376,7 +377,7 @@
     picked = sum(contract_rows(onehot, piece) for piece in split3(means))
     held = jnp.concatenate([left_ref[...], held_ref[...], right_ref[...]], axis=1)
     centred = held.astype(F32) - picked
-    pieces = split3(centred)
+    pieces = split3(centred)[:2]
     score = jnp.zeros((held_ref.shape[0], 128), F32)
     for m in range(width // BLK):
         inside = slice(m * BLK, (m + 1) * BLK)
@@ -484,13 +485,13 @@
     distance_ref[...] = ((own[...] + beside) + (across + beyond)) / features
     arrival.wait()
     stores = []
-    for k, t in enumerate(range(0, width, BLK)):
-        part = contract_rows(last_ref[:count, t : t + BLK], right[...])
-        part = part + contract_rows(last_ref[count:, t : t + BLK], right[...])
-        tiles[t : t + BLK, :] = (total_ref[t : t + BLK, :] + part) * scale
+    for k, t in enumerate(range(0, width, TILE)):
+        part = contract_rows(last_ref[:count, t : t + TILE], right[...])
+        part = part + contract_rows(last_ref[count:, t : t + TILE], right[...])
+        tiles[t : t + TILE, :] = (total_ref[t : t + TILE, :] + part) * scale
         stores.append(
             pltpu.make_async_copy(
-                tiles.at[pl.ds(t, BLK)], out_ref.at[pl.ds(t, BLK)], out_sem.at[k]
+                tiles.at[pl.ds(t, TILE)], out_ref.at[pl.ds(t, TILE)], out_sem.at[k]
             )
         )
         stores[-1].start()
@@ -511,7 +512,7 @@
             pltpu.VMEM((count, width), BF16),
             pltpu.VMEM((width, width), F32),
             pltpu.SemaphoreType.DMA((1,)),
-            pltpu.SemaphoreType.DMA((width // BLK,)),
+            pltpu.SemaphoreType.DMA((width // TILE,)),
         ],
         compiler_params=MEDIUM,
         cost_estimate=cost(LONG),
@@ -536,24 +537,25 @@
     third = lax.ppermute(train_rows, "dp", flip[1])
     second = lax.ppermute(train_rows, "dp", flip[2])
     own_labels, head, tail = outgoing(train_labels.reshape(1, count), held_rows)
+    left = lax.ppermute(tail, "feat", to_right)
+    right = lax.ppermute(head, "feat", to_left)
+    left, own_labels = tie((left, own_labels))
     next_labels = lax.ppermute(own_labels, "dp", flip[2])
-    left = lax.ppermute(tail, "feat", to_right)
-    third, second, across_own, left, next_labels = tie(
-        (third, second, across_own, left, next_labels)
+    third, second, across_own, left, right, next_labels = tie(
+        (third, second, across_own, left, right, next_labels)
     )
     second_outer, second_inner = halves(own_labels, next_labels, second)
     outer = lax.ppermute(second_outer, "dp", flip[1])
     inner = lax.ppermute(second_inner, "dp", flip[1])
     early = early_sums(own_labels, next_labels, train_rows, second)
-    early, head, *sent = tie((early, head, second, third))
+    early, *sent = tie((early, second, third))
     role = role.reshape(1)
     own_most = stack(role, sent, sent)
     across_most = hop(own_most, (0, 2))
-    right = lax.ppermute(head, "feat", to_left)
     head, tail = edge_means(own_labels, next_labels, early, third, outer)
     left_means = lax.ppermute(tail, "feat", to_right)
     right_means = lax.ppermute(head, "feat", to_left)
-    inner, across_most, right, head, tail = tie((inner, across_most, right, head, tail))
+    inner, head, tail = tie((inner, head, tail))
     means, fourth, labels = class_means(own_labels, next_labels, early, third, outer, inner)
     across_last = hop(fourth, (0, 2))
     rows = [train_rows, second, third, fourth]
@@ -564,11 +566,13 @@
     white, score = whiten(
         held_rows, left, right, means, left_means, right_means, held_labels.reshape(1, -1), precision
     )
-    score, across_last, most = tie((score, across_last, most))
+    score, most = tie((score, most))
     total = gram_most(role, most, near_most, far_most)
+    beside = lax.ppermute(score, "feat", flip[1])
+    beside, across_last = tie((beside, across_last))
     near_last = stack(role, [fourth], [across_last])
     far_last = hop(near_last, (0, 1), (2, 3))
-    scores = [score] + [lax.ppermute(score, "feat", flip[k]) for k in (1, 2, 3)]
+    scores = [score, beside] + [lax.ppermute(score, "feat", flip[k]) for k in (2, 3)]
     cov, distance = gram_last(
         role, total, last, near_last, far_last, scores, 1.0 / (n * count - C), float(n * width)
     )

time: 74.4 us -> 68.7 us (0.923)
  the two profiles are of different devices: /device:TPU:31 before, /device:TPU:0 now
where the time goes in v3:
time: 68.7 us; the launch traced here: 68.3 us
  starting transfers between devices  30.4 us (44%)
  waiting for transfers between devices  19.1 us (28%)
  Pallas kernels  15.3 us (22%)
  local copies, waits for them, and re-layouts  2.62 us (4%)
  between operations  0.94 us (1%)
    ppermute x5, starting transfers between devices, hop(): return lax.ppermute(array, ('dp', 'feat'), pairs)  14.9 us
    ppermute x1, waiting for transfers between devices, four_by_four(): next_labels = lax.ppermute(own_labels, 'dp', flip[2])  13 us
    pallas_call x1, Pallas kernels, whiten(): pl.pallas_call(white_kernel, out_shape=(jax.ShapeDtypeStruct((count, widt...  4.21 us
    pallas_call x1, Pallas kernels, gram_most(): pl.pallas_call(most_kernel, out_shape=jax.ShapeDtypeStruct((width, width)...  3.62 us
    ppermute x1, waiting for transfers between devices, four_by_four(): outer = lax.ppermute(second_outer, 'dp', flip[1])  3.35 us
    pallas_call x1, Pallas kernels, gram_last(): pl.pallas_call(lambda *refs: last_kernel(scale, features, *refs), out_sha...  3.09 us
    ppermute x1, starting transfers between devices, four_by_four(): third = lax.ppermute(train_rows, 'dp', flip[1])  3.09 us
    unnamed x16, local copies, waits for them, and re-layouts  2.62 us
  transfers between devices with their start and end apart: 17, of which 4 were waited for; matrix products, arithmetic and copies ran while one was open for 0% of the time, Pallas kernels for 18%

profile of v3, /device:TPU:0, one launch (start us, length us, event | category | flops | bytes accessed | tf_op | source)
XLA Modules:
  0.0 68.3 jit_solution(3603618817712036164)
XLA Ops:
  0.6 3.1 %collective-permute-start = (bf16[256,1024]{1,0:T(8,128)(2,1)}, bf16[256,1024]{1,0:T(8,128)(2,1)S(1)}, u32[]{:S(2)}, u32[]{:S(2)}) collective-permute-start(bf16[256,1024]{1,0:T(8,128)(2,1)} %refs_1_.1), channel_id=1, source_target_pairs={{0,4},{4,0},{8,12},{12,8},{1,5},{5,1},{9,13},{13,9},{2,6},{6,2},{1... | collective-permute-start | bytes 1572872 | tf_op jit(solution)/shard_map/ppermute | solution.py:537
  3.7 2.6 %collective-permute-start.1 = (bf16[256,1024]{1,0:T(8,128)(2,1)}, bf16[256,1024]{1,0:T(8,128)(2,1)S(1)}, u32[]{:S(2)}, u32[]{:S(2)}) collective-permute-start(bf16[256,1024]{1,0:T(8,128)(2,1)} %refs_1_.1), channel_id=1, source_target_pairs={{0,8},{4,12},{8,0},{12,4},{1,9},{5,13},{9,1},{13,5},{2,10},{6,14},... | collective-permute-start | bytes 1572872 | tf_op jit(solution)/shard_map/ppermute | solution.py:538
  6.3 3.4 %collective-permute-start.2 = (bf16[256,1024]{1,0:T(8,128)(2,1)}, bf16[256,1024]{1,0:T(8,128)(2,1)S(1)}, u32[]{:S(2)}, u32[]{:S(2)}) collective-permute-start(bf16[256,1024]{1,0:T(8,128)(2,1)} %refs_1_.1), channel_id=1, source_target_pairs={{0,2},{5,7},{10,8},{15,13},{16,18},{21,23},{26,24},{31,29}} | collective-permute-start | bytes 1572872 | tf_op jit(solution)/shard_map/ppermute | solution.py:534
  9.7 1.2 %copy-done.2 = bf16[512,1024]{1,0:T(8,128)(2,1)S(1)} copy-done((bf16[512,1024]{1,0:T(8,128)(2,1)S(1)}, bf16[512,1024]{1,0:T(8,128)(2,1)}, u32[]{:S(2)}) %copy-start.2) | copy-done | bytes 1048600
  11.0 0.7 copy-done.7
  11.8 1.4 %collective-permute-start.3 = (bf16[512,256]{1,0:T(8,128)(2,1)S(1)}, bf16[512,256]{1,0:T(8,128)(2,1)S(1)}, u32[]{:S(2)}, u32[]{:S(2)}) collective-permute-start(bf16[512,256]{1,0:T(8,128)(2,1)S(1)} %get-tuple-element.38), channel_id=1, source_target_pairs={{0,1},{1,2},{2,3},{4,5},{5,6},{6,7},{8,9},{9,10},{10,11},{12,13},{... | collective-permute-start | bytes 786440 | tf_op jit(solution)/shard_map/ppermute | solution.py:540
  13.2 1.3 %collective-permute-start.4 = (bf16[512,256]{1,0:T(8,128)(2,1)S(1)}, bf16[512,256]{1,0:T(8,128)(2,1)S(1)}, u32[]{:S(2)}, u32[]{:S(2)}) collective-permute-start(bf16[512,256]{1,0:T(8,128)(2,1)S(1)} %get-tuple-element.41), channel_id=1, source_target_pairs={{1,0},{2,1},{3,2},{5,4},{6,5},{7,6},{9,8},{10,9},{11,10},{13,12},{... | collective-permute-start | bytes 786440 | tf_op jit(solution)/shard_map/ppermute | solution.py:541
  14.5 0.7 %copy-done.4 = bf16[512,256]{1,0:T(8,128)(2,1)} copy-done((bf16[512,256]{1,0:T(8,128)(2,1)}, bf16[512,256]{1,0:T(8,128)(2,1)S(1)}, u32[]{:S(2)}) %copy-start.4) | copy-done | bytes 262168
  15.2 1.4 %collective-permute-done.4.right_ref = bf16[512,256]{1,0:T(8,128)(2,1)S(1)} collective-permute-done((bf16[512,256]{1,0:T(8,128)(2,1)S(1)}, bf16[512,256]{1,0:T(8,128)(2,1)S(1)}, u32[]{:S(2)}, u32[]{:S(2)}) %collective-permute-start.4) | collective-permute-done | bytes 262176 | tf_op jit(solution)/shard_map/ppermute | solution.py:541
  16.6 13.0 %collective-permute-done.5.next_label.next_ref = s32[1,256]{1,0:T(1,128)S(1)} collective-permute-done((s32[1,256]{1,0:T(1,128)S(1)}, s32[1,256]{1,0:T(1,128)S(1)}, u32[]{:S(2)}, u32[]{:S(2)}) %collective-permute-start.5) | collective-permute-done | bytes 1056 | tf_op jit(solution)/shard_map/ppermute | solution.py:543
  30.2 1.6 %collective-permute-start.7 = (bf16[256,512]{1,0:T(8,128)(2,1)S(1)}, bf16[256,512]{1,0:T(8,128)(2,1)S(1)}, u32[]{:S(2)}, u32[]{:S(2)}) collective-permute-start(bf16[256,512]{1,0:T(8,128)(2,1)S(1)} %get-tuple-element.50), channel_id=1, source_target_pairs={{0,4},{4,0},{8,12},{12,8},{1,5},{5,1},{9,13},{13,9},{2,6},{6,2},{1... | collective-permute-start | bytes 786440 | tf_op jit(solution)/shard_map/ppermute | solution.py:549
  32.5 3.5 %collective-permute-start.10 = (bf16[512,1024]{1,0:T(8,128)(2,1)S(1)}, bf16[512,1024]{1,0:T(8,128)(2,1)S(1)}, u32[]{:S(2)}, u32[]{:S(2)}) collective-permute-start(bf16[512,1024]{1,0:T(8,128)(2,1)S(1)} %stack.3), channel_id=1, source_target_pairs={{0,2},{5,7},{10,8},{15,13},{16,18},{21,23},{26,24},{31,29}} | collective-permute-start | bytes 3145736 | tf_op jit(solution)/shard_map/ppermute | solution.py:534
  36.0 3.3 %collective-permute-done.6.outer_ref = bf16[272,512]{1,0:T(8,128)(2,1)S(1)} collective-permute-done((bf16[272,512]{1,0:T(8,128)(2,1)S(1)}, bf16[272,512]{1,0:T(8,128)(2,1)S(1)}, u32[]{:S(2)}, u32[]{:S(2)}) %collective-permute-start.6) | collective-permute-done | bytes 278560 | tf_op jit(solution)/shard_map/ppermute | solution.py:548
  40.0 1.3 %collective-permute-start.8 = (f32[256,256]{1,0:T(8,128)S(1)}, f32[256,256]{1,0:T(8,128)S(1)}, u32[]{:S(2)}, u32[]{:S(2)}) collective-permute-start(f32[256,256]{1,0:T(8,128)S(1)} %get-tuple-element.52), channel_id=1, source_target_pairs={{0,1},{1,2},{2,3},{4,5},{5,6},{6,7},{8,9},{9,10},{10,11},{12,13},{... | collective-permute-start | bytes 786440 | tf_op jit(solution)/shard_map/ppermute | solution.py:556
  41.3 1.3 %collective-permute-start.9 = (f32[256,256]{1,0:T(8,128)S(1)}, f32[256,256]{1,0:T(8,128)S(1)}, u32[]{:S(2)}, u32[]{:S(2)}) collective-permute-start(f32[256,256]{1,0:T(8,128)S(1)} %get-tuple-element.51), channel_id=1, source_target_pairs={{1,0},{2,1},{3,2},{5,4},{6,5},{7,6},{9,8},{10,9},{11,10},{13,12},{... | collective-permute-start | bytes 786440 | tf_op jit(solution)/shard_map/ppermute | solution.py:557
  42.6 1.4 %collective-permute-done.7.inner_ref = bf16[256,512]{1,0:T(8,128)(2,1)S(1)} collective-permute-done((bf16[256,512]{1,0:T(8,128)(2,1)S(1)}, bf16[256,512]{1,0:T(8,128)(2,1)S(1)}, u32[]{:S(2)}, u32[]{:S(2)}) %collective-permute-start.7) | collective-permute-done | bytes 262176 | tf_op jit(solution)/shard_map/ppermute | solution.py:549
  44.6 4.4 %collective-permute-start.13 = (bf16[256,1024]{1,0:T(8,128)(2,1)S(1)}, bf16[256,1024]{1,0:T(8,128)(2,1)S(1)}, u32[]{:S(2)}, u32[]{:S(2)}) collective-permute-start(bf16[256,1024]{1,0:T(8,128)(2,1)S(1)} %get-tuple-element.56.refs_3_.refs_1_), channel_id=1, source_target_pairs={{0,2},{5,7},{10,8},{15,13},{16,18},{21,23},{26,24},{31,29}} | collective-permute-start | bytes 1572872 | tf_op jit(solution)/shard_map/ppermute | solution.py:534
  49.0 2.0 %centre.1 = (bf16[1536,1024]{1,0:T(8,128)(2,1)S(1)}, bf16[512,1024]{1,0:T(8,128)(2,1)S(1)}) custom-call(f32[4,256]{1,0:T(4,128)S(1)} %get-tuple-element.54.labels_ref, f32[256,1024]{1,0:T(8,128)S(1)} %get-tuple-element.59.means_ref, bf16[256,1024]{1,0:T(8,128)(2,1)S(1)} %copy-done, ...), custom_call_target="tpu_custom_call" | custom-call | flops 1 | tf_op jit(solution)/shard_map/centre/pallas_call | solution.py:444
  51.3 1.5 %collective-permute-start.11 = (bf16[768,1024]{1,0:T(8,128)(2,1)S(1)}, bf16[768,1024]{1,0:T(8,128)(2,1)S(1)}, u32[]{:S(2)}, u32[]{:S(2)}) collective-permute-start(bf16[768,1024]{1,0:T(8,128)(2,1)S(1)} %stack.4.near), channel_id=1, source_target_pairs={{0,1},{2,3},{5,4},{7,6},{10,11},{8,9},{15,14},{13,12},{16,17},{18,... | collective-permute-start | bytes 4718600 | tf_op jit(solution)/shard_map/ppermute | solution.py:534
  52.8 4.2 %whiten.1 = (bf16[512,1024]{1,0:T(8,128)(2,1)}, f32[1,512]{1,0:T(1,128)S(1)}) custom-call(bf16[512,1024]{1,0:T(8,128)(2,1)S(1)} %copy-done.3, bf16[512,256]{1,0:T(8,128)(2,1)S(1)} %copy-done.5, bf16[512,256]{1,0:T(8,128)(2,1)S(1)} %collective-permute-done.4.right_ref, f32[256,1024]{1,0:T(8,128)S(1)} %get-tuple-element.59.means_ref, ...), custom_call_target="tpu_custom_call" | custom-call | flops 99999997952 | tf_op jit(solution)/shard_map/whiten/pallas_call | solution.py:396
  57.1 2.3 %collective-permute-start.15 = (f32[1,512]{1,0:T(1,128)S(1)}, f32[1,512]{1,0:T(1,128)S(1)}, u32[]{:S(2)}, u32[]{:S(2)}) collective-permute-start(f32[1,512]{1,0:T(1,128)S(1)} %get-tuple-element.67.refs_5_), channel_id=1, source_target_pairs={{0,2},{1,3},{2,0},{3,1},{4,6},{5,7},{6,4},{7,5},{8,10},{9,11},{10,... | collective-permute-start | bytes 6152 | tf_op jit(solution)/shard_map/ppermute | solution.py:575
  59.5 2.0 %collective-permute-start.14 = (bf16[256,1024]{1,0:T(8,128)(2,1)S(1)}, bf16[256,1024]{1,0:T(8,128)(2,1)S(1)}, u32[]{:S(2)}, u32[]{:S(2)}) collective-permute-start(bf16[256,1024]{1,0:T(8,128)(2,1)S(1)} %stack.5.refs_3_), channel_id=1, source_target_pairs={{0,1},{2,3},{5,4},{7,6},{10,11},{8,9},{15,14},{13,12},{16,17},{18,... | collective-permute-start | bytes 1572872 | tf_op jit(solution)/shard_map/ppermute | solution.py:534
  61.6 3.6 %gram_most.1.refs_1_ = f32[1024,1024]{1,0:T(8,128)S(1)} custom-call(s32[1]{0:T(128)} %bitcast.refs_0_.role_ref, bf16[1536,1024]{1,0:T(8,128)(2,1)S(1)} %get-tuple-element.62.left, bf16[768,1024]{1,0:T(8,128)(2,1)S(1)} %stack.4.near, bf16[768,1024]{1,0:T(8,128)(2,1)S(1)} %collective-permute-done.11.far), custom_call_target="tpu_custom_call" | custom-call | flops 99999997952 | tf_op jit(solution)/shard_map/gram_most/pallas_call | solution.py:468
  65.2 3.1 %gram_last.1 = (f32[1024,1024]{1,0:T(8,128)}, f32[1,512]{1,0:T(1,128)}) custom-call(s32[1]{0:T(128)} %bitcast.refs_0_.role_ref, f32[1024,1024]{1,0:T(8,128)S(1)} %gram_most.1.refs_1_, bf16[512,1024]{1,0:T(8,128)(2,1)S(1)} %get-tuple-element.66.refs_2_, bf16[256,1024]{1,0:T(8,128)(2,1)S(1)} %stack.5.refs_3_, ...), custom_call_target="tpu_custom_call" | custom-call | flops 99999997952 | tf_op jit(solution)/shard_map/gram_last/pallas_call | solution.py:503
  (38 shorter events, 3.1 us)
Async XLA Ops:
  0.6 29.0 %collective-permute-start = (bf16[256,1024]{1,0:T(8,128)(2,1)}, bf16[256,1024]{1,0:T(8,128)(2,1)S(1)}, u32[]{:S(2)}, u32[]{:S(2)}) collective-permute-start(bf16[256,1024]{1,0:T(8,128)(2,1)} %refs_1_.1), channel_id=1, source_target_pairs={{0,4},{4,0},{8,12},{12,8},{1,5},{5,1},{9,13},{13,9},{2,6},{6,2},{1... | collective-permute-start | bytes 1572872 | tf_op jit(solution)/shard_map/ppermute | solution.py:537
  3.7 25.9 %collective-permute-start.1 = (bf16[256,1024]{1,0:T(8,128)(2,1)}, bf16[256,1024]{1,0:T(8,128)(2,1)S(1)}, u32[]{:S(2)}, u32[]{:S(2)}) collective-permute-start(bf16[256,1024]{1,0:T(8,128)(2,1)} %refs_1_.1), channel_id=1, source_target_pairs={{0,8},{4,12},{8,0},{12,4},{1,9},{5,13},{9,1},{13,5},{2,10},{6,14},... | collective-permute-start | bytes 1572872 | tf_op jit(solution)/shard_map/ppermute | solution.py:538
  6.3 23.3 %collective-permute-start.2 = (bf16[256,1024]{1,0:T(8,128)(2,1)}, bf16[256,1024]{1,0:T(8,128)(2,1)S(1)}, u32[]{:S(2)}, u32[]{:S(2)}) collective-permute-start(bf16[256,1024]{1,0:T(8,128)(2,1)} %refs_1_.1), channel_id=1, source_target_pairs={{0,2},{5,7},{10,8},{15,13},{16,18},{21,23},{26,24},{31,29}} | collective-permute-start | bytes 1572872 | tf_op jit(solution)/shard_map/ppermute | solution.py:534
  9.7 1.2 %copy-start.2 = (bf16[512,1024]{1,0:T(8,128)(2,1)S(1)}, bf16[512,1024]{1,0:T(8,128)(2,1)}, u32[]{:S(2)}) copy-start(bf16[512,1024]{1,0:T(8,128)(2,1)} %held_ref.3) | copy-start | bytes 3145732
  11.6 20.2 %copy-start = (bf16[256,1024]{1,0:T(8,128)(2,1)S(1)}, bf16[256,1024]{1,0:T(8,128)(2,1)}, u32[]{:S(2)}) copy-start(bf16[256,1024]{1,0:T(8,128)(2,1)} %refs_1_.1) | copy-start | bytes 1572868
  11.8 2.7 %collective-permute-start.3 = (bf16[512,256]{1,0:T(8,128)(2,1)S(1)}, bf16[512,256]{1,0:T(8,128)(2,1)S(1)}, u32[]{:S(2)}, u32[]{:S(2)}) collective-permute-start(bf16[512,256]{1,0:T(8,128)(2,1)S(1)} %get-tuple-element.38), channel_id=1, source_target_pairs={{0,1},{1,2},{2,3},{4,5},{5,6},{6,7},{8,9},{9,10},{10,11},{12,13},{... | collective-permute-start | bytes 786440 | tf_op jit(solution)/shard_map/ppermute | solution.py:540
  13.2 3.4 %collective-permute-start.4 = (bf16[512,256]{1,0:T(8,128)(2,1)S(1)}, bf16[512,256]{1,0:T(8,128)(2,1)S(1)}, u32[]{:S(2)}, u32[]{:S(2)}) collective-permute-start(bf16[512,256]{1,0:T(8,128)(2,1)S(1)} %get-tuple-element.41), channel_id=1, source_target_pairs={{1,0},{2,1},{3,2},{5,4},{6,5},{7,6},{9,8},{10,9},{11,10},{13,12},{... | collective-permute-start | bytes 786440 | tf_op jit(solution)/shard_map/ppermute | solution.py:541
  14.5 0.7 %copy-start.4 = (bf16[512,256]{1,0:T(8,128)(2,1)}, bf16[512,256]{1,0:T(8,128)(2,1)S(1)}, u32[]{:S(2)}) copy-start(bf16[512,256]{1,0:T(8,128)(2,1)S(1)} %collective-permute-done.3.left_ref) | copy-start | bytes 786436
  15.2 14.4 %collective-permute-start.5 = (s32[1,256]{1,0:T(1,128)S(1)}, s32[1,256]{1,0:T(1,128)S(1)}, u32[]{:S(2)}, u32[]{:S(2)}) collective-permute-start(s32[1,256]{1,0:T(1,128)S(1)} %get-tuple-element.42.own_label.own_ref), channel_id=1, source_target_pairs={{0,8},{4,12},{8,0},{12,4},{1,9},{5,13},{9,1},{13,5},{2,10},{6,14},... | collective-permute-start | bytes 3080 | tf_op jit(solution)/shard_map/ppermute | solution.py:543
  29.7 9.6 %collective-permute-start.6 = (bf16[272,512]{1,0:T(8,128)(2,1)S(1)}, bf16[272,512]{1,0:T(8,128)(2,1)S(1)}, u32[]{:S(2)}, u32[]{:S(2)}) collective-permute-start(bf16[272,512]{1,0:T(8,128)(2,1)S(1)} %get-tuple-element.49), channel_id=1, source_target_pairs={{0,4},{4,0},{8,12},{12,8},{1,5},{5,1},{9,13},{13,9},{2,6},{6,2},{1... | collective-permute-start | bytes 835592 | tf_op jit(solution)/shard_map/ppermute | solution.py:548
  30.2 13.8 %collective-permute-start.7 = (bf16[256,512]{1,0:T(8,128)(2,1)S(1)}, bf16[256,512]{1,0:T(8,128)(2,1)S(1)}, u32[]{:S(2)}, u32[]{:S(2)}) collective-permute-start(bf16[256,512]{1,0:T(8,128)(2,1)S(1)} %get-tuple-element.50), channel_id=1, source_target_pairs={{0,4},{4,0},{8,12},{12,8},{1,5},{5,1},{9,13},{13,9},{2,6},{6,2},{1... | collective-permute-start | bytes 786440 | tf_op jit(solution)/shard_map/ppermute | solution.py:549
  32.5 18.6 %collective-permute-start.10 = (bf16[512,1024]{1,0:T(8,128)(2,1)S(1)}, bf16[512,1024]{1,0:T(8,128)(2,1)S(1)}, u32[]{:S(2)}, u32[]{:S(2)}) collective-permute-start(bf16[512,1024]{1,0:T(8,128)(2,1)S(1)} %stack.3), channel_id=1, source_target_pairs={{0,2},{5,7},{10,8},{15,13},{16,18},{21,23},{26,24},{31,29}} | collective-permute-start | bytes 3145736 | tf_op jit(solution)/shard_map/ppermute | solution.py:534
  40.0 12.8 %collective-permute-start.8 = (f32[256,256]{1,0:T(8,128)S(1)}, f32[256,256]{1,0:T(8,128)S(1)}, u32[]{:S(2)}, u32[]{:S(2)}) collective-permute-start(f32[256,256]{1,0:T(8,128)S(1)} %get-tuple-element.52), channel_id=1, source_target_pairs={{0,1},{1,2},{2,3},{4,5},{5,6},{6,7},{8,9},{9,10},{10,11},{12,13},{... | collective-permute-start | bytes 786440 | tf_op jit(solution)/shard_map/ppermute | solution.py:556
  41.3 11.5 %collective-permute-start.9 = (f32[256,256]{1,0:T(8,128)S(1)}, f32[256,256]{1,0:T(8,128)S(1)}, u32[]{:S(2)}, u32[]{:S(2)}) collective-permute-start(f32[256,256]{1,0:T(8,128)S(1)} %get-tuple-element.51), channel_id=1, source_target_pairs={{1,0},{2,1},{3,2},{5,4},{6,5},{7,6},{9,8},{10,9},{11,10},{13,12},{... | collective-permute-start | bytes 786440 | tf_op jit(solution)/shard_map/ppermute | solution.py:557
  44.6 14.9 %collective-permute-start.13 = (bf16[256,1024]{1,0:T(8,128)(2,1)S(1)}, bf16[256,1024]{1,0:T(8,128)(2,1)S(1)}, u32[]{:S(2)}, u32[]{:S(2)}) collective-permute-start(bf16[256,1024]{1,0:T(8,128)(2,1)S(1)} %get-tuple-element.56.refs_3_.refs_1_), channel_id=1, source_target_pairs={{0,2},{5,7},{10,8},{15,13},{16,18},{21,23},{26,24},{31,29}} | collective-permute-start | bytes 1572872 | tf_op jit(solution)/shard_map/ppermute | solution.py:534
  51.0 1.8 %copy-start.1 = (bf16[3,1024,256]{2,1,0:T(8,128)(2,1)S(1)}, bf16[3,1024,256]{2,1,0:T(8,128)(2,1)}, u32[]{:S(2)}) copy-start(bf16[3,1024,256]{2,1,0:T(8,128)(2,1)} %precision.1) | copy-start | bytes 4718596
  51.0 1.8 %copy-start.3 = (bf16[512,1024]{1,0:T(8,128)(2,1)S(1)}, bf16[512,1024]{1,0:T(8,128)(2,1)}, u32[]{:S(2)}) copy-start(bf16[512,1024]{1,0:T(8,128)(2,1)} %held_ref.3) | copy-start | bytes 3145732
  51.1 1.8 %copy-start.5 = (bf16[512,256]{1,0:T(8,128)(2,1)S(1)}, bf16[512,256]{1,0:T(8,128)(2,1)}, u32[]{:S(2)}) copy-start(bf16[512,256]{1,0:T(8,128)(2,1)} %copy-done.4) | copy-start | bytes 786436
  51.1 1.8 %copy-start.6 = (s32[512]{0:T(512)S(1)}, s32[512]{0:T(512)}, u32[]{:S(2)}) copy-start(s32[512]{0:T(512)} %param.8) | copy-start | bytes 6148
  51.3 10.3 %collective-permute-start.11 = (bf16[768,1024]{1,0:T(8,128)(2,1)S(1)}, bf16[768,1024]{1,0:T(8,128)(2,1)S(1)}, u32[]{:S(2)}, u32[]{:S(2)}) collective-permute-start(bf16[768,1024]{1,0:T(8,128)(2,1)S(1)} %stack.4.near), channel_id=1, source_target_pairs={{0,1},{2,3},{5,4},{7,6},{10,11},{8,9},{15,14},{13,12},{16,17},{18,... | collective-permute-start | bytes 4718600 | tf_op jit(solution)/shard_map/ppermute | solution.py:534
  57.1 2.4 %collective-permute-start.12 = (f32[1,512]{1,0:T(1,128)S(1)}, f32[1,512]{1,0:T(1,128)S(1)}, u32[]{:S(2)}, u32[]{:S(2)}) collective-permute-start(f32[1,512]{1,0:T(1,128)S(1)} %get-tuple-element.67.refs_5_), channel_id=1, source_target_pairs={{0,1},{1,0},{2,3},{3,2},{4,5},{5,4},{6,7},{7,6},{8,9},{9,8},{10,11... | collective-permute-start | bytes 6152 | tf_op jit(solution)/shard_map/ppermute | solution.py:571
  57.1 8.2 %collective-permute-start.15 = (f32[1,512]{1,0:T(1,128)S(1)}, f32[1,512]{1,0:T(1,128)S(1)}, u32[]{:S(2)}, u32[]{:S(2)}) collective-permute-start(f32[1,512]{1,0:T(1,128)S(1)} %get-tuple-element.67.refs_5_), channel_id=1, source_target_pairs={{0,2},{1,3},{2,0},{3,1},{4,6},{5,7},{6,4},{7,5},{8,10},{9,11},{10,... | collective-permute-start | bytes 6152 | tf_op jit(solution)/shard_map/ppermute | solution.py:575
  59.3 5.9 %collective-permute-start.16 = (f32[1,512]{1,0:T(1,128)S(1)}, f32[1,512]{1,0:T(1,128)S(1)}, u32[]{:S(2)}, u32[]{:S(2)}) collective-permute-start(f32[1,512]{1,0:T(1,128)S(1)} %get-tuple-element.67.refs_5_), channel_id=1, source_target_pairs={{0,3},{1,2},{2,1},{3,0},{4,7},{5,6},{6,5},{7,4},{8,11},{9,10},{10,... | collective-permute-start | bytes 6152 | tf_op jit(solution)/shard_map/ppermute | solution.py:575
  59.5 5.7 %collective-permute-start.14 = (bf16[256,1024]{1,0:T(8,128)(2,1)S(1)}, bf16[256,1024]{1,0:T(8,128)(2,1)S(1)}, u32[]{:S(2)}, u32[]{:S(2)}) collective-permute-start(bf16[256,1024]{1,0:T(8,128)(2,1)S(1)} %stack.5.refs_3_), channel_id=1, source_target_pairs={{0,1},{2,3},{5,4},{7,6},{10,11},{8,9},{15,14},{13,12},{16,17},{18,... | collective-permute-start | bytes 1572872 | tf_op jit(solution)/shard_map/ppermute | solution.py:534
  (1 other events, 0.7 us)

commit v4 on v3

--- a/solution.py
+++ b/solution.py
@@ -143,30 +143,37 @@
         copy.wait()
 
 
-def outgoing_kernel(labels_ref, held_ref, labels_out, head_ref, tail_ref, sem):
+def edges_of(place_ref, first, last, near, far, sem):
+    @pl.when(place_ref[0] // 4 % 2 == 0)
+    def _():
+        wait(fetch(sem, (last, near), (first, far)))
+
+    @pl.when(place_ref[0] // 4 % 2 != 0)
+    def _():
+        wait(fetch(sem, (first, near), (last, far)))
+
+
+def outgoing_kernel(place_ref, labels_ref, held_ref, labels_out, near_ref, far_ref, sem, edge_sem):
     width = held_ref.shape[1]
-    wait(
-        fetch(
-            sem,
-            (labels_ref, labels_out),
-            (held_ref.at[:, pl.ds(0, BLK)], head_ref),
-            (held_ref.at[:, pl.ds(width - BLK, BLK)], tail_ref),
-        )
-    )
-
-
-def outgoing(labels, held):
+    copies = fetch(sem, (labels_ref, labels_out))
+    first = held_ref.at[:, pl.ds(0, BLK)]
+    last = held_ref.at[:, pl.ds(width - BLK, BLK)]
+    edges_of(place_ref, first, last, near_ref, far_ref, edge_sem)
+    wait(copies)
+
+
+def outgoing(place, labels, held):
     edge = jax.ShapeDtypeStruct((held.shape[0], BLK), BF16)
     return pl.pallas_call(
         outgoing_kernel,
         out_shape=(jax.ShapeDtypeStruct(labels.shape, labels.dtype), edge, edge),
-        in_specs=[HBM] * 2,
+        in_specs=[SMEM] + [HBM] * 2,
         out_specs=(VMEM,) * 3,
-        scratch_shapes=[pltpu.SemaphoreType.DMA((3,))],
+        scratch_shapes=[pltpu.SemaphoreType.DMA((1,)), pltpu.SemaphoreType.DMA((2,))],
         compiler_params=SMALL,
         cost_estimate=cost(LONG),
         name="outgoing",
-    )(labels, held)
+    )(place, labels, held)
 
 
 def halves_kernel(own_ref, next_ref, rows_ref, outer_ref, inner_ref, labels, sem):
@@ -244,7 +251,7 @@
     return labels[0:1].astype(F32), labels[1:2].astype(F32), late[0:1], late[1:2]
 
 
-def edges_kernel(own_ref, next_ref, early_ref, third_ref, outer_ref, head_ref, tail_ref,
+def edges_kernel(place_ref, own_ref, next_ref, early_ref, third_ref, outer_ref, near_ref, far_ref,
                  labels, third, outer, sem):
     count, width = third_ref.shape
     copies = fetch(
@@ -261,17 +268,27 @@
     late = jnp.dot(hots[3].astype(BF16), outer[:count, :], preferred_element_type=F32)
     wait(copies[3:])
     late = late + jnp.dot(hots[2].astype(BF16), third[...], preferred_element_type=F32)
-    head_ref[...] = (early_ref[:, :BLK] + late[:, :BLK]) / counts
-    tail_ref[...] = (early_ref[:, width - BLK :] + late[:, BLK:]) / counts
-
-
-def edge_means(own_labels, next_labels, early, third, outer):
+    first = (early_ref[:, :BLK] + late[:, :BLK]) / counts
+    last = (early_ref[:, width - BLK :] + late[:, BLK:]) / counts
+
+    @pl.when(place_ref[0] // 4 % 2 == 0)
+    def _():
+        near_ref[...] = last
+        far_ref[...] = first
+
+    @pl.when(place_ref[0] // 4 % 2 != 0)
+    def _():
+        near_ref[...] = first
+        far_ref[...] = last
+
+
+def edge_means(place, own_labels, next_labels, early, third, outer):
     edge = jax.ShapeDtypeStruct((C, BLK), F32)
     count = third.shape[0]
     return pl.pallas_call(
         edges_kernel,
         out_shape=(edge, edge),
-        in_specs=[HBM, HBM, VMEM, HBM, HBM],
+        in_specs=[SMEM, HBM, HBM, VMEM, HBM, HBM],
         out_specs=(VMEM, VMEM),
         scratch_shapes=[
             pltpu.VMEM((2, count), jnp.int32),
@@ -282,7 +299,7 @@
         compiler_params=SMALL,
         cost_estimate=cost(1),
         name="edge_means",
-    )(own_labels, next_labels, early, third, outer)
+    )(place, own_labels, next_labels, early, third, outer)
 
 
 def means_kernel(own_ref, next_ref, early_ref, third_ref, outer_ref, inner_ref,
@@ -347,7 +364,7 @@
 
     for owner, group in zip((True, False), groups, strict=True):
 
-        @pl.when((role_ref[0] == 0) == owner)
+        @pl.when((role_ref[0] % 4 == 0) == owner)
         def _():
             wait(fetch(sem, *pairs(group)))
 
@@ -367,16 +384,34 @@
     )(role, *own, *other)
 
 
-def white_kernel(held_ref, left_ref, right_ref, means_ref, left_means, right_means, held_labels,
-                 precision, white_ref, score_ref, bands):
+def white_kernel(place_ref, held_ref, near_ref, far_ref, means_ref, near_means, far_means,
+                 held_labels, precision, white_ref, score_ref, bands, held, means):
     width = held_ref.shape[1]
     for k in range(3):
         bands[:, k * BLK : (k + 1) * BLK] = precision[k]
-    means = jnp.concatenate([left_means[...], means_ref[...], right_means[...]], axis=1)
+    held[:, BLK : BLK + width] = held_ref[...]
+    means[:, BLK : BLK + width] = means_ref[...]
+    sides = (slice(0, BLK), slice(BLK + width, 2 * BLK + width))
+    for odd, (far_side, near_side) in enumerate((sides, sides[::-1])):
+
+        @pl.when(place_ref[0] // 4 % 2 == odd)
+        def _():
+            held[:, near_side] = near_ref[...]
+            means[:, near_side] = near_means[...]
+
+        @pl.when(place_ref[0] // 4 == odd)
+        def _():
+            held[:, far_side] = far_ref[...]
+            means[:, far_side] = far_means[...]
+
+        @pl.when(place_ref[0] // 4 == odd + 2)
+        def _():
+            held[:, far_side] = jnp.zeros(far_ref.shape, BF16)
+            means[:, far_side] = jnp.zeros(far_means.shape, F32)
+
     onehot = onehot_rows(held_labels[...]).astype(BF16)
-    picked = sum(contract_rows(onehot, piece) for piece in split3(means))
-    held = jnp.concatenate([left_ref[...], held_ref[...], right_ref[...]], axis=1)
-    centred = held.astype(F32) - picked
+    picked = sum(contract_rows(onehot, piece) for piece in split3(means[...]))
+    centred = held[...].astype(F32) - picked
     pieces = split3(centred)[:2]
     score = jnp.zeros((held_ref.shape[0], 128), F32)
     for m in range(width // BLK):
@@ -391,7 +426,7 @@
     score_ref[...] = jnp.sum(score.T, axis=0, keepdims=True)
 
 
-def whiten(held, left, right, means, left_means, right_means, held_labels, precision):
+def whiten(place, held, near, far, means, near_means, far_means, held_labels, precision):
     count, width = held.shape
     return pl.pallas_call(
         white_kernel,
@@ -399,17 +434,21 @@
             jax.ShapeDtypeStruct((count, width), BF16),
             jax.ShapeDtypeStruct((1, count), F32),
         ),
-        in_specs=[VMEM] * 8,
+        in_specs=[SMEM] + [VMEM] * 8,
         out_specs=(VMEM, VMEM),
-        scratch_shapes=[pltpu.VMEM((width, 3 * BLK), BF16)],
+        scratch_shapes=[
+            pltpu.VMEM((width, 3 * BLK), BF16),
+            pltpu.VMEM((count, width + 2 * BLK), BF16),
+            pltpu.VMEM((C, width + 2 * BLK), F32),
+        ],
         compiler_params=MEDIUM,
         cost_estimate=cost(LONG),
         name="whiten",
-    )(held, left, right, means, left_means, right_means, held_labels, precision)
+    )(place, held, near, far, means, near_means, far_means, held_labels, precision)
 
 
 def choose(role_ref, sem, near, far, target):
-    here = (role_ref[0] % 2) == 0
+    here = role_ref[0] % 2 == 0
 
     @pl.when(here)
     def _():
@@ -525,9 +564,11 @@
     n = 4
     tie = lax.optimization_barrier
     flip = {k: [(i, i ^ k) for i in range(n)] for k in (1, 2, 3)}
-    to_right = [(i, i + 1) for i in range(n - 1)]
-    to_left = [(i + 1, i) for i in range(n - 1)]
-    role = (lax.axis_index("dp") ^ lax.axis_index("feat")).astype(jnp.int32)
+    inward = [(1, 2), (2, 1)]
+    feat = lax.axis_index("feat")
+    at_end = (feat == 0) | (feat == n - 1)
+    role = (lax.axis_index("dp") ^ feat) + n * (feat % 2) + 2 * n * at_end.astype(jnp.int32)
+    role = role.astype(jnp.int32).reshape(1)
 
     def hop(array, *moves):
         pairs = [(d * n + (d ^ s), d * n + (d ^ e)) for d in range(n) for s, e in moves]
@@ -536,42 +577,41 @@
     across_own = hop(train_rows, (0, 2))
     third = lax.ppermute(train_rows, "dp", flip[1])
     second = lax.ppermute(train_rows, "dp", flip[2])
-    own_labels, head, tail = outgoing(train_labels.reshape(1, count), held_rows)
-    left = lax.ppermute(tail, "feat", to_right)
-    right = lax.ppermute(head, "feat", to_left)
-    left, own_labels = tie((left, own_labels))
+    own_labels, near, far = outgoing(role, train_labels.reshape(1, count), held_rows)
+    near = lax.ppermute(near, "feat", flip[1])
+    far = lax.ppermute(far, "feat", flip[3])
+    near, own_labels = tie((near, own_labels))
     next_labels = lax.ppermute(own_labels, "dp", flip[2])
-    third, second, across_own, left, right, next_labels = tie(
-        (third, second, across_own, left, right, next_labels)
+    third, second, across_own, near, far, next_labels = tie(
+        (third, second, across_own, near, far, next_labels)
     )
     second_outer, second_inner = halves(own_labels, next_labels, second)
     outer = lax.ppermute(second_outer, "dp", flip[1])
     inner = lax.ppermute(second_inner, "dp", flip[1])
     early = early_sums(own_labels, next_labels, train_rows, second)
     early, *sent = tie((early, second, third))
-    role = role.reshape(1)
     own_most = stack(role, sent, sent)
     across_most = hop(own_most, (0, 2))
-    head, tail = edge_means(own_labels, next_labels, early, third, outer)
-    left_means = lax.ppermute(tail, "feat", to_right)
-    right_means = lax.ppermute(head, "feat", to_left)
-    inner, head, tail = tie((inner, head, tail))
+    near_edge, far_edge = edge_means(role, own_labels, next_labels, early, third, outer)
+    near_means = lax.ppermute(near_edge, "feat", flip[1])
+    far_means = lax.ppermute(far_edge, "feat", inward)
+    inner, near_edge = tie((inner, near_edge))
     means, fourth, labels = class_means(own_labels, next_labels, early, third, outer, inner)
     across_last = hop(fourth, (0, 2))
     rows = [train_rows, second, third, fourth]
     near_most = stack(role, rows[:3], [across_own, across_most])
-    far_most = hop(near_most, (0, 1), (2, 3))
+    far_most = lax.ppermute(near_most, "feat", flip[1])
     most, last = centre(labels, means, rows)
     most, last, means = tie((most, last, means))
     white, score = whiten(
-        held_rows, left, right, means, left_means, right_means, held_labels.reshape(1, -1), precision
+        role, held_rows, near, far, means, near_means, far_means, held_labels.reshape(1, -1), precision
     )
     score, most = tie((score, most))
     total = gram_most(role, most, near_most, far_most)
     beside = lax.ppermute(score, "feat", flip[1])
     beside, across_last = tie((beside, across_last))
     near_last = stack(role, [fourth], [across_last])
-    far_last = hop(near_last, (0, 1), (2, 3))
+    far_last = lax.ppermute(near_last, "feat", flip[1])
     scores = [score, beside] + [lax.ppermute(score, "feat", flip[k]) for k in (2, 3)]
     cov, distance = gram_last(
         role, total, last, near_last, far_last, scores, 1.0 / (n * count - C), float(n * width)

time: 68.7 us -> 66 us (0.961)
  starting transfers between devices: 30.4 us -> 23.4 us
  waiting for transfers between devices: 19.1 us -> 23.8 us
    ppermute x4 -> x6, waiting for transfers between devices: 1.42 us -> 10.3 us  [the longest x1 8.82 us: four_by_four(): far = lax.ppermute(far, 'feat', flip[3])]
    ppermute x1, waiting for transfers between devices: 13 us -> 7.38 us  [four_by_four(): next_labels = lax.ppermute(own_labels, 'dp', flip[2])]
    ppermute x4 -> x6, starting transfers between devices: 5.33 us -> 1.14 us  [the longest x1 0.67 us: four_by_four(): far_means = lax.ppermute(far_edge, 'feat', inward)]
    ppermute x5 -> x3, starting transfers between devices: 14.9 us -> 11.6 us  [hop(): return lax.ppermute(array, ('dp', 'feat'), pairs)]
    ppermute x5 -> x3, waiting for transfers between devices: 0.01 us -> 1.45 us  [hop(): return lax.ppermute(array, ('dp', 'feat'), pairs)]
    unnamed x16 -> x20, local copies, waits for them, and re-layouts: 2.62 us -> 1.97 us
  transfers between devices with their start and end apart: 17 -> 17, of which waited for: 4 -> 6; matrix products, arithmetic and copies ran while one was open for 0% -> 0% of each run, Pallas kernels for 18% -> 19%
where the time goes in v4:
time: 66 us; the launch traced here: 65.8 us
  waiting for transfers between devices  23.8 us (36%)
  starting transfers between devices  23.4 us (35%)
  Pallas kernels  15.6 us (24%)
  local copies, waits for them, and re-layouts  1.97 us (3%)
  between operations  0.93 us (1%)
    ppermute x3, starting transfers between devices, hop(): return lax.ppermute(array, ('dp', 'feat'), pairs)  11.6 us
    ppermute x1, waiting for transfers between devices, four_by_four(): far = lax.ppermute(far, 'feat', flip[3])  8.82 us
    ppermute x1, waiting for transfers between devices, four_by_four(): next_labels = lax.ppermute(own_labels, 'dp', flip[2])  7.38 us
    pallas_call x1, Pallas kernels, whiten(): pl.pallas_call(white_kernel, out_shape=(jax.ShapeDtypeStruct((count, widt...  4.47 us
    pallas_call x1, Pallas kernels, gram_most(): pl.pallas_call(most_kernel, out_shape=jax.ShapeDtypeStruct((width, width)...  3.61 us
    pallas_call x1, Pallas kernels, gram_last(): pl.pallas_call(lambda *refs: last_kernel(scale, features, *refs), out_sha...  3.09 us
    ppermute x1, starting transfers between devices, four_by_four(): third = lax.ppermute(train_rows, 'dp', flip[1])  3.09 us
    ppermute x1, waiting for transfers between devices, four_by_four(): outer = lax.ppermute(second_outer, 'dp', flip[1])  2.71 us
  transfers between devices with their start and end apart: 17, of which 6 were waited for; matrix products, arithmetic and copies ran while one was open for 0% of the time, Pallas kernels for 19%

profile of v4, /device:TPU:0, one launch (start us, length us, event | category | flops | bytes accessed | tf_op | source)
XLA Modules:
  0.0 65.8 jit_solution(5698874812275167623)
XLA Ops:
  0.6 3.1 %collective-permute-start = (bf16[256,1024]{1,0:T(8,128)(2,1)}, bf16[256,1024]{1,0:T(8,128)(2,1)S(1)}, u32[]{:S(2)}, u32[]{:S(2)}) collective-permute-start(bf16[256,1024]{1,0:T(8,128)(2,1)} %refs_1_.1), channel_id=1, source_target_pairs={{0,4},{4,0},{8,12},{12,8},{1,5},{5,1},{9,13},{13,9},{2,6},{6,2},{1... | collective-permute-start | bytes 1572872 | tf_op jit(solution)/shard_map/ppermute | solution.py:578
  3.7 2.6 %collective-permute-start.1 = (bf16[256,1024]{1,0:T(8,128)(2,1)}, bf16[256,1024]{1,0:T(8,128)(2,1)S(1)}, u32[]{:S(2)}, u32[]{:S(2)}) collective-permute-start(bf16[256,1024]{1,0:T(8,128)(2,1)} %refs_1_.1), channel_id=1, source_target_pairs={{0,8},{4,12},{8,0},{12,4},{1,9},{5,13},{9,1},{13,5},{2,10},{6,14},... | collective-permute-start | bytes 1572872 | tf_op jit(solution)/shard_map/ppermute | solution.py:579
  6.3 3.4 %collective-permute-start.2 = (bf16[256,1024]{1,0:T(8,128)(2,1)}, bf16[256,1024]{1,0:T(8,128)(2,1)S(1)}, u32[]{:S(2)}, u32[]{:S(2)}) collective-permute-start(bf16[256,1024]{1,0:T(8,128)(2,1)} %refs_1_.1), channel_id=1, source_target_pairs={{0,2},{5,7},{10,8},{15,13},{16,18},{21,23},{26,24},{31,29}} | collective-permute-start | bytes 1572872 | tf_op jit(solution)/shard_map/ppermute | solution.py:575
  9.8 1.2 %copy-done.2 = bf16[512,1024]{1,0:T(8,128)(2,1)S(1)} copy-done((bf16[512,1024]{1,0:T(8,128)(2,1)S(1)}, bf16[512,1024]{1,0:T(8,128)(2,1)}, u32[]{:S(2)}) %copy-start.2) | copy-done | bytes 1048600
  11.0 0.7 %copy-done.9 = s32[256,1]{0,1:T(1,128)S(1)} copy-done((s32[256,1]{0,1:T(1,128)S(1)}, s32[256,1]{0,1:T(1,128)}, u32[]{:S(2)}) %copy-start.9) | copy-done | bytes 1048
  11.9 1.4 %collective-permute-done.3.near_ref = bf16[512,256]{1,0:T(8,128)(2,1)S(1)} collective-permute-done((bf16[512,256]{1,0:T(8,128)(2,1)S(1)}, bf16[512,256]{1,0:T(8,128)(2,1)S(1)}, u32[]{:S(2)}, u32[]{:S(2)}) %collective-permute-start.3) | collective-permute-done | bytes 262176 | tf_op jit(solution)/shard_map/ppermute | solution.py:581
  13.4 8.8 %collective-permute-done.4.far_ref = bf16[512,256]{1,0:T(8,128)(2,1)S(1)} collective-permute-done((bf16[512,256]{1,0:T(8,128)(2,1)S(1)}, bf16[512,256]{1,0:T(8,128)(2,1)S(1)}, u32[]{:S(2)}, u32[]{:S(2)}) %collective-permute-start.4) | collective-permute-done | bytes 262176 | tf_op jit(solution)/shard_map/ppermute | solution.py:582
  22.2 7.4 %collective-permute-done.5.next_label.next_ref = s32[1,256]{1,0:T(1,128)S(1)} collective-permute-done((s32[1,256]{1,0:T(1,128)S(1)}, s32[1,256]{1,0:T(1,128)S(1)}, u32[]{:S(2)}, u32[]{:S(2)}) %collective-permute-start.5) | collective-permute-done | bytes 1056 | tf_op jit(solution)/shard_map/ppermute | solution.py:584
  29.7 0.5 collective-permute-start.6
  30.2 1.6 %collective-permute-start.7 = (bf16[256,512]{1,0:T(8,128)(2,1)S(1)}, bf16[256,512]{1,0:T(8,128)(2,1)S(1)}, u32[]{:S(2)}, u32[]{:S(2)}) collective-permute-start(bf16[256,512]{1,0:T(8,128)(2,1)S(1)} %get-tuple-element.50), channel_id=1, source_target_pairs={{0,4},{4,0},{8,12},{12,8},{1,5},{5,1},{9,13},{13,9},{2,6},{6,2},{1... | collective-permute-start | bytes 786440 | tf_op jit(solution)/shard_map/ppermute | solution.py:590
  31.8 0.6 early_sums.1.early_ref
  32.5 3.5 %collective-permute-start.10 = (bf16[512,1024]{1,0:T(8,128)(2,1)S(1)}, bf16[512,1024]{1,0:T(8,128)(2,1)S(1)}, u32[]{:S(2)}, u32[]{:S(2)}) collective-permute-start(bf16[512,1024]{1,0:T(8,128)(2,1)S(1)} %stack.3), channel_id=1, source_target_pairs={{0,2},{5,7},{10,8},{15,13},{16,18},{21,23},{26,24},{31,29}} | collective-permute-start | bytes 3145736 | tf_op jit(solution)/shard_map/ppermute | solution.py:575
  36.0 2.7 %collective-permute-done.6.outer_ref = bf16[272,512]{1,0:T(8,128)(2,1)S(1)} collective-permute-done((bf16[272,512]{1,0:T(8,128)(2,1)S(1)}, bf16[272,512]{1,0:T(8,128)(2,1)S(1)}, u32[]{:S(2)}, u32[]{:S(2)}) %collective-permute-start.6) | collective-permute-done | bytes 278560 | tf_op jit(solution)/shard_map/ppermute | solution.py:589
  38.7 0.7 %edge_means.1 = (f32[256,256]{1,0:T(8,128)S(1)}, f32[256,256]{1,0:T(8,128)S(1)}) custom-call(s32[1]{0:T(128)} %bitcast.place_ref.refs_0_.role_ref, s32[1,256]{1,0:T(1,128)S(1)} %get-tuple-element.42.own_label.own_ref, s32[1,256]{1,0:T(1,128)S(1)} %collective-permute-done.5.next_label.next_ref, f32[256,1024]{1,0:T(8,128)S(1)} %early_sums.1.early_ref, ...), custom_call_target="tpu_custom_call" | custom-call | flops 1 | tf_op jit(solution)/shard_map/edge_means/pallas_call | solution.py:288
  39.5 2.0 %collective-permute-done.7.inner_ref = bf16[256,512]{1,0:T(8,128)(2,1)S(1)} collective-permute-done((bf16[256,512]{1,0:T(8,128)(2,1)S(1)}, bf16[256,512]{1,0:T(8,128)(2,1)S(1)}, u32[]{:S(2)}, u32[]{:S(2)}) %collective-permute-start.7) | collective-permute-done | bytes 262176 | tf_op jit(solution)/shard_map/ppermute | solution.py:590
  41.5 0.7 %collective-permute-start.9 = (f32[256,256]{1,0:T(8,128)S(1)}, f32[256,256]{1,0:T(8,128)S(1)}, u32[]{:S(2)}, u32[]{:S(2)}) collective-permute-start(f32[256,256]{1,0:T(8,128)S(1)} %get-tuple-element.59), channel_id=1, source_target_pairs={{1,2},{2,1},{5,6},{6,5},{9,10},{10,9},{13,14},{14,13},{17,18},{18,... | collective-permute-start | bytes 786440 | tf_op jit(solution)/shard_map/ppermute | solution.py:597
  42.2 0.6 class_means.1
  42.8 4.7 %collective-permute-start.13 = (bf16[256,1024]{1,0:T(8,128)(2,1)S(1)}, bf16[256,1024]{1,0:T(8,128)(2,1)S(1)}, u32[]{:S(2)}, u32[]{:S(2)}) collective-permute-start(bf16[256,1024]{1,0:T(8,128)(2,1)S(1)} %get-tuple-element.55.refs_3_.refs_1_), channel_id=1, source_target_pairs={{0,2},{5,7},{10,8},{15,13},{16,18},{21,23},{26,24},{31,29}} | collective-permute-start | bytes 1572872 | tf_op jit(solution)/shard_map/ppermute | solution.py:575
  47.5 2.0 %centre.1 = (bf16[1536,1024]{1,0:T(8,128)(2,1)S(1)}, bf16[512,1024]{1,0:T(8,128)(2,1)S(1)}) custom-call(f32[4,256]{1,0:T(4,128)S(1)} %get-tuple-element.53.labels_ref, f32[256,1024]{1,0:T(8,128)S(1)} %get-tuple-element.58.means_ref, bf16[256,1024]{1,0:T(8,128)(2,1)S(1)} %copy-done, ...), custom_call_target="tpu_custom_call" | custom-call | flops 1 | tf_op jit(solution)/shard_map/centre/pallas_call | solution.py:483
  49.6 1.4 %collective-permute-done.10.refs_5_ = bf16[512,1024]{1,0:T(8,128)(2,1)S(1)} collective-permute-done((bf16[512,1024]{1,0:T(8,128)(2,1)S(1)}, bf16[512,1024]{1,0:T(8,128)(2,1)S(1)}, u32[]{:S(2)}, u32[]{:S(2)}) %collective-permute-start.10) | collective-permute-done | bytes 1048608 | tf_op jit(solution)/shard_map/ppermute | solution.py:575
  51.3 4.5 %whiten.1 = (bf16[512,1024]{1,0:T(8,128)(2,1)}, f32[1,512]{1,0:T(1,128)S(1)}) custom-call(s32[1]{0:T(128)} %bitcast.place_ref.refs_0_.role_ref, bf16[512,1024]{1,0:T(8,128)(2,1)S(1)} %copy-done.3, bf16[512,256]{1,0:T(8,128)(2,1)S(1)} %copy-done.5, bf16[512,256]{1,0:T(8,128)(2,1)S(1)} %copy-done.7, f32[256,1024]{1,0:T(8,128)S(1)} %get-tuple-element.58.means_ref, ...), custom_call_target="tpu_custom_call" | custom-call | flops 99999997952 | tf_op jit(solution)/shard_map/whiten/pallas_call | solution.py:431
  56.3 2.5 %collective-permute-start.15 = (f32[1,512]{1,0:T(1,128)S(1)}, f32[1,512]{1,0:T(1,128)S(1)}, u32[]{:S(2)}, u32[]{:S(2)}) collective-permute-start(f32[1,512]{1,0:T(1,128)S(1)} %get-tuple-element.67.refs_5_), channel_id=1, source_target_pairs={{0,2},{1,3},{2,0},{3,1},{4,6},{5,7},{6,4},{7,5},{8,10},{9,11},{10,... | collective-permute-start | bytes 6152 | tf_op jit(solution)/shard_map/ppermute | solution.py:615
  59.0 3.6 %gram_most.1.refs_1_ = f32[1024,1024]{1,0:T(8,128)S(1)} custom-call(s32[1]{0:T(128)} %bitcast.place_ref.refs_0_.role_ref, bf16[1536,1024]{1,0:T(8,128)(2,1)S(1)} %get-tuple-element.62.left, bf16[768,1024]{1,0:T(8,128)(2,1)S(1)} %stack.4.near, bf16[768,1024]{1,0:T(8,128)(2,1)S(1)} %collective-permute-done.11.far), custom_call_target="tpu_custom_call" | custom-call | flops 99999997952 | tf_op jit(solution)/shard_map/gram_most/pallas_call | solution.py:507
  62.7 3.1 %gram_last.1 = (f32[1024,1024]{1,0:T(8,128)}, f32[1,512]{1,0:T(1,128)}) custom-call(s32[1]{0:T(128)} %bitcast.place_ref.refs_0_.role_ref, f32[1024,1024]{1,0:T(8,128)S(1)} %gram_most.1.refs_1_, bf16[512,1024]{1,0:T(8,128)(2,1)S(1)} %get-tuple-element.66.refs_2_, bf16[256,1024]{1,0:T(8,128)(2,1)S(1)} %stack.5.refs_3_, ...), custom_call_target="tpu_custom_call" | custom-call | flops 99999997952 | tf_op jit(solution)/shard_map/gram_last/pallas_call | solution.py:542
  (42 shorter events, 1.6 us)
Async XLA Ops:
  0.6 29.0 %collective-permute-start = (bf16[256,1024]{1,0:T(8,128)(2,1)}, bf16[256,1024]{1,0:T(8,128)(2,1)S(1)}, u32[]{:S(2)}, u32[]{:S(2)}) collective-permute-start(bf16[256,1024]{1,0:T(8,128)(2,1)} %refs_1_.1), channel_id=1, source_target_pairs={{0,4},{4,0},{8,12},{12,8},{1,5},{5,1},{9,13},{13,9},{2,6},{6,2},{1... | collective-permute-start | bytes 1572872 | tf_op jit(solution)/shard_map/ppermute | solution.py:578
  3.7 25.9 %collective-permute-start.1 = (bf16[256,1024]{1,0:T(8,128)(2,1)}, bf16[256,1024]{1,0:T(8,128)(2,1)S(1)}, u32[]{:S(2)}, u32[]{:S(2)}) collective-permute-start(bf16[256,1024]{1,0:T(8,128)(2,1)} %refs_1_.1), channel_id=1, source_target_pairs={{0,8},{4,12},{8,0},{12,4},{1,9},{5,13},{9,1},{13,5},{2,10},{6,14},... | collective-permute-start | bytes 1572872 | tf_op jit(solution)/shard_map/ppermute | solution.py:579
  6.3 23.3 %collective-permute-start.2 = (bf16[256,1024]{1,0:T(8,128)(2,1)}, bf16[256,1024]{1,0:T(8,128)(2,1)S(1)}, u32[]{:S(2)}, u32[]{:S(2)}) collective-permute-start(bf16[256,1024]{1,0:T(8,128)(2,1)} %refs_1_.1), channel_id=1, source_target_pairs={{0,2},{5,7},{10,8},{15,13},{16,18},{21,23},{26,24},{31,29}} | collective-permute-start | bytes 1572872 | tf_op jit(solution)/shard_map/ppermute | solution.py:575
  11.7 20.2 %copy-start = (bf16[256,1024]{1,0:T(8,128)(2,1)S(1)}, bf16[256,1024]{1,0:T(8,128)(2,1)}, u32[]{:S(2)}) copy-start(bf16[256,1024]{1,0:T(8,128)(2,1)} %refs_1_.1) | copy-start | bytes 1572868
  11.8 1.6 %collective-permute-start.3 = (bf16[512,256]{1,0:T(8,128)(2,1)S(1)}, bf16[512,256]{1,0:T(8,128)(2,1)S(1)}, u32[]{:S(2)}, u32[]{:S(2)}) collective-permute-start(bf16[512,256]{1,0:T(8,128)(2,1)S(1)} %get-tuple-element.38), channel_id=1, source_target_pairs={{0,1},{1,0},{2,3},{3,2},{4,5},{5,4},{6,7},{7,6},{8,9},{9,8},{10,11... | collective-permute-start | bytes 786440 | tf_op jit(solution)/shard_map/ppermute | solution.py:581
  11.9 10.3 %collective-permute-start.4 = (bf16[512,256]{1,0:T(8,128)(2,1)S(1)}, bf16[512,256]{1,0:T(8,128)(2,1)S(1)}, u32[]{:S(2)}, u32[]{:S(2)}) collective-permute-start(bf16[512,256]{1,0:T(8,128)(2,1)S(1)} %get-tuple-element.41), channel_id=1, source_target_pairs={{0,3},{1,2},{2,1},{3,0},{4,7},{5,6},{6,5},{7,4},{8,11},{9,10},{10,... | collective-permute-start | bytes 786440 | tf_op jit(solution)/shard_map/ppermute | solution.py:582
  13.4 19.0 %copy-start.4 = (bf16[512,256]{1,0:T(8,128)(2,1)}, bf16[512,256]{1,0:T(8,128)(2,1)S(1)}, u32[]{:S(2)}) copy-start(bf16[512,256]{1,0:T(8,128)(2,1)S(1)} %collective-permute-done.3.near_ref) | copy-start | bytes 786436
  13.4 16.2 %collective-permute-start.5 = (s32[1,256]{1,0:T(1,128)S(1)}, s32[1,256]{1,0:T(1,128)S(1)}, u32[]{:S(2)}, u32[]{:S(2)}) collective-permute-start(s32[1,256]{1,0:T(1,128)S(1)} %get-tuple-element.42.own_label.own_ref), channel_id=1, source_target_pairs={{0,8},{4,12},{8,0},{12,4},{1,9},{5,13},{9,1},{13,5},{2,10},{6,14},... | collective-permute-start | bytes 3080 | tf_op jit(solution)/shard_map/ppermute | solution.py:584
  22.2 9.6 %copy-start.6 = (bf16[512,256]{1,0:T(8,128)(2,1)}, bf16[512,256]{1,0:T(8,128)(2,1)S(1)}, u32[]{:S(2)}) copy-start(bf16[512,256]{1,0:T(8,128)(2,1)S(1)} %collective-permute-done.4.far_ref) | copy-start | bytes 786436
  29.7 9.0 %collective-permute-start.6 = (bf16[272,512]{1,0:T(8,128)(2,1)S(1)}, bf16[272,512]{1,0:T(8,128)(2,1)S(1)}, u32[]{:S(2)}, u32[]{:S(2)}) collective-permute-start(bf16[272,512]{1,0:T(8,128)(2,1)S(1)} %get-tuple-element.49), channel_id=1, source_target_pairs={{0,4},{4,0},{8,12},{12,8},{1,5},{5,1},{9,13},{13,9},{2,6},{6,2},{1... | collective-permute-start | bytes 835592 | tf_op jit(solution)/shard_map/ppermute | solution.py:589
  30.2 11.3 %collective-permute-start.7 = (bf16[256,512]{1,0:T(8,128)(2,1)S(1)}, bf16[256,512]{1,0:T(8,128)(2,1)S(1)}, u32[]{:S(2)}, u32[]{:S(2)}) collective-permute-start(bf16[256,512]{1,0:T(8,128)(2,1)S(1)} %get-tuple-element.50), channel_id=1, source_target_pairs={{0,4},{4,0},{8,12},{12,8},{1,5},{5,1},{9,13},{13,9},{2,6},{6,2},{1... | collective-permute-start | bytes 786440 | tf_op jit(solution)/shard_map/ppermute | solution.py:590
  32.5 18.5 %collective-permute-start.10 = (bf16[512,1024]{1,0:T(8,128)(2,1)S(1)}, bf16[512,1024]{1,0:T(8,128)(2,1)S(1)}, u32[]{:S(2)}, u32[]{:S(2)}) collective-permute-start(bf16[512,1024]{1,0:T(8,128)(2,1)S(1)} %stack.3), channel_id=1, source_target_pairs={{0,2},{5,7},{10,8},{15,13},{16,18},{21,23},{26,24},{31,29}} | collective-permute-start | bytes 3145736 | tf_op jit(solution)/shard_map/ppermute | solution.py:575
  39.4 11.8 %collective-permute-start.8 = (f32[256,256]{1,0:T(8,128)S(1)}, f32[256,256]{1,0:T(8,128)S(1)}, u32[]{:S(2)}, u32[]{:S(2)}) collective-permute-start(f32[256,256]{1,0:T(8,128)S(1)} %get-tuple-element.51), channel_id=1, source_target_pairs={{0,1},{1,0},{2,3},{3,2},{4,5},{5,4},{6,7},{7,6},{8,9},{9,8},{10,11... | collective-permute-start | bytes 786440 | tf_op jit(solution)/shard_map/ppermute | solution.py:596
  41.5 9.7 %collective-permute-start.9 = (f32[256,256]{1,0:T(8,128)S(1)}, f32[256,256]{1,0:T(8,128)S(1)}, u32[]{:S(2)}, u32[]{:S(2)}) collective-permute-start(f32[256,256]{1,0:T(8,128)S(1)} %get-tuple-element.59), channel_id=1, source_target_pairs={{1,2},{2,1},{5,6},{6,5},{9,10},{10,9},{13,14},{14,13},{17,18},{18,... | collective-permute-start | bytes 786440 | tf_op jit(solution)/shard_map/ppermute | solution.py:597
  42.8 15.9 %collective-permute-start.13 = (bf16[256,1024]{1,0:T(8,128)(2,1)S(1)}, bf16[256,1024]{1,0:T(8,128)(2,1)S(1)}, u32[]{:S(2)}, u32[]{:S(2)}) collective-permute-start(bf16[256,1024]{1,0:T(8,128)(2,1)S(1)} %get-tuple-element.55.refs_3_.refs_1_), channel_id=1, source_target_pairs={{0,2},{5,7},{10,8},{15,13},{16,18},{21,23},{26,24},{31,29}} | collective-permute-start | bytes 1572872 | tf_op jit(solution)/shard_map/ppermute | solution.py:575
  49.5 1.8 %copy-start.1 = (bf16[3,1024,256]{2,1,0:T(8,128)(2,1)S(1)}, bf16[3,1024,256]{2,1,0:T(8,128)(2,1)}, u32[]{:S(2)}) copy-start(bf16[3,1024,256]{2,1,0:T(8,128)(2,1)} %precision.1) | copy-start | bytes 4718596
  49.5 1.8 %copy-start.3 = (bf16[512,1024]{1,0:T(8,128)(2,1)S(1)}, bf16[512,1024]{1,0:T(8,128)(2,1)}, u32[]{:S(2)}) copy-start(bf16[512,1024]{1,0:T(8,128)(2,1)} %held_ref.3) | copy-start | bytes 3145732
  49.5 1.8 %copy-start.7 = (bf16[512,256]{1,0:T(8,128)(2,1)S(1)}, bf16[512,256]{1,0:T(8,128)(2,1)}, u32[]{:S(2)}) copy-start(bf16[512,256]{1,0:T(8,128)(2,1)} %copy-done.6) | copy-start | bytes 786436
  49.5 1.8 %copy-start.8 = (s32[512]{0:T(512)S(1)}, s32[512]{0:T(512)}, u32[]{:S(2)}) copy-start(s32[512]{0:T(512)} %param.8) | copy-start | bytes 6148
  51.2 7.9 %collective-permute-start.11 = (bf16[768,1024]{1,0:T(8,128)(2,1)S(1)}, bf16[768,1024]{1,0:T(8,128)(2,1)S(1)}, u32[]{:S(2)}, u32[]{:S(2)}) collective-permute-start(bf16[768,1024]{1,0:T(8,128)(2,1)S(1)} %stack.4.near), channel_id=1, source_target_pairs={{0,1},{1,0},{2,3},{3,2},{4,5},{5,4},{6,7},{7,6},{8,9},{9,8},{10,11... | collective-permute-start | bytes 4718600 | tf_op jit(solution)/shard_map/ppermute | solution.py:603
  55.8 2.9 %collective-permute-start.12 = (f32[1,512]{1,0:T(1,128)S(1)}, f32[1,512]{1,0:T(1,128)S(1)}, u32[]{:S(2)}, u32[]{:S(2)}) collective-permute-start(f32[1,512]{1,0:T(1,128)S(1)} %get-tuple-element.67.refs_5_), channel_id=1, source_target_pairs={{0,1},{1,0},{2,3},{3,2},{4,5},{5,4},{6,7},{7,6},{8,9},{9,8},{10,11... | collective-permute-start | bytes 6152 | tf_op jit(solution)/shard_map/ppermute | solution.py:611
  56.3 6.4 %collective-permute-start.15 = (f32[1,512]{1,0:T(1,128)S(1)}, f32[1,512]{1,0:T(1,128)S(1)}, u32[]{:S(2)}, u32[]{:S(2)}) collective-permute-start(f32[1,512]{1,0:T(1,128)S(1)} %get-tuple-element.67.refs_5_), channel_id=1, source_target_pairs={{0,2},{1,3},{2,0},{3,1},{4,6},{5,7},{6,4},{7,5},{8,10},{9,11},{10,... | collective-permute-start | bytes 6152 | tf_op jit(solution)/shard_map/ppermute | solution.py:615
  58.7 3.9 %collective-permute-start.16 = (f32[1,512]{1,0:T(1,128)S(1)}, f32[1,512]{1,0:T(1,128)S(1)}, u32[]{:S(2)}, u32[]{:S(2)}) collective-permute-start(f32[1,512]{1,0:T(1,128)S(1)} %get-tuple-element.67.refs_5_), channel_id=1, source_target_pairs={{0,3},{1,2},{2,1},{3,0},{4,7},{5,6},{6,5},{7,4},{8,11},{9,10},{10,... | collective-permute-start | bytes 6152 | tf_op jit(solution)/shard_map/ppermute | solution.py:615
  58.8 3.8 %collective-permute-start.14 = (bf16[256,1024]{1,0:T(8,128)(2,1)S(1)}, bf16[256,1024]{1,0:T(8,128)(2,1)S(1)}, u32[]{:S(2)}, u32[]{:S(2)}) collective-permute-start(bf16[256,1024]{1,0:T(8,128)(2,1)S(1)} %stack.5.refs_3_), channel_id=1, source_target_pairs={{0,1},{1,0},{2,3},{3,2},{4,5},{5,4},{6,7},{7,6},{8,9},{9,8},{10,11... | collective-permute-start | bytes 1572872 | tf_op jit(solution)/shard_map/ppermute | solution.py:614
  (3 other events, 3.7 us)

commit v5 on v4

--- a/solution.py
+++ b/solution.py
@@ -18,7 +18,7 @@
 HBM = pl.BlockSpec(memory_space=pltpu.HBM)
 SMALL = pltpu.CompilerParams(vmem_limit_bytes=8 * 1024 * 1024)
 MEDIUM = pltpu.CompilerParams(vmem_limit_bytes=20 * 1024 * 1024)
-LARGE = pltpu.CompilerParams(vmem_limit_bytes=24 * 1024 * 1024)
+MIDDLE = pltpu.CompilerParams(vmem_limit_bytes=12 * 1024 * 1024)
 
 
 def padded(cells, sides, width):
@@ -346,7 +346,7 @@
             pltpu.VMEM(inner.shape, BF16),
             pltpu.SemaphoreType.DMA((5,)),
         ],
-        compiler_params=MEDIUM,
+        compiler_params=MIDDLE,
         cost_estimate=cost(LONG),
         name="class_means",
     )(own_labels, next_labels, early, third, outer, inner)
@@ -488,7 +488,7 @@
         ),
         in_specs=[VMEM] * (2 + len(rows)),
         out_specs=(VMEM, VMEM),
-        compiler_params=MEDIUM,
+        compiler_params=MIDDLE,
         cost_estimate=cost(1),
         name="centre",
     )(labels, means, *rows)
@@ -510,7 +510,7 @@
         in_specs=[SMEM, VMEM, ANY, ANY],
         out_specs=VMEM,
         scratch_shapes=[pltpu.VMEM(near.shape, BF16), pltpu.SemaphoreType.DMA((1,))],
-        compiler_params=MEDIUM,
+        compiler_params=MIDDLE,
         cost_estimate=cost(LONG),
         name="gram_most",
     )(role, centred, near, far)
@@ -553,7 +553,7 @@
             pltpu.SemaphoreType.DMA((1,)),
             pltpu.SemaphoreType.DMA((width // TILE,)),
         ],
-        compiler_params=MEDIUM,
+        compiler_params=MIDDLE,
         cost_estimate=cost(LONG),
         name="gram_last",
     )(role, total, last, near, far, *scores)
@@ -582,8 +582,8 @@
     far = lax.ppermute(far, "feat", flip[3])
     near, own_labels = tie((near, own_labels))
     next_labels = lax.ppermute(own_labels, "dp", flip[2])
-    third, second, across_own, near, far, next_labels = tie(
-        (third, second, across_own, near, far, next_labels)
+    second, third, across_own, near, far, next_labels = tie(
+        (second, third, across_own, near, far, next_labels)
     )
     second_outer, second_inner = halves(own_labels, next_labels, second)
     outer = lax.ppermute(second_outer, "dp", flip[1])

time: 66 us -> 65.5 us (level)
  local copies, waits for them, and re-layouts: 1.97 us -> 3.41 us
  waiting for transfers between devices: 23.8 us -> 22.7 us
  starting transfers between devices: 23.4 us -> 22.7 us
    ppermute x1, starting transfers between devices: 2.59 us -> 4.1 us  [four_by_four(): second = lax.ppermute(train_rows, 'dp', flip[2])]
    ppermute x1, starting transfers between devices: 3.09 us -> 1.58 us  [four_by_four(): third = lax.ppermute(train_rows, 'dp', flip[1])]
    ppermute x3, waiting for transfers between devices: 1.45 us -> 0.01 us  [hop(): return lax.ppermute(array, ('dp', 'feat'), pairs)]
    unnamed x20, local copies, waits for them, and re-layouts: 1.97 us -> 3.41 us
    ppermute x1, waiting for transfers between devices: 7.38 us -> 6.06 us  [four_by_four(): next_labels = lax.ppermute(own_labels, 'dp', flip[2])]
    ppermute x1, starting transfers between devices: 1.62 us -> 0.55 us  [four_by_four(): inner = lax.ppermute(second_inner, 'dp', flip[1])]
    ppermute x1, starting transfers between devices: 0.48 us -> 1.54 us  [four_by_four(): outer = lax.ppermute(second_outer, 'dp', flip[1])]
    ppermute x1, waiting for transfers between devices: 2.02 us -> 2.84 us  [four_by_four(): inner = lax.ppermute(second_inner, 'dp', flip[1])]
where the time goes in v5:
time: 65.5 us; the launch traced here: 65.3 us
  starting transfers between devices  22.7 us (35%)
  waiting for transfers between devices  22.7 us (35%)
  Pallas kernels  15.6 us (24%)
  local copies, waits for them, and re-layouts  3.41 us (5%)
  between operations  0.91 us (1%)
    ppermute x3, starting transfers between devices, hop(): return lax.ppermute(array, ('dp', 'feat'), pairs)  11.4 us
    ppermute x1, waiting for transfers between devices, four_by_four(): far = lax.ppermute(far, 'feat', flip[3])  8.82 us
    ppermute x1, waiting for transfers between devices, four_by_four(): next_labels = lax.ppermute(own_labels, 'dp', flip[2])  6.06 us
    pallas_call x1, Pallas kernels, whiten(): pl.pallas_call(white_kernel, out_shape=(jax.ShapeDtypeStruct((count, widt...  4.47 us
    ppermute x1, starting transfers between devices, four_by_four(): second = lax.ppermute(train_rows, 'dp', flip[2])  4.1 us
    pallas_call x1, Pallas kernels, gram_most(): pl.pallas_call(most_kernel, out_shape=jax.ShapeDtypeStruct((width, width)...  3.61 us
    unnamed x20, local copies, waits for them, and re-layouts  3.41 us
    ppermute x1, waiting for transfers between devices, four_by_four(): outer = lax.ppermute(second_outer, 'dp', flip[1])  3.34 us
  transfers between devices with their start and end apart: 17, of which 6 were waited for; matrix products, arithmetic and copies ran while one was open for 0% of the time, Pallas kernels for 19%

profile of v5, /device:TPU:0, one launch (start us, length us, event | category | flops | bytes accessed | tf_op | source)
XLA Modules:
  0.0 65.3 jit_solution(11223414582571882474)
XLA Ops:
  0.6 4.1 %collective-permute-start = (bf16[256,1024]{1,0:T(8,128)(2,1)}, bf16[256,1024]{1,0:T(8,128)(2,1)S(1)}, u32[]{:S(2)}, u32[]{:S(2)}) collective-permute-start(bf16[256,1024]{1,0:T(8,128)(2,1)} %refs_1_.1), channel_id=1, source_target_pairs={{0,8},{4,12},{8,0},{12,4},{1,9},{5,13},{9,1},{13,5},{2,10},{6,14},... | collective-permute-start | bytes 1572872 | tf_op jit(solution)/shard_map/ppermute | solution.py:579
  4.7 1.6 %collective-permute-start.1 = (bf16[256,1024]{1,0:T(8,128)(2,1)}, bf16[256,1024]{1,0:T(8,128)(2,1)S(1)}, u32[]{:S(2)}, u32[]{:S(2)}) collective-permute-start(bf16[256,1024]{1,0:T(8,128)(2,1)} %refs_1_.1), channel_id=1, source_target_pairs={{0,4},{4,0},{8,12},{12,8},{1,5},{5,1},{9,13},{13,9},{2,6},{6,2},{1... | collective-permute-start | bytes 1572872 | tf_op jit(solution)/shard_map/ppermute | solution.py:578
  6.3 3.4 %collective-permute-start.2 = (bf16[256,1024]{1,0:T(8,128)(2,1)}, bf16[256,1024]{1,0:T(8,128)(2,1)S(1)}, u32[]{:S(2)}, u32[]{:S(2)}) collective-permute-start(bf16[256,1024]{1,0:T(8,128)(2,1)} %refs_1_.1), channel_id=1, source_target_pairs={{0,2},{5,7},{10,8},{15,13},{16,18},{21,23},{26,24},{31,29}} | collective-permute-start | bytes 1572872 | tf_op jit(solution)/shard_map/ppermute | solution.py:575
  9.8 1.2 %copy-done.2 = bf16[512,1024]{1,0:T(8,128)(2,1)S(1)} copy-done((bf16[512,1024]{1,0:T(8,128)(2,1)S(1)}, bf16[512,1024]{1,0:T(8,128)(2,1)}, u32[]{:S(2)}) %copy-start.2) | copy-done | bytes 1048600
  11.0 0.7 %copy-done.9 = s32[256,1]{0,1:T(1,128)S(1)} copy-done((s32[256,1]{0,1:T(1,128)S(1)}, s32[256,1]{0,1:T(1,128)}, u32[]{:S(2)}) %copy-start.9) | copy-done | bytes 1048
  11.9 1.4 %collective-permute-done.3.near_ref = bf16[512,256]{1,0:T(8,128)(2,1)S(1)} collective-permute-done((bf16[512,256]{1,0:T(8,128)(2,1)S(1)}, bf16[512,256]{1,0:T(8,128)(2,1)S(1)}, u32[]{:S(2)}, u32[]{:S(2)}) %collective-permute-start.3) | collective-permute-done | bytes 262176 | tf_op jit(solution)/shard_map/ppermute | solution.py:581
  13.4 8.8 %collective-permute-done.4.far_ref = bf16[512,256]{1,0:T(8,128)(2,1)S(1)} collective-permute-done((bf16[512,256]{1,0:T(8,128)(2,1)S(1)}, bf16[512,256]{1,0:T(8,128)(2,1)S(1)}, u32[]{:S(2)}, u32[]{:S(2)}) %collective-permute-start.4) | collective-permute-done | bytes 262176 | tf_op jit(solution)/shard_map/ppermute | solution.py:582
  22.2 6.1 %collective-permute-done.5.next_label.next_ref = s32[1,256]{1,0:T(1,128)S(1)} collective-permute-done((s32[1,256]{1,0:T(1,128)S(1)}, s32[1,256]{1,0:T(1,128)S(1)}, u32[]{:S(2)}, u32[]{:S(2)}) %collective-permute-start.5) | collective-permute-done | bytes 1056 | tf_op jit(solution)/shard_map/ppermute | solution.py:584
  28.5 1.5 %collective-permute-start.6 = (bf16[272,512]{1,0:T(8,128)(2,1)S(1)}, bf16[272,512]{1,0:T(8,128)(2,1)S(1)}, u32[]{:S(2)}, u32[]{:S(2)}) collective-permute-start(bf16[272,512]{1,0:T(8,128)(2,1)S(1)} %get-tuple-element.49), channel_id=1, source_target_pairs={{0,4},{4,0},{8,12},{12,8},{1,5},{5,1},{9,13},{13,9},{2,6},{6,2},{1... | collective-permute-start | bytes 835592 | tf_op jit(solution)/shard_map/ppermute | solution.py:589
  30.1 0.6 collective-permute-start.7
  30.6 0.6 early_sums.1.early_ref
  31.3 3.5 %collective-permute-start.10 = (bf16[512,1024]{1,0:T(8,128)(2,1)S(1)}, bf16[512,1024]{1,0:T(8,128)(2,1)S(1)}, u32[]{:S(2)}, u32[]{:S(2)}) collective-permute-start(bf16[512,1024]{1,0:T(8,128)(2,1)S(1)} %stack.3), channel_id=1, source_target_pairs={{0,2},{5,7},{10,8},{15,13},{16,18},{21,23},{26,24},{31,29}} | collective-permute-start | bytes 3145736 | tf_op jit(solution)/shard_map/ppermute | solution.py:575
  34.9 3.3 %collective-permute-done.6.outer_ref = bf16[272,512]{1,0:T(8,128)(2,1)S(1)} collective-permute-done((bf16[272,512]{1,0:T(8,128)(2,1)S(1)}, bf16[272,512]{1,0:T(8,128)(2,1)S(1)}, u32[]{:S(2)}, u32[]{:S(2)}) %collective-permute-start.6) | collective-permute-done | bytes 278560 | tf_op jit(solution)/shard_map/ppermute | solution.py:589
  38.2 0.7 %edge_means.1 = (f32[256,256]{1,0:T(8,128)S(1)}, f32[256,256]{1,0:T(8,128)S(1)}) custom-call(s32[1]{0:T(128)} %bitcast.place_ref.refs_0_.role_ref, s32[1,256]{1,0:T(1,128)S(1)} %get-tuple-element.42.own_label.own_ref, s32[1,256]{1,0:T(1,128)S(1)} %collective-permute-done.5.next_label.next_ref, f32[256,1024]{1,0:T(8,128)S(1)} %early_sums.1.early_ref, ...), custom_call_target="tpu_custom_call" | custom-call | flops 1 | tf_op jit(solution)/shard_map/edge_means/pallas_call | solution.py:288
  39.0 2.8 %collective-permute-done.7.inner_ref = bf16[256,512]{1,0:T(8,128)(2,1)S(1)} collective-permute-done((bf16[256,512]{1,0:T(8,128)(2,1)S(1)}, bf16[256,512]{1,0:T(8,128)(2,1)S(1)}, u32[]{:S(2)}, u32[]{:S(2)}) %collective-permute-start.7) | collective-permute-done | bytes 262176 | tf_op jit(solution)/shard_map/ppermute | solution.py:590
  41.8 0.7 %collective-permute-start.9 = (f32[256,256]{1,0:T(8,128)S(1)}, f32[256,256]{1,0:T(8,128)S(1)}, u32[]{:S(2)}, u32[]{:S(2)}) collective-permute-start(f32[256,256]{1,0:T(8,128)S(1)} %get-tuple-element.59), channel_id=1, source_target_pairs={{1,2},{2,1},{5,6},{6,5},{9,10},{10,9},{13,14},{14,13},{17,18},{18,... | collective-permute-start | bytes 786440 | tf_op jit(solution)/shard_map/ppermute | solution.py:597
  42.5 0.6 class_means.1
  43.1 4.4 %collective-permute-start.13 = (bf16[256,1024]{1,0:T(8,128)(2,1)S(1)}, bf16[256,1024]{1,0:T(8,128)(2,1)S(1)}, u32[]{:S(2)}, u32[]{:S(2)}) collective-permute-start(bf16[256,1024]{1,0:T(8,128)(2,1)S(1)} %get-tuple-element.55.refs_3_.refs_1_), channel_id=1, source_target_pairs={{0,2},{5,7},{10,8},{15,13},{16,18},{21,23},{26,24},{31,29}} | collective-permute-start | bytes 1572872 | tf_op jit(solution)/shard_map/ppermute | solution.py:575
  47.6 2.0 %centre.1 = (bf16[1536,1024]{1,0:T(8,128)(2,1)S(1)}, bf16[512,1024]{1,0:T(8,128)(2,1)S(1)}) custom-call(f32[4,256]{1,0:T(4,128)S(1)} %get-tuple-element.53.labels_ref, f32[256,1024]{1,0:T(8,128)S(1)} %get-tuple-element.58.means_ref, bf16[256,1024]{1,0:T(8,128)(2,1)S(1)} %copy-done, ...), custom_call_target="tpu_custom_call" | custom-call | flops 1 | tf_op jit(solution)/shard_map/centre/pallas_call | solution.py:483
  49.9 1.1 %copy-done.1 = bf16[3,1024,256]{2,1,0:T(8,128)(2,1)S(1)} copy-done((bf16[3,1024,256]{2,1,0:T(8,128)(2,1)S(1)}, bf16[3,1024,256]{2,1,0:T(8,128)(2,1)}, u32[]{:S(2)}) %copy-start.1) | copy-done | bytes 1572888
  51.4 4.5 %whiten.1 = (bf16[512,1024]{1,0:T(8,128)(2,1)}, f32[1,512]{1,0:T(1,128)S(1)}) custom-call(s32[1]{0:T(128)} %bitcast.place_ref.refs_0_.role_ref, bf16[512,1024]{1,0:T(8,128)(2,1)S(1)} %copy-done.3, bf16[512,256]{1,0:T(8,128)(2,1)S(1)} %copy-done.5, bf16[512,256]{1,0:T(8,128)(2,1)S(1)} %copy-done.7, f32[256,1024]{1,0:T(8,128)S(1)} %get-tuple-element.58.means_ref, ...), custom_call_target="tpu_custom_call" | custom-call | flops 99999997952 | tf_op jit(solution)/shard_map/whiten/pallas_call | solution.py:431
  55.9 2.3 %collective-permute-start.15 = (f32[1,512]{1,0:T(1,128)S(1)}, f32[1,512]{1,0:T(1,128)S(1)}, u32[]{:S(2)}, u32[]{:S(2)}) collective-permute-start(f32[1,512]{1,0:T(1,128)S(1)} %get-tuple-element.67.refs_5_), channel_id=1, source_target_pairs={{0,2},{1,3},{2,0},{3,1},{4,6},{5,7},{6,4},{7,5},{8,10},{9,11},{10,... | collective-permute-start | bytes 6152 | tf_op jit(solution)/shard_map/ppermute | solution.py:615
  58.5 3.6 %gram_most.1.refs_1_ = f32[1024,1024]{1,0:T(8,128)S(1)} custom-call(s32[1]{0:T(128)} %bitcast.place_ref.refs_0_.role_ref, bf16[1536,1024]{1,0:T(8,128)(2,1)S(1)} %get-tuple-element.62.left, bf16[768,1024]{1,0:T(8,128)(2,1)S(1)} %stack.4.near, bf16[768,1024]{1,0:T(8,128)(2,1)S(1)} %collective-permute-done.11.far), custom_call_target="tpu_custom_call" | custom-call | flops 99999997952 | tf_op jit(solution)/shard_map/gram_most/pallas_call | solution.py:507
  62.2 3.1 %gram_last.1 = (f32[1024,1024]{1,0:T(8,128)}, f32[1,512]{1,0:T(1,128)}) custom-call(s32[1]{0:T(128)} %bitcast.place_ref.refs_0_.role_ref, f32[1024,1024]{1,0:T(8,128)S(1)} %gram_most.1.refs_1_, bf16[512,1024]{1,0:T(8,128)(2,1)S(1)} %get-tuple-element.66.refs_2_, bf16[256,1024]{1,0:T(8,128)(2,1)S(1)} %stack.5.refs_3_, ...), custom_call_target="tpu_custom_call" | custom-call | flops 99999997952 | tf_op jit(solution)/shard_map/gram_last/pallas_call | solution.py:542
  (42 shorter events, 1.8 us)
Async XLA Ops:
  0.6 27.6 %collective-permute-start = (bf16[256,1024]{1,0:T(8,128)(2,1)}, bf16[256,1024]{1,0:T(8,128)(2,1)S(1)}, u32[]{:S(2)}, u32[]{:S(2)}) collective-permute-start(bf16[256,1024]{1,0:T(8,128)(2,1)} %refs_1_.1), channel_id=1, source_target_pairs={{0,8},{4,12},{8,0},{12,4},{1,9},{5,13},{9,1},{13,5},{2,10},{6,14},... | collective-permute-start | bytes 1572872 | tf_op jit(solution)/shard_map/ppermute | solution.py:579
  4.7 23.7 %collective-permute-start.1 = (bf16[256,1024]{1,0:T(8,128)(2,1)}, bf16[256,1024]{1,0:T(8,128)(2,1)S(1)}, u32[]{:S(2)}, u32[]{:S(2)}) collective-permute-start(bf16[256,1024]{1,0:T(8,128)(2,1)} %refs_1_.1), channel_id=1, source_target_pairs={{0,4},{4,0},{8,12},{12,8},{1,5},{5,1},{9,13},{13,9},{2,6},{6,2},{1... | collective-permute-start | bytes 1572872 | tf_op jit(solution)/shard_map/ppermute | solution.py:578
  6.3 22.1 %collective-permute-start.2 = (bf16[256,1024]{1,0:T(8,128)(2,1)}, bf16[256,1024]{1,0:T(8,128)(2,1)S(1)}, u32[]{:S(2)}, u32[]{:S(2)}) collective-permute-start(bf16[256,1024]{1,0:T(8,128)(2,1)} %refs_1_.1), channel_id=1, source_target_pairs={{0,2},{5,7},{10,8},{15,13},{16,18},{21,23},{26,24},{31,29}} | collective-permute-start | bytes 1572872 | tf_op jit(solution)/shard_map/ppermute | solution.py:575
  11.7 19.0 %copy-start = (bf16[256,1024]{1,0:T(8,128)(2,1)S(1)}, bf16[256,1024]{1,0:T(8,128)(2,1)}, u32[]{:S(2)}) copy-start(bf16[256,1024]{1,0:T(8,128)(2,1)} %refs_1_.1) | copy-start | bytes 1572868
  11.8 1.6 %collective-permute-start.3 = (bf16[512,256]{1,0:T(8,128)(2,1)S(1)}, bf16[512,256]{1,0:T(8,128)(2,1)S(1)}, u32[]{:S(2)}, u32[]{:S(2)}) collective-permute-start(bf16[512,256]{1,0:T(8,128)(2,1)S(1)} %get-tuple-element.38), channel_id=1, source_target_pairs={{0,1},{1,0},{2,3},{3,2},{4,5},{5,4},{6,7},{7,6},{8,9},{9,8},{10,11... | collective-permute-start | bytes 786440 | tf_op jit(solution)/shard_map/ppermute | solution.py:581
  11.9 10.3 %collective-permute-start.4 = (bf16[512,256]{1,0:T(8,128)(2,1)S(1)}, bf16[512,256]{1,0:T(8,128)(2,1)S(1)}, u32[]{:S(2)}, u32[]{:S(2)}) collective-permute-start(bf16[512,256]{1,0:T(8,128)(2,1)S(1)} %get-tuple-element.41), channel_id=1, source_target_pairs={{0,3},{1,2},{2,1},{3,0},{4,7},{5,6},{6,5},{7,4},{8,11},{9,10},{10,... | collective-permute-start | bytes 786440 | tf_op jit(solution)/shard_map/ppermute | solution.py:582
  13.4 17.8 %copy-start.4 = (bf16[512,256]{1,0:T(8,128)(2,1)}, bf16[512,256]{1,0:T(8,128)(2,1)S(1)}, u32[]{:S(2)}) copy-start(bf16[512,256]{1,0:T(8,128)(2,1)S(1)} %collective-permute-done.3.near_ref) | copy-start | bytes 786436
  13.4 14.9 %collective-permute-start.5 = (s32[1,256]{1,0:T(1,128)S(1)}, s32[1,256]{1,0:T(1,128)S(1)}, u32[]{:S(2)}, u32[]{:S(2)}) collective-permute-start(s32[1,256]{1,0:T(1,128)S(1)} %get-tuple-element.42.own_label.own_ref), channel_id=1, source_target_pairs={{0,8},{4,12},{8,0},{12,4},{1,9},{5,13},{9,1},{13,5},{2,10},{6,14},... | collective-permute-start | bytes 3080 | tf_op jit(solution)/shard_map/ppermute | solution.py:584
  22.2 8.4 %copy-start.6 = (bf16[512,256]{1,0:T(8,128)(2,1)}, bf16[512,256]{1,0:T(8,128)(2,1)S(1)}, u32[]{:S(2)}) copy-start(bf16[512,256]{1,0:T(8,128)(2,1)S(1)} %collective-permute-done.4.far_ref) | copy-start | bytes 786436
  28.5 9.7 %collective-permute-start.6 = (bf16[272,512]{1,0:T(8,128)(2,1)S(1)}, bf16[272,512]{1,0:T(8,128)(2,1)S(1)}, u32[]{:S(2)}, u32[]{:S(2)}) collective-permute-start(bf16[272,512]{1,0:T(8,128)(2,1)S(1)} %get-tuple-element.49), channel_id=1, source_target_pairs={{0,4},{4,0},{8,12},{12,8},{1,5},{5,1},{9,13},{13,9},{2,6},{6,2},{1... | collective-permute-start | bytes 835592 | tf_op jit(solution)/shard_map/ppermute | solution.py:589
  30.1 11.7 %collective-permute-start.7 = (bf16[256,512]{1,0:T(8,128)(2,1)S(1)}, bf16[256,512]{1,0:T(8,128)(2,1)S(1)}, u32[]{:S(2)}, u32[]{:S(2)}) collective-permute-start(bf16[256,512]{1,0:T(8,128)(2,1)S(1)} %get-tuple-element.50), channel_id=1, source_target_pairs={{0,4},{4,0},{8,12},{12,8},{1,5},{5,1},{9,13},{13,9},{2,6},{6,2},{1... | collective-permute-start | bytes 786440 | tf_op jit(solution)/shard_map/ppermute | solution.py:590
  31.3 18.3 %collective-permute-start.10 = (bf16[512,1024]{1,0:T(8,128)(2,1)S(1)}, bf16[512,1024]{1,0:T(8,128)(2,1)S(1)}, u32[]{:S(2)}, u32[]{:S(2)}) collective-permute-start(bf16[512,1024]{1,0:T(8,128)(2,1)S(1)} %stack.3), channel_id=1, source_target_pairs={{0,2},{5,7},{10,8},{15,13},{16,18},{21,23},{26,24},{31,29}} | collective-permute-start | bytes 3145736 | tf_op jit(solution)/shard_map/ppermute | solution.py:575
  38.9 11.0 %collective-permute-start.8 = (f32[256,256]{1,0:T(8,128)S(1)}, f32[256,256]{1,0:T(8,128)S(1)}, u32[]{:S(2)}, u32[]{:S(2)}) collective-permute-start(f32[256,256]{1,0:T(8,128)S(1)} %get-tuple-element.51), channel_id=1, source_target_pairs={{0,1},{1,0},{2,3},{3,2},{4,5},{5,4},{6,7},{7,6},{8,9},{9,8},{10,11... | collective-permute-start | bytes 786440 | tf_op jit(solution)/shard_map/ppermute | solution.py:596
  41.8 8.1 %collective-permute-start.9 = (f32[256,256]{1,0:T(8,128)S(1)}, f32[256,256]{1,0:T(8,128)S(1)}, u32[]{:S(2)}, u32[]{:S(2)}) collective-permute-start(f32[256,256]{1,0:T(8,128)S(1)} %get-tuple-element.59), channel_id=1, source_target_pairs={{1,2},{2,1},{5,6},{6,5},{9,10},{10,9},{13,14},{14,13},{17,18},{18,... | collective-permute-start | bytes 786440 | tf_op jit(solution)/shard_map/ppermute | solution.py:597
  43.1 15.2 %collective-permute-start.13 = (bf16[256,1024]{1,0:T(8,128)(2,1)S(1)}, bf16[256,1024]{1,0:T(8,128)(2,1)S(1)}, u32[]{:S(2)}, u32[]{:S(2)}) collective-permute-start(bf16[256,1024]{1,0:T(8,128)(2,1)S(1)} %get-tuple-element.55.refs_3_.refs_1_), channel_id=1, source_target_pairs={{0,2},{5,7},{10,8},{15,13},{16,18},{21,23},{26,24},{31,29}} | collective-permute-start | bytes 1572872 | tf_op jit(solution)/shard_map/ppermute | solution.py:575
  49.6 1.7 %copy-start.3 = (bf16[512,1024]{1,0:T(8,128)(2,1)S(1)}, bf16[512,1024]{1,0:T(8,128)(2,1)}, u32[]{:S(2)}) copy-start(bf16[512,1024]{1,0:T(8,128)(2,1)} %held_ref.3) | copy-start | bytes 3145732
  49.6 1.7 %copy-start.5 = (bf16[512,256]{1,0:T(8,128)(2,1)S(1)}, bf16[512,256]{1,0:T(8,128)(2,1)}, u32[]{:S(2)}) copy-start(bf16[512,256]{1,0:T(8,128)(2,1)} %copy-done.4) | copy-start | bytes 786436
  49.6 1.8 %copy-start.7 = (bf16[512,256]{1,0:T(8,128)(2,1)S(1)}, bf16[512,256]{1,0:T(8,128)(2,1)}, u32[]{:S(2)}) copy-start(bf16[512,256]{1,0:T(8,128)(2,1)} %copy-done.6) | copy-start | bytes 786436
  49.6 1.8 %copy-start.8 = (s32[512]{0:T(512)S(1)}, s32[512]{0:T(512)}, u32[]{:S(2)}) copy-start(s32[512]{0:T(512)} %param.8) | copy-start | bytes 6148
  49.8 8.7 %collective-permute-start.11 = (bf16[768,1024]{1,0:T(8,128)(2,1)S(1)}, bf16[768,1024]{1,0:T(8,128)(2,1)S(1)}, u32[]{:S(2)}, u32[]{:S(2)}) collective-permute-start(bf16[768,1024]{1,0:T(8,128)(2,1)S(1)} %stack.4.near), channel_id=1, source_target_pairs={{0,1},{1,0},{2,3},{3,2},{4,5},{5,4},{6,7},{7,6},{8,9},{9,8},{10,11... | collective-permute-start | bytes 4718600 | tf_op jit(solution)/shard_map/ppermute | solution.py:603
  55.9 2.4 %collective-permute-start.12 = (f32[1,512]{1,0:T(1,128)S(1)}, f32[1,512]{1,0:T(1,128)S(1)}, u32[]{:S(2)}, u32[]{:S(2)}) collective-permute-start(f32[1,512]{1,0:T(1,128)S(1)} %get-tuple-element.67.refs_5_), channel_id=1, source_target_pairs={{0,1},{1,0},{2,3},{3,2},{4,5},{5,4},{6,7},{7,6},{8,9},{9,8},{10,11... | collective-permute-start | bytes 6152 | tf_op jit(solution)/shard_map/ppermute | solution.py:611
  55.9 6.3 %collective-permute-start.15 = (f32[1,512]{1,0:T(1,128)S(1)}, f32[1,512]{1,0:T(1,128)S(1)}, u32[]{:S(2)}, u32[]{:S(2)}) collective-permute-start(f32[1,512]{1,0:T(1,128)S(1)} %get-tuple-element.67.refs_5_), channel_id=1, source_target_pairs={{0,2},{1,3},{2,0},{3,1},{4,6},{5,7},{6,4},{7,5},{8,10},{9,11},{10,... | collective-permute-start | bytes 6152 | tf_op jit(solution)/shard_map/ppermute | solution.py:615
  58.2 4.0 %collective-permute-start.16 = (f32[1,512]{1,0:T(1,128)S(1)}, f32[1,512]{1,0:T(1,128)S(1)}, u32[]{:S(2)}, u32[]{:S(2)}) collective-permute-start(f32[1,512]{1,0:T(1,128)S(1)} %get-tuple-element.67.refs_5_), channel_id=1, source_target_pairs={{0,3},{1,2},{2,1},{3,0},{4,7},{5,6},{6,5},{7,4},{8,11},{9,10},{10,... | collective-permute-start | bytes 6152 | tf_op jit(solution)/shard_map/ppermute | solution.py:615
  58.4 3.8 %collective-permute-start.14 = (bf16[256,1024]{1,0:T(8,128)(2,1)S(1)}, bf16[256,1024]{1,0:T(8,128)(2,1)S(1)}, u32[]{:S(2)}, u32[]{:S(2)}) collective-permute-start(bf16[256,1024]{1,0:T(8,128)(2,1)S(1)} %stack.5.refs_3_), channel_id=1, source_target_pairs={{0,1},{1,0},{2,3},{3,2},{4,5},{5,4},{6,7},{7,6},{8,9},{9,8},{10,11... | collective-permute-start | bytes 1572872 | tf_op jit(solution)/shard_map/ppermute | solution.py:614
  (3 other events, 3.3 us)

commit v6 on v5

--- a/solution.py
+++ b/solution.py
@@ -297,7 +297,7 @@
             pltpu.SemaphoreType.DMA((5,)),
         ],
         compiler_params=SMALL,
-        cost_estimate=cost(1),
+        cost_estimate=cost(LONG),
         name="edge_means",
     )(place, own_labels, next_labels, early, third, outer)
 
@@ -347,7 +347,7 @@
             pltpu.SemaphoreType.DMA((5,)),
         ],
         compiler_params=MIDDLE,
-        cost_estimate=cost(LONG),
+        cost_estimate=cost(10**9),
         name="class_means",
     )(own_labels, next_labels, early, third, outer, inner)
 
@@ -384,11 +384,27 @@
     )(role, *own, *other)
 
 
+def bands_kernel(precision, bands, sem):
+    wait(fetch(sem, *[(precision.at[k], bands.at[:, pl.ds(k * BLK, BLK)]) for k in range(3)]))
+
+
+def bands_beside(precision):
+    width = precision.shape[1]
+    return pl.pallas_call(
+        bands_kernel,
+        out_shape=jax.ShapeDtypeStruct((width, 3 * BLK), BF16),
+        in_specs=[HBM],
+        out_specs=VMEM,
+        scratch_shapes=[pltpu.SemaphoreType.DMA((3,))],
+        compiler_params=SMALL,
+        cost_estimate=cost(1),
+        name="bands_beside",
+    )(precision)
+
+
 def white_kernel(place_ref, held_ref, near_ref, far_ref, means_ref, near_means, far_means,
-                 held_labels, precision, white_ref, score_ref, bands, held, means):
+                 held_labels, bands, white_ref, score_ref, held, means):
     width = held_ref.shape[1]
-    for k in range(3):
-        bands[:, k * BLK : (k + 1) * BLK] = precision[k]
     held[:, BLK : BLK + width] = held_ref[...]
     means[:, BLK : BLK + width] = means_ref[...]
     sides = (slice(0, BLK), slice(BLK + width, 2 * BLK + width))
@@ -437,7 +453,6 @@
         in_specs=[SMEM] + [VMEM] * 8,
         out_specs=(VMEM, VMEM),
         scratch_shapes=[
-            pltpu.VMEM((width, 3 * BLK), BF16),
             pltpu.VMEM((count, width + 2 * BLK), BF16),
             pltpu.VMEM((C, width + 2 * BLK), F32),
         ],
@@ -595,7 +610,7 @@
     near_edge, far_edge = edge_means(role, own_labels, next_labels, early, third, outer)
     near_means = lax.ppermute(near_edge, "feat", flip[1])
     far_means = lax.ppermute(far_edge, "feat", inward)
-    inner, near_edge = tie((inner, near_edge))
+    inner, near_edge, bands = tie((inner, near_edge, bands_beside(precision)))
     means, fourth, labels = class_means(own_labels, next_labels, early, third, outer, inner)
     across_last = hop(fourth, (0, 2))
     rows = [train_rows, second, third, fourth]
@@ -604,7 +619,7 @@
     most, last = centre(labels, means, rows)
     most, last, means = tie((most, last, means))
     white, score = whiten(
-        role, held_rows, near, far, means, near_means, far_means, held_labels.reshape(1, -1), precision
+        role, held_rows, near, far, means, near_means, far_means, held_labels.reshape(1, -1), bands
     )
     score, most = tie((score, most))
     total = gram_most(role, most, near_most, far_most)

time: 65.5 us -> 65.1 us (level)
  local copies, waits for them, and re-layouts: 3.41 us -> 1.94 us
  waiting for transfers between devices: 22.7 us -> 23.9 us
    ppermute x3, waiting for transfers between devices: 0.01 us -> 2.29 us  [hop(): return lax.ppermute(array, ('dp', 'feat'), pairs)]
    unnamed x20, local copies, waits for them, and re-layouts: 3.41 us -> 1.94 us
    ppermute x3, starting transfers between devices: 11.4 us -> 10.4 us  [hop(): return lax.ppermute(array, ('dp', 'feat'), pairs)]
    ppermute x1, waiting for transfers between devices: 2.84 us -> 2 us  [four_by_four(): inner = lax.ppermute(second_inner, 'dp', flip[1])]
  transfers between devices with their start and end apart: 17 -> 17, of which waited for: 6 -> 7; matrix products, arithmetic and copies ran while one was open for 0% -> 0% of each run, Pallas kernels for 19% -> 19%
where the time goes in v6:
time: 65.1 us; the launch traced here: 64.8 us
  waiting for transfers between devices  23.9 us (37%)
  starting transfers between devices  22.3 us (34%)
  Pallas kernels  15.7 us (24%)
  local copies, waits for them, and re-layouts  1.94 us (3%)
  between operations  0.96 us (1%)
    ppermute x3, starting transfers between devices, hop(): return lax.ppermute(array, ('dp', 'feat'), pairs)  10.4 us
    ppermute x1, waiting for transfers between devices, four_by_four(): far = lax.ppermute(far, 'feat', flip[3])  8.82 us
    ppermute x1, waiting for transfers between devices, four_by_four(): next_labels = lax.ppermute(own_labels, 'dp', flip[2])  6.06 us
    pallas_call x1, Pallas kernels, whiten(): pl.pallas_call(white_kernel, out_shape=(jax.ShapeDtypeStruct((count, widt...  4.47 us
    ppermute x1, starting transfers between devices, four_by_four(): second = lax.ppermute(train_rows, 'dp', flip[2])  4.1 us
    pallas_call x1, Pallas kernels, gram_most(): pl.pallas_call(most_kernel, out_shape=jax.ShapeDtypeStruct((width, width)...  3.62 us
    ppermute x1, waiting for transfers between devices, four_by_four(): outer = lax.ppermute(second_outer, 'dp', flip[1])  3.15 us
    pallas_call x1, Pallas kernels, gram_last(): pl.pallas_call(lambda *refs: last_kernel(scale, features, *refs), out_sha...  3.07 us
  transfers between devices with their start and end apart: 17, of which 7 were waited for; matrix products, arithmetic and copies ran while one was open for 0% of the time, Pallas kernels for 19%

profile of v6, /device:TPU:0, one launch (start us, length us, event | category | flops | bytes accessed | tf_op | source)
XLA Modules:
  0.0 64.8 jit_solution(538992023681434046)
XLA Ops:
  0.6 4.1 %collective-permute-start = (bf16[256,1024]{1,0:T(8,128)(2,1)}, bf16[256,1024]{1,0:T(8,128)(2,1)S(1)}, u32[]{:S(2)}, u32[]{:S(2)}) collective-permute-start(bf16[256,1024]{1,0:T(8,128)(2,1)} %refs_1_.1), channel_id=1, source_target_pairs={{0,8},{4,12},{8,0},{12,4},{1,9},{5,13},{9,1},{13,5},{2,10},{6,14},... | collective-permute-start | bytes 1572872 | tf_op jit(solution)/shard_map/ppermute | solution.py:594
  4.7 1.6 %collective-permute-start.1 = (bf16[256,1024]{1,0:T(8,128)(2,1)}, bf16[256,1024]{1,0:T(8,128)(2,1)S(1)}, u32[]{:S(2)}, u32[]{:S(2)}) collective-permute-start(bf16[256,1024]{1,0:T(8,128)(2,1)} %refs_1_.1), channel_id=1, source_target_pairs={{0,4},{4,0},{8,12},{12,8},{1,5},{5,1},{9,13},{13,9},{2,6},{6,2},{1... | collective-permute-start | bytes 1572872 | tf_op jit(solution)/shard_map/ppermute | solution.py:593
  6.3 3.4 %collective-permute-start.2 = (bf16[256,1024]{1,0:T(8,128)(2,1)}, bf16[256,1024]{1,0:T(8,128)(2,1)S(1)}, u32[]{:S(2)}, u32[]{:S(2)}) collective-permute-start(bf16[256,1024]{1,0:T(8,128)(2,1)} %refs_1_.1), channel_id=1, source_target_pairs={{0,2},{5,7},{10,8},{15,13},{16,18},{21,23},{26,24},{31,29}} | collective-permute-start | bytes 1572872 | tf_op jit(solution)/shard_map/ppermute | solution.py:590
  9.8 1.2 %copy-done.2 = bf16[512,1024]{1,0:T(8,128)(2,1)S(1)} copy-done((bf16[512,1024]{1,0:T(8,128)(2,1)S(1)}, bf16[512,1024]{1,0:T(8,128)(2,1)}, u32[]{:S(2)}) %copy-start.2) | copy-done | bytes 1048600
  11.0 0.7 %copy-done.9 = s32[256,1]{0,1:T(1,128)S(1)} copy-done((s32[256,1]{0,1:T(1,128)S(1)}, s32[256,1]{0,1:T(1,128)}, u32[]{:S(2)}) %copy-start.9) | copy-done | bytes 1048
  11.9 1.4 %collective-permute-done.3.near_ref = bf16[512,256]{1,0:T(8,128)(2,1)S(1)} collective-permute-done((bf16[512,256]{1,0:T(8,128)(2,1)S(1)}, bf16[512,256]{1,0:T(8,128)(2,1)S(1)}, u32[]{:S(2)}, u32[]{:S(2)}) %collective-permute-start.3) | collective-permute-done | bytes 262176 | tf_op jit(solution)/shard_map/ppermute | solution.py:596
  13.4 8.8 %collective-permute-done.4.far_ref = bf16[512,256]{1,0:T(8,128)(2,1)S(1)} collective-permute-done((bf16[512,256]{1,0:T(8,128)(2,1)S(1)}, bf16[512,256]{1,0:T(8,128)(2,1)S(1)}, u32[]{:S(2)}, u32[]{:S(2)}) %collective-permute-start.4) | collective-permute-done | bytes 262176 | tf_op jit(solution)/shard_map/ppermute | solution.py:597
  22.2 6.1 %collective-permute-done.5.next_label.next_ref = s32[1,256]{1,0:T(1,128)S(1)} collective-permute-done((s32[1,256]{1,0:T(1,128)S(1)}, s32[1,256]{1,0:T(1,128)S(1)}, u32[]{:S(2)}, u32[]{:S(2)}) %collective-permute-start.5) | collective-permute-done | bytes 1056 | tf_op jit(solution)/shard_map/ppermute | solution.py:599
  28.5 1.5 %collective-permute-start.6 = (bf16[272,512]{1,0:T(8,128)(2,1)S(1)}, bf16[272,512]{1,0:T(8,128)(2,1)S(1)}, u32[]{:S(2)}, u32[]{:S(2)}) collective-permute-start(bf16[272,512]{1,0:T(8,128)(2,1)S(1)} %get-tuple-element.50), channel_id=1, source_target_pairs={{0,4},{4,0},{8,12},{12,8},{1,5},{5,1},{9,13},{13,9},{2,6},{6,2},{1... | collective-permute-start | bytes 835592 | tf_op jit(solution)/shard_map/ppermute | solution.py:604
  30.1 0.6 early_sums.1.early_ref
  30.7 0.6 collective-permute-start.7
  31.4 3.6 %collective-permute-start.10 = (bf16[512,1024]{1,0:T(8,128)(2,1)S(1)}, bf16[512,1024]{1,0:T(8,128)(2,1)S(1)}, u32[]{:S(2)}, u32[]{:S(2)}) collective-permute-start(bf16[512,1024]{1,0:T(8,128)(2,1)S(1)} %stack.3), channel_id=1, source_target_pairs={{0,2},{5,7},{10,8},{15,13},{16,18},{21,23},{26,24},{31,29}} | collective-permute-start | bytes 3145736 | tf_op jit(solution)/shard_map/ppermute | solution.py:590
  35.1 3.2 %collective-permute-done.6.outer_ref = bf16[272,512]{1,0:T(8,128)(2,1)S(1)} collective-permute-done((bf16[272,512]{1,0:T(8,128)(2,1)S(1)}, bf16[272,512]{1,0:T(8,128)(2,1)S(1)}, u32[]{:S(2)}, u32[]{:S(2)}) %collective-permute-start.6) | collective-permute-done | bytes 278560 | tf_op jit(solution)/shard_map/ppermute | solution.py:604
  38.2 0.7 %edge_means.1 = (f32[256,256]{1,0:T(8,128)S(1)}, f32[256,256]{1,0:T(8,128)S(1)}) custom-call(s32[1]{0:T(128)} %bitcast.place_ref.refs_0_.role_ref, s32[1,256]{1,0:T(1,128)S(1)} %get-tuple-element.43.own_label.own_ref, s32[1,256]{1,0:T(1,128)S(1)} %collective-permute-done.5.next_label.next_ref, f32[256,1024]{1,0:T(8,128)S(1)} %early_sums.1.early_ref, ...), custom_call_target="tpu_custom_call" | custom-call | flops 99999997952 | tf_op jit(solution)/shard_map/edge_means/pallas_call | solution.py:288
  39.0 0.7 %collective-permute-start.9 = (f32[256,256]{1,0:T(8,128)S(1)}, f32[256,256]{1,0:T(8,128)S(1)}, u32[]{:S(2)}, u32[]{:S(2)}) collective-permute-start(f32[256,256]{1,0:T(8,128)S(1)} %get-tuple-element.60), channel_id=1, source_target_pairs={{1,2},{2,1},{5,6},{6,5},{9,10},{10,9},{13,14},{14,13},{17,18},{18,... | collective-permute-start | bytes 786440 | tf_op jit(solution)/shard_map/ppermute | solution.py:612
  39.8 2.0 %collective-permute-done.7.inner_ref = bf16[256,512]{1,0:T(8,128)(2,1)S(1)} collective-permute-done((bf16[256,512]{1,0:T(8,128)(2,1)S(1)}, bf16[256,512]{1,0:T(8,128)(2,1)S(1)}, u32[]{:S(2)}, u32[]{:S(2)}) %collective-permute-start.7) | collective-permute-done | bytes 262176 | tf_op jit(solution)/shard_map/ppermute | solution.py:605
  41.8 0.6 class_means.1
  42.4 3.3 %collective-permute-start.13 = (bf16[256,1024]{1,0:T(8,128)(2,1)S(1)}, bf16[256,1024]{1,0:T(8,128)(2,1)S(1)}, u32[]{:S(2)}, u32[]{:S(2)}) collective-permute-start(bf16[256,1024]{1,0:T(8,128)(2,1)S(1)} %get-tuple-element.56.refs_3_.refs_1_), channel_id=1, source_target_pairs={{0,2},{5,7},{10,8},{15,13},{16,18},{21,23},{26,24},{31,29}} | collective-permute-start | bytes 1572872 | tf_op jit(solution)/shard_map/ppermute | solution.py:590
  45.8 2.0 %centre.1 = (bf16[1536,1024]{1,0:T(8,128)(2,1)S(1)}, bf16[512,1024]{1,0:T(8,128)(2,1)S(1)}) custom-call(f32[4,256]{1,0:T(4,128)S(1)} %get-tuple-element.54.labels_ref, f32[256,1024]{1,0:T(8,128)S(1)} %get-tuple-element.59.means_ref, bf16[256,1024]{1,0:T(8,128)(2,1)S(1)} %copy-done, ...), custom_call_target="tpu_custom_call" | custom-call | flops 1 | tf_op jit(solution)/shard_map/centre/pallas_call | solution.py:498
  47.8 2.3 %collective-permute-done.10.refs_5_ = bf16[512,1024]{1,0:T(8,128)(2,1)S(1)} collective-permute-done((bf16[512,1024]{1,0:T(8,128)(2,1)S(1)}, bf16[512,1024]{1,0:T(8,128)(2,1)S(1)}, u32[]{:S(2)}, u32[]{:S(2)}) %collective-permute-start.10) | collective-permute-done | bytes 1048608 | tf_op jit(solution)/shard_map/ppermute | solution.py:590
  50.4 4.5 %whiten.1 = (bf16[512,1024]{1,0:T(8,128)(2,1)}, f32[1,512]{1,0:T(1,128)S(1)}) custom-call(s32[1]{0:T(128)} %bitcast.place_ref.refs_0_.role_ref, bf16[512,1024]{1,0:T(8,128)(2,1)S(1)} %copy-done.3, bf16[512,256]{1,0:T(8,128)(2,1)S(1)} %copy-done.5, bf16[512,256]{1,0:T(8,128)(2,1)S(1)} %copy-done.7, f32[256,1024]{1,0:T(8,128)S(1)} %get-tuple-element.59.means_ref, ...), custom_call_target="tpu_custom_call" | custom-call | flops 99999997952 | tf_op jit(solution)/shard_map/whiten/pallas_call | solution.py:447
  55.3 2.5 %collective-permute-start.15 = (f32[1,512]{1,0:T(1,128)S(1)}, f32[1,512]{1,0:T(1,128)S(1)}, u32[]{:S(2)}, u32[]{:S(2)}) collective-permute-start(f32[1,512]{1,0:T(1,128)S(1)} %get-tuple-element.69.refs_5_), channel_id=1, source_target_pairs={{0,2},{1,3},{2,0},{3,1},{4,6},{5,7},{6,4},{7,5},{8,10},{9,11},{10,... | collective-permute-start | bytes 6152 | tf_op jit(solution)/shard_map/ppermute | solution.py:630
  58.1 3.6 %gram_most.1.refs_1_ = f32[1024,1024]{1,0:T(8,128)S(1)} custom-call(s32[1]{0:T(128)} %bitcast.place_ref.refs_0_.role_ref, bf16[1536,1024]{1,0:T(8,128)(2,1)S(1)} %get-tuple-element.64.left, bf16[768,1024]{1,0:T(8,128)(2,1)S(1)} %stack.4.near, bf16[768,1024]{1,0:T(8,128)(2,1)S(1)} %collective-permute-done.11.far), custom_call_target="tpu_custom_call" | custom-call | flops 99999997952 | tf_op jit(solution)/shard_map/gram_most/pallas_call | solution.py:522
  61.7 3.1 %gram_last.1 = (f32[1024,1024]{1,0:T(8,128)}, f32[1,512]{1,0:T(1,128)}) custom-call(s32[1]{0:T(128)} %bitcast.place_ref.refs_0_.role_ref, f32[1024,1024]{1,0:T(8,128)S(1)} %gram_most.1.refs_1_, bf16[512,1024]{1,0:T(8,128)(2,1)S(1)} %get-tuple-element.68.refs_2_, bf16[256,1024]{1,0:T(8,128)(2,1)S(1)} %stack.5.refs_3_, ...), custom_call_target="tpu_custom_call" | custom-call | flops 99999997952 | tf_op jit(solution)/shard_map/gram_last/pallas_call | solution.py:557
  (43 shorter events, 1.9 us)
Async XLA Ops:
  0.6 27.6 %collective-permute-start = (bf16[256,1024]{1,0:T(8,128)(2,1)}, bf16[256,1024]{1,0:T(8,128)(2,1)S(1)}, u32[]{:S(2)}, u32[]{:S(2)}) collective-permute-start(bf16[256,1024]{1,0:T(8,128)(2,1)} %refs_1_.1), channel_id=1, source_target_pairs={{0,8},{4,12},{8,0},{12,4},{1,9},{5,13},{9,1},{13,5},{2,10},{6,14},... | collective-permute-start | bytes 1572872 | tf_op jit(solution)/shard_map/ppermute | solution.py:594
  4.7 23.7 %collective-permute-start.1 = (bf16[256,1024]{1,0:T(8,128)(2,1)}, bf16[256,1024]{1,0:T(8,128)(2,1)S(1)}, u32[]{:S(2)}, u32[]{:S(2)}) collective-permute-start(bf16[256,1024]{1,0:T(8,128)(2,1)} %refs_1_.1), channel_id=1, source_target_pairs={{0,4},{4,0},{8,12},{12,8},{1,5},{5,1},{9,13},{13,9},{2,6},{6,2},{1... | collective-permute-start | bytes 1572872 | tf_op jit(solution)/shard_map/ppermute | solution.py:593
  6.3 22.1 %collective-permute-start.2 = (bf16[256,1024]{1,0:T(8,128)(2,1)}, bf16[256,1024]{1,0:T(8,128)(2,1)S(1)}, u32[]{:S(2)}, u32[]{:S(2)}) collective-permute-start(bf16[256,1024]{1,0:T(8,128)(2,1)} %refs_1_.1), channel_id=1, source_target_pairs={{0,2},{5,7},{10,8},{15,13},{16,18},{21,23},{26,24},{31,29}} | collective-permute-start | bytes 1572872 | tf_op jit(solution)/shard_map/ppermute | solution.py:590
  11.7 18.4 %copy-start = (bf16[256,1024]{1,0:T(8,128)(2,1)S(1)}, bf16[256,1024]{1,0:T(8,128)(2,1)}, u32[]{:S(2)}) copy-start(bf16[256,1024]{1,0:T(8,128)(2,1)} %refs_1_.1) | copy-start | bytes 1572868
  11.8 1.6 %collective-permute-start.3 = (bf16[512,256]{1,0:T(8,128)(2,1)S(1)}, bf16[512,256]{1,0:T(8,128)(2,1)S(1)}, u32[]{:S(2)}, u32[]{:S(2)}) collective-permute-start(bf16[512,256]{1,0:T(8,128)(2,1)S(1)} %get-tuple-element.39), channel_id=1, source_target_pairs={{0,1},{1,0},{2,3},{3,2},{4,5},{5,4},{6,7},{7,6},{8,9},{9,8},{10,11... | collective-permute-start | bytes 786440 | tf_op jit(solution)/shard_map/ppermute | solution.py:596
  11.9 10.3 %collective-permute-start.4 = (bf16[512,256]{1,0:T(8,128)(2,1)S(1)}, bf16[512,256]{1,0:T(8,128)(2,1)S(1)}, u32[]{:S(2)}, u32[]{:S(2)}) collective-permute-start(bf16[512,256]{1,0:T(8,128)(2,1)S(1)} %get-tuple-element.42), channel_id=1, source_target_pairs={{0,3},{1,2},{2,1},{3,0},{4,7},{5,6},{6,5},{7,4},{8,11},{9,10},{10,... | collective-permute-start | bytes 786440 | tf_op jit(solution)/shard_map/ppermute | solution.py:597
  13.4 17.3 %copy-start.4 = (bf16[512,256]{1,0:T(8,128)(2,1)}, bf16[512,256]{1,0:T(8,128)(2,1)S(1)}, u32[]{:S(2)}) copy-start(bf16[512,256]{1,0:T(8,128)(2,1)S(1)} %collective-permute-done.3.near_ref) | copy-start | bytes 786436
  13.4 14.9 %collective-permute-start.5 = (s32[1,256]{1,0:T(1,128)S(1)}, s32[1,256]{1,0:T(1,128)S(1)}, u32[]{:S(2)}, u32[]{:S(2)}) collective-permute-start(s32[1,256]{1,0:T(1,128)S(1)} %get-tuple-element.43.own_label.own_ref), channel_id=1, source_target_pairs={{0,8},{4,12},{8,0},{12,4},{1,9},{5,13},{9,1},{13,5},{2,10},{6,14},... | collective-permute-start | bytes 3080 | tf_op jit(solution)/shard_map/ppermute | solution.py:599
  22.2 8.5 %copy-start.6 = (bf16[512,256]{1,0:T(8,128)(2,1)}, bf16[512,256]{1,0:T(8,128)(2,1)S(1)}, u32[]{:S(2)}) copy-start(bf16[512,256]{1,0:T(8,128)(2,1)S(1)} %collective-permute-done.4.far_ref) | copy-start | bytes 786436
  28.5 9.7 %collective-permute-start.6 = (bf16[272,512]{1,0:T(8,128)(2,1)S(1)}, bf16[272,512]{1,0:T(8,128)(2,1)S(1)}, u32[]{:S(2)}, u32[]{:S(2)}) collective-permute-start(bf16[272,512]{1,0:T(8,128)(2,1)S(1)} %get-tuple-element.50), channel_id=1, source_target_pairs={{0,4},{4,0},{8,12},{12,8},{1,5},{5,1},{9,13},{13,9},{2,6},{6,2},{1... | collective-permute-start | bytes 835592 | tf_op jit(solution)/shard_map/ppermute | solution.py:604
  30.7 11.2 %collective-permute-start.7 = (bf16[256,512]{1,0:T(8,128)(2,1)S(1)}, bf16[256,512]{1,0:T(8,128)(2,1)S(1)}, u32[]{:S(2)}, u32[]{:S(2)}) collective-permute-start(bf16[256,512]{1,0:T(8,128)(2,1)S(1)} %get-tuple-element.51), channel_id=1, source_target_pairs={{0,4},{4,0},{8,12},{12,8},{1,5},{5,1},{9,13},{13,9},{2,6},{6,2},{1... | collective-permute-start | bytes 786440 | tf_op jit(solution)/shard_map/ppermute | solution.py:605
  31.4 8.3 %copy-start.1 = (bf16[3,1024,256]{2,1,0:T(8,128)(2,1)S(1)}, bf16[3,1024,256]{2,1,0:T(8,128)(2,1)}, u32[]{:S(2)}) copy-start(bf16[3,1024,256]{2,1,0:T(8,128)(2,1)} %precision.1) | copy-start | bytes 4718596
  31.4 18.7 %collective-permute-start.10 = (bf16[512,1024]{1,0:T(8,128)(2,1)S(1)}, bf16[512,1024]{1,0:T(8,128)(2,1)S(1)}, u32[]{:S(2)}, u32[]{:S(2)}) collective-permute-start(bf16[512,1024]{1,0:T(8,128)(2,1)S(1)} %stack.3), channel_id=1, source_target_pairs={{0,2},{5,7},{10,8},{15,13},{16,18},{21,23},{26,24},{31,29}} | collective-permute-start | bytes 3145736 | tf_op jit(solution)/shard_map/ppermute | solution.py:590
  38.9 11.4 %collective-permute-start.8 = (f32[256,256]{1,0:T(8,128)S(1)}, f32[256,256]{1,0:T(8,128)S(1)}, u32[]{:S(2)}, u32[]{:S(2)}) collective-permute-start(f32[256,256]{1,0:T(8,128)S(1)} %get-tuple-element.52), channel_id=1, source_target_pairs={{0,1},{1,0},{2,3},{3,2},{4,5},{5,4},{6,7},{7,6},{8,9},{9,8},{10,11... | collective-permute-start | bytes 786440 | tf_op jit(solution)/shard_map/ppermute | solution.py:611
  39.0 11.4 %collective-permute-start.9 = (f32[256,256]{1,0:T(8,128)S(1)}, f32[256,256]{1,0:T(8,128)S(1)}, u32[]{:S(2)}, u32[]{:S(2)}) collective-permute-start(f32[256,256]{1,0:T(8,128)S(1)} %get-tuple-element.60), channel_id=1, source_target_pairs={{1,2},{2,1},{5,6},{6,5},{9,10},{10,9},{13,14},{14,13},{17,18},{18,... | collective-permute-start | bytes 786440 | tf_op jit(solution)/shard_map/ppermute | solution.py:612
  42.4 15.4 %collective-permute-start.13 = (bf16[256,1024]{1,0:T(8,128)(2,1)S(1)}, bf16[256,1024]{1,0:T(8,128)(2,1)S(1)}, u32[]{:S(2)}, u32[]{:S(2)}) collective-permute-start(bf16[256,1024]{1,0:T(8,128)(2,1)S(1)} %get-tuple-element.56.refs_3_.refs_1_), channel_id=1, source_target_pairs={{0,2},{5,7},{10,8},{15,13},{16,18},{21,23},{26,24},{31,29}} | collective-permute-start | bytes 1572872 | tf_op jit(solution)/shard_map/ppermute | solution.py:590
  47.8 2.6 %copy-start.3 = (bf16[512,1024]{1,0:T(8,128)(2,1)S(1)}, bf16[512,1024]{1,0:T(8,128)(2,1)}, u32[]{:S(2)}) copy-start(bf16[512,1024]{1,0:T(8,128)(2,1)} %held_ref.3) | copy-start | bytes 3145732
  47.8 2.6 %copy-start.5 = (bf16[512,256]{1,0:T(8,128)(2,1)S(1)}, bf16[512,256]{1,0:T(8,128)(2,1)}, u32[]{:S(2)}) copy-start(bf16[512,256]{1,0:T(8,128)(2,1)} %copy-done.4) | copy-start | bytes 786436
  47.8 2.6 %copy-start.7 = (bf16[512,256]{1,0:T(8,128)(2,1)S(1)}, bf16[512,256]{1,0:T(8,128)(2,1)}, u32[]{:S(2)}) copy-start(bf16[512,256]{1,0:T(8,128)(2,1)} %copy-done.6) | copy-start | bytes 786436
  50.2 7.8 %collective-permute-start.11 = (bf16[768,1024]{1,0:T(8,128)(2,1)S(1)}, bf16[768,1024]{1,0:T(8,128)(2,1)S(1)}, u32[]{:S(2)}, u32[]{:S(2)}) collective-permute-start(bf16[768,1024]{1,0:T(8,128)(2,1)S(1)} %stack.4.near), channel_id=1, source_target_pairs={{0,1},{1,0},{2,3},{3,2},{4,5},{5,4},{6,7},{7,6},{8,9},{9,8},{10,11... | collective-permute-start | bytes 4718600 | tf_op jit(solution)/shard_map/ppermute | solution.py:618
  54.9 3.0 %collective-permute-start.12 = (f32[1,512]{1,0:T(1,128)S(1)}, f32[1,512]{1,0:T(1,128)S(1)}, u32[]{:S(2)}, u32[]{:S(2)}) collective-permute-start(f32[1,512]{1,0:T(1,128)S(1)} %get-tuple-element.69.refs_5_), channel_id=1, source_target_pairs={{0,1},{1,0},{2,3},{3,2},{4,5},{5,4},{6,7},{7,6},{8,9},{9,8},{10,11... | collective-permute-start | bytes 6152 | tf_op jit(solution)/shard_map/ppermute | solution.py:626
  55.3 6.4 %collective-permute-start.15 = (f32[1,512]{1,0:T(1,128)S(1)}, f32[1,512]{1,0:T(1,128)S(1)}, u32[]{:S(2)}, u32[]{:S(2)}) collective-permute-start(f32[1,512]{1,0:T(1,128)S(1)} %get-tuple-element.69.refs_5_), channel_id=1, source_target_pairs={{0,2},{1,3},{2,0},{3,1},{4,6},{5,7},{6,4},{7,5},{8,10},{9,11},{10,... | collective-permute-start | bytes 6152 | tf_op jit(solution)/shard_map/ppermute | solution.py:630
  57.8 3.9 %collective-permute-start.16 = (f32[1,512]{1,0:T(1,128)S(1)}, f32[1,512]{1,0:T(1,128)S(1)}, u32[]{:S(2)}, u32[]{:S(2)}) collective-permute-start(f32[1,512]{1,0:T(1,128)S(1)} %get-tuple-element.69.refs_5_), channel_id=1, source_target_pairs={{0,3},{1,2},{2,1},{3,0},{4,7},{5,6},{6,5},{7,4},{8,11},{9,10},{10,... | collective-permute-start | bytes 6152 | tf_op jit(solution)/shard_map/ppermute | solution.py:630
  57.9 3.8 %collective-permute-start.14 = (bf16[256,1024]{1,0:T(8,128)(2,1)S(1)}, bf16[256,1024]{1,0:T(8,128)(2,1)S(1)}, u32[]{:S(2)}, u32[]{:S(2)}) collective-permute-start(bf16[256,1024]{1,0:T(8,128)(2,1)S(1)} %stack.5.refs_3_), channel_id=1, source_target_pairs={{0,1},{1,0},{2,3},{3,2},{4,5},{5,4},{6,7},{7,6},{8,9},{9,8},{10,11... | collective-permute-start | bytes 1572872 | tf_op jit(solution)/shard_map/ppermute | solution.py:629
  (3 other events, 4.5 us)
